TPU v7x, 128 devices: a whole 4x4x4 slice. The times are simulated.
128 devices in a mesh: group: 8 (over z_hi, y), row: 4 (over z_lo, core), col: 4 (over x).
Axes of the slice: x: 4, y: 4, z: 4 (z_hi: 2, z_lo: 2; z = z_hi * 2 + z_lo), core: 2. Of those that a mesh axis runs over, the one named last changes fastest.
Arguments:
- frontal: bfloat16 [8, 8192, 8192], P('group', 'row', 'col'), may hold values from -6 to 6
- panel_cols: bfloat16 [8, 8192, 384], P('group', ('row', 'col')), may hold values from -1.25 to 1.25
- inv_factor: bfloat16 [8, 384, 384], P('group'), as said below
- child_map: int32 [8, 64], replicated, may hold values from 0 to 63, as said below
- child_mask: int32 [8, 64], replicated, may hold values from 0 to 1, as said below
Outputs:
- assembled: bfloat16 [8, 8192, 8192], P('group', 'row', 'col')
Inputs may be any that keep to these rules, and one draw needn't show every extreme that they name: `child_mask`: in each aligned run of 16 blocks exactly 8 blocks are live. `child_map`: the live blocks of one group map to distinct blocks; of the live blocks in one aligned run of 16 blocks exactly 2 map into each aligned run. A padding block maps to its own index. `inv_factor`: zero above the diagonal.
All inputs are finite; a program needn't handle non-finite values.
Results may differ from a plain program's by a relative error of at most 0.0053.
Values may be sent and summed in bfloat16 or wider, within the bound.
No kernel may reach another device: no remote copies, remote signals or barrier semaphores. Data moves between devices by JAX's collectives and lax.ppermute only.
A program may use at most 128 MiB of HBM per device.

v0:
```python
import jax
import jax.numpy as jnp
from jax import lax
from jax.sharding import PartitionSpec as P

BLK = 128
PAIR = 2


def shifted(array, axis, by):
    count = lax.axis_size(axis)
    pairs = [(i, i + by) for i in range(count) if 0 <= i + by < count]
    return lax.ppermute(array, axis, pairs)


def range_ranks(targets, live, span):
    count = targets.shape[0]
    block_ids = jnp.arange(count, dtype=jnp.int32)
    same_run = block_ids[:, None] // span == block_ids[None, :] // span
    smaller = targets[None, :] < targets[:, None]
    return jnp.sum(same_run & smaller & (live[None, :] == 1), axis=1)


def local_order(ranks, live, start, span, live_count):
    seg_rank = lax.dynamic_slice_in_dim(ranks, start, span)
    seg_live = lax.dynamic_slice_in_dim(live, start, span)
    wanted = jnp.arange(live_count, dtype=jnp.int32)
    hits = (seg_rank[None, :] == wanted[:, None]) & (seg_live[None, :] == 1)
    return jnp.sum(jnp.where(hits, jnp.arange(span, dtype=jnp.int32)[None, :], 0), axis=1)


def arrivals(ranks, targets, live, run_index, span):
    count = targets.shape[0]
    block_ids = jnp.arange(count, dtype=jnp.int32)
    local_slot = targets - run_index * span
    valid = (live == 1) & (local_slot >= 0) & (local_slot < span)
    arrive = block_ids // span * PAIR + ranks - run_index * PAIR
    hits = valid[:, None] & (local_slot[:, None] == jnp.arange(span, dtype=jnp.int32)[None, :])
    index = jnp.sum(jnp.where(hits, arrive[:, None], 0), axis=0)
    present = jnp.any(hits, axis=0).astype(jnp.float32)
    return (index, present)


def on_device(frontal, panel_cols, inv_factor, child_map, child_mask):
    group_index = lax.axis_index("group")
    row_index = lax.axis_index("row")
    col_index = lax.axis_index("col")
    runs = lax.axis_size("row")
    span = child_map.shape[1] // runs
    live_count = PAIR * runs
    tile = frontal.shape[1]
    factor = jnp.dot(panel_cols[0], inv_factor[0].T, preferred_element_type=jnp.float32).astype(
        jnp.bfloat16
    )
    everything = lax.all_gather(factor, ("row", "col"), axis=0, tiled=True)
    rows_mine = lax.dynamic_slice_in_dim(everything, row_index * tile, tile, 0)
    cols_mine = lax.dynamic_slice_in_dim(everything, col_index * tile, tile, 0)
    product = lax.dot_general(
        rows_mine, cols_mine, (((1,), (1,)), ((), ())), preferred_element_type=jnp.float32
    )
    update = frontal[0].astype(jnp.float32) - product
    carried = update.astype(jnp.bfloat16)
    own_map = lax.dynamic_index_in_dim(child_map, group_index, 0, False)
    own_mask = lax.dynamic_index_in_dim(child_mask, group_index, 0, False)
    child = jnp.minimum(group_index + 1, child_map.shape[0] - 1)
    other_map = lax.dynamic_index_in_dim(child_map, child, 0, False)
    other_mask = lax.dynamic_index_in_dim(child_mask, child, 0, False)
    own_ranks = range_ranks(own_map, own_mask, span)
    row_pick = local_order(own_ranks, own_mask, row_index * span, span, live_count)
    col_pick = local_order(own_ranks, own_mask, col_index * span, span, live_count)
    tile_blocks = carried.reshape(span, BLK, span, BLK)
    compact = jnp.take(jnp.take(tile_blocks, row_pick, axis=0), col_pick, axis=2)
    compact = compact.reshape(live_count * BLK, live_count * BLK)
    received = shifted(compact, "group", -1)
    arrived = lax.all_to_all(
        lax.all_to_all(received, "row", split_axis=0, concat_axis=0, tiled=True),
        "col",
        split_axis=1,
        concat_axis=1,
        tiled=True,
    )
    other_ranks = range_ranks(other_map, other_mask, span)
    row_arrive, row_there = arrivals(other_ranks, other_map, other_mask, row_index, span)
    col_arrive, col_there = arrivals(other_ranks, other_map, other_mask, col_index, span)
    arrived_blocks = arrived.reshape(live_count, BLK, live_count, BLK)
    placed = jnp.take(jnp.take(arrived_blocks, row_arrive, axis=0), col_arrive, axis=2).astype(
        jnp.float32
    )
    placed = placed * (row_there[:, None, None, None] * col_there[None, None, :, None])
    assembled = (update + placed.reshape(tile, tile)).astype(jnp.bfloat16)
    return assembled[None]


def solution(mesh):
    placed = (
        P("group", "row", "col"),
        P("group", ("row", "col"), None),
        P("group", None, None),
        P(),
        P(),
    )
    return jax.shard_map(
        on_device, mesh=mesh, in_specs=placed, out_specs=P("group", "row", "col"), check_vma=False
    )
```

profile of v0, /device:TPU:72, one launch (start us, length us, event | category | flops | bytes accessed | tf_op | source)
XLA Modules:
  0.0 294.0 jit_solution(12988885825333989966)
XLA Ops:
  6.5 0.0 copy-start
  6.5 0.0 all-gather.2.cloned.1.call-start
  6.5 1.0 copy-done
  7.5 2.1 convolution_convert_fusion
  9.7 0.0 all-gather.2.cloned.1.call-update
  9.7 0.7 fusion.20
  10.4 0.7 compare_bitcast_fusion.2
  11.1 0.7 compare_and_fusion.5
  11.8 0.2 convert_reduce_fusion.1
  12.0 0.1 fusion.26
  12.1 0.8 compare_bitcast_fusion.1
  12.9 0.1 select_reduce_fusion.3
  13.1 0.1 select_reduce_fusion.2
  13.2 0.1 broadcast_bitcast_fusion.1
  13.3 50.9 %all-gather.2.cloned.1.call-done = bf16[8192,384]{1,0:T(8,128)(2,1)} async-done(((bf16[512,384]{1,0:T(8,128)(2,1)}), bf16[8192,384]{1,0:T(8,128)(2,1)}) %all-gather.2.cloned.1.call-update) | async-done | bytes 6291472 | tf_op jit(solution)/shard_map/all_gather | solution.py:55
  64.2 6.6 %fusion.5 = f32[2048,2048]{1,0:T(8,128)S(1)} fusion(bf16[8192,384]{1,0:T(8,128)(2,1)} %all-gather.2.cloned.1.call-done, s32[]{:T(128)S(6)} %select_n.158, s32[]{:T(128)S(6)} %select_n.157), kind=kOutput, calls=%fused_computation.15 | convolution fusion | flops 3221225472 | bytes 19922952 | tf_op jit(solution)/shard_map/dot_general | solution.py:58
  70.7 0.0 copy-start.2
  70.7 5.7 %copy-done.2 = f32[2048,2048]{1,0:T(8,128)} copy-done((f32[2048,2048]{1,0:T(8,128)}, f32[2048,2048]{1,0:T(8,128)S(1)}, u32[]{:S(2)}) %copy-start.2) | copy-done | bytes 16777240
  76.4 8.6 %fusion.3 = bf16[256,8,16,128]{3,1,2,0:T(8,128)(2,1)} fusion(f32[2048,2048]{1,0:T(8,128)S(1)} %fusion.5, bf16[1,2048,2048]{2,1,0:T(8,128)(2,1)} %param.5), kind=kLoop, calls=%fused_computation.9 | loop fusion | flops 12582912 | bytes 33554432
  85.0 9.8 %copy.28 = bf16[256,8,16,128]{3,2,1,0:T(8,128)(2,1)} copy(bf16[256,8,16,128]{3,1,2,0:T(8,128)(2,1)} %fusion.3) | data formatting | bytes 16777216
  94.8 6.5 %gather_fusion = bf16[8,128,16,128]{3,2,1,0:T(8,128)(2,1)} fusion(bf16[16,128,16,128]{3,2,1,0:T(8,128)(2,1)} %bitcast.76, s32[1024]{0:T(1024)S(1)} %pad_clamp_fusion.3), kind=kCustom, calls=%fused_computation | custom fusion | bytes 8388640 | tf_op jit(solution)/shard_map/jit(_take)/gather | solution.py:72
  101.2 2.7 broadcast_select_fusion
  103.9 3.2 %copy.22 = bf16[8,128,16,128]{3,1,2,0:T(8,128)(2,1)} copy(bf16[8,128,16,128]{3,2,1,0:T(8,128)(2,1)S(1)} %broadcast_select_fusion) | data formatting | bytes 8388608 | tf_op jit(solution)/shard_map/jit(_take)/select_n | solution.py:72
  107.1 3.1 %gather_fusion.1 = bf16[8,8,128,128]{3,2,1,0:T(8,128)(2,1)S(1)} fusion(bf16[8,128,16,128]{3,1,2,0:T(8,128)(2,1)} %copy.22, s32[1024]{0:T(1024)S(1)} %pad_clamp_fusion.2), kind=kCustom, calls=%fused_computation.1 | custom fusion | bytes 4194336 | tf_op jit(solution)/shard_map/jit(_take)/gather | solution.py:72
  110.2 1.4 copy.23
  111.6 0.3 bitcast_select_fusion.1
  111.9 2.6 collective-permute-start
  114.5 47.2 %collective-permute-done = bf16[1024,1024]{1,0:T(8,128)(2,1)S(1)} collective-permute-done((bf16[1024,1024]{1,0:T(8,128)(2,1)S(1)}, bf16[1024,1024]{1,0:T(8,128)(2,1)S(1)}, u32[]{:S(2)}, u32[]{:S(2)}) %collective-permute-start) | collective-permute-done | bytes 2097184 | tf_op jit(solution)/shard_map/ppermute | solution.py:13
  161.7 0.0 copy-start.3
  161.7 1.3 copy-done.3
  163.1 3.6 %all-to-all-start = ((bf16[4,256,1024]{2,1,0:T(8,128)(2,1)}), bf16[4,256,1024]{2,1,0:T(8,128)(2,1)S(1)}, u32[]{:S(2)}, u32[]{:S(2)}) async-start(bf16[4,256,1024]{2,1,0:T(8,128)(2,1)} %bitcast.79), calls=%async_computation | async-start | bytes 4194304 | tf_op jit(solution)/shard_map/all_to_all | solution.py:76
  166.7 0.1 fusion.15
  166.8 0.1 fusion.13
  167.0 0.1 select_reduce_fusion.1
  167.1 25.3 %all-to-all-done = bf16[4,256,1024]{2,1,0:T(8,128)(2,1)S(1)} async-done(((bf16[4,256,1024]{2,1,0:T(8,128)(2,1)}), bf16[4,256,1024]{2,1,0:T(8,128)(2,1)S(1)}, u32[]{:S(2)}, u32[]{:S(2)}) %all-to-all-start) | async-done | bytes 2097184 | tf_op jit(solution)/shard_map/all_to_all | solution.py:76
  192.3 2.7 all_to_all.14
  195.1 3.2 %copy.24 = bf16[1024,4,256]{2,0,1:T(8,128)(2,1)} copy(bf16[1024,4,256]{2,1,0:T(4,128)(2,1)} %all_to_all.14) | data formatting | bytes 4194304 | tf_op jit(solution)/shard_map/all_to_all | solution.py:75
  198.3 4.2 %all-to-all-start.1 = ((bf16[1024,4,256]{2,0,1:T(8,128)(2,1)}), bf16[1024,4,256]{2,0,1:T(8,128)(2,1)S(1)}, u32[]{:S(2)}, u32[]{:S(2)}) async-start(bf16[1024,4,256]{2,0,1:T(8,128)(2,1)} %copy.24), calls=%async_computation.1 | async-start | bytes 4194304 | tf_op jit(solution)/shard_map/all_to_all | solution.py:75
  202.6 0.1 select_reduce_fusion
  202.7 0.1 broadcast_bitcast_fusion
  202.8 0.1 broadcast_multiply_fusion
  202.9 25.8 %all-to-all-done.1 = bf16[1024,4,256]{2,0,1:T(8,128)(2,1)S(1)} async-done(((bf16[1024,4,256]{2,0,1:T(8,128)(2,1)}), bf16[1024,4,256]{2,0,1:T(8,128)(2,1)S(1)}, u32[]{:S(2)}, u32[]{:S(2)}) %all-to-all-start.1) | async-done | bytes 2097184 | tf_op jit(solution)/shard_map/all_to_all | solution.py:75
  228.7 2.9 copy.25
  231.6 2.7 reshape.267
  234.4 3.1 %gather_fusion.2 = bf16[16,128,8,128]{3,2,1,0:T(8,128)(2,1)} fusion(bf16[8,128,8,128]{3,2,1,0:T(8,128)(2,1)S(1)} %reshape.267, s32[1024]{0:T(1024)S(1)} %pad_clamp_fusion.1), kind=kCustom, calls=%fused_computation.2 | custom fusion | bytes 8388672 | tf_op jit(solution)/shard_map/jit(_take)/gather | solution.py:86
  237.5 2.6 broadcast_select_fusion.1
  240.1 3.2 %copy.26 = bf16[16,128,8,128]{3,1,2,0:T(8,128)(2,1)} copy(bf16[16,128,8,128]{3,2,1,0:T(8,128)(2,1)S(1)} %broadcast_select_fusion.1) | data formatting | bytes 8388608 | tf_op jit(solution)/shard_map/jit(_take)/select_n | solution.py:86
  243.3 7.0 %gather_fusion.3 = bf16[16,16,128,128]{3,2,1,0:T(8,128)(2,1)} fusion(bf16[16,128,8,128]{3,1,2,0:T(8,128)(2,1)} %copy.26, s32[1024]{0:T(1024)S(1)} %pad_clamp_fusion), kind=kCustom, calls=%fused_computation.3 | custom fusion | bytes 16777280 | tf_op jit(solution)/shard_map/jit(_take)/gather | solution.py:86
  250.3 13.7 %copy.27 = bf16[16,128,16,128]{3,2,1,0:T(8,128)(2,1)} copy(bf16[16,128,16,128]{3,1,0,2:T(8,128)(2,1)} %bitcast.74) | data formatting | bytes 16777216 | tf_op jit(solution)/shard_map/jit(_take)/gather | solution.py:86
  264.0 1.1 mul.70
  265.2 0.0 copy-start.1
  265.2 21.9 %fusion.4 = bf16[1,2048,2048]{2,1,0:T(8,128)(2,1)} fusion(f32[256,8,16,128]{3,2,1,0:T(8,128)S(1)} %bitcast.73, f32[2048,2048]{1,0:T(8,128)} %copy-done.2, bf16[256,8,16,128]{3,2,1,0:T(8,128)(2,1)} %bitcast.75, bf16[1,2048,2048]{2,1,0:T(8,128)(2,1)} %param.5, pred[2048]{0:T(1024)(128)(4,1)S(1)} %broadcast_bitcast_fusion), kind=kLoop, calls=%fused_computation.10 | loop fusion | flops 29360128 | bytes 58722304 | tf_op jit(solution)/shard_map/broadcast_in_dim | solution.py:91
  287.1 0.0 copy-done.1
  (15 shorter events, 0.1 us)
Async XLA Ops:
  6.5 1.0 copy-start
  6.5 57.6 %all-gather.2.cloned.1.call-start = ((), (), s32[]{:S(2)}) async-start(), calls=%async_computation.2 | async-start | bytes 6684672 | tf_op jit(solution)/shard_map/all_gather | solution.py:55
  70.7 5.7 %copy-start.2 = (f32[2048,2048]{1,0:T(8,128)}, f32[2048,2048]{1,0:T(8,128)S(1)}, u32[]{:S(2)}) copy-start(f32[2048,2048]{1,0:T(8,128)S(1)} %fusion.5) | copy-start | bytes 50331652
  111.9 49.9 %collective-permute-start = (bf16[1024,1024]{1,0:T(8,128)(2,1)S(1)}, bf16[1024,1024]{1,0:T(8,128)(2,1)S(1)}, u32[]{:S(2)}, u32[]{:S(2)}) collective-permute-start(bf16[1024,1024]{1,0:T(8,128)(2,1)S(1)} %bitcast_select_fusion.1), channel_id=1, source_target_pairs={{16,0},{32,16},{48,32},{64,48},{80,64},{96,80},{112,96},{17,1},{33... | collective-permute-start | bytes 6291464 | tf_op jit(solution)/shard_map/ppermute | solution.py:13
  161.7 1.3 copy-start.3
  163.1 29.3 %all-to-all-start = ((bf16[4,256,1024]{2,1,0:T(8,128)(2,1)}), bf16[4,256,1024]{2,1,0:T(8,128)(2,1)S(1)}, u32[]{:S(2)}, u32[]{:S(2)}) async-start(bf16[4,256,1024]{2,1,0:T(8,128)(2,1)} %bitcast.79), calls=%async_computation | async-start | bytes 4194304 | tf_op jit(solution)/shard_map/all_to_all | solution.py:76
  198.3 30.4 %all-to-all-start.1 = ((bf16[1024,4,256]{2,0,1:T(8,128)(2,1)}), bf16[1024,4,256]{2,0,1:T(8,128)(2,1)S(1)}, u32[]{:S(2)}, u32[]{:S(2)}) async-start(bf16[1024,4,256]{2,0,1:T(8,128)(2,1)} %copy.24), calls=%async_computation.1 | async-start | bytes 4194304 | tf_op jit(solution)/shard_map/all_to_all | solution.py:75
  265.2 22.0 %copy-start.1 = (bf16[1,512,384]{2,1,0:T(8,128)(2,1)S(1)}, bf16[1,512,384]{2,1,0:T(8,128)(2,1)}, u32[]{:S(2)}) copy-start(bf16[1,512,384]{2,1,0:T(8,128)(2,1)} %param.6) | copy-start | bytes 1179652
Sparse Core Ops, SparseCore 0:
  9.8 54.3 all-gather.1
where the time goes:
time: 299 us; the launch traced here: 294 us
  waiting for transfers between devices  149 us (50%)
  local copies, waits for them, and re-layouts  72.6 us (24%)
  other arithmetic  39.4 us (13%)
  between operations  13.6 us (5%)
  starting transfers between devices  10.5 us (4%)
  matrix products  8.69 us (3%)
    all_gather x1, waiting for transfers between devices, on_device(): everything = lax.all_gather(factor, ('row', 'col'), axis=0, tiled=True)  50.9 us
    ppermute x1, waiting for transfers between devices, shifted(): return lax.ppermute(array, axis, pairs)  47.2 us
    all_to_all x1, waiting for transfers between devices, on_device(): lax.all_to_all(lax.all_to_all(received, 'row', split_axis=0, concat_axis=...  25.8 us
    all_to_all x1, waiting for transfers between devices, on_device(): lax.all_to_all(received, 'row', split_axis=0, concat_axis=0, tiled=True)  25.3 us
    broadcast_in_dim x1, other arithmetic, on_device(): return assembled[None]  21.9 us
    gather x2, local copies, waits for them, and re-layouts, on_device(): jnp.take(jnp.take(arrived_blocks, row_arrive, axis=0), col_arrive, axis=2)  20.7 us
    unnamed x9, local copies, waits for them, and re-layouts  17.8 us
    all_to_all x3, local copies, waits for them, and re-layouts, on_device(): lax.all_to_all(lax.all_to_all(received, 'row', split_axis=0, concat_axis=...  8.89 us
  transfers between devices with their start and end apart: 4, of which 4 were waited for; matrix products, arithmetic and copies ran while one was open for 1% of the time, Pallas kernels for 0%

commit v1 on v0

v1 whole, which is shorter than its diff:
```python
import functools

import jax
import jax.numpy as jnp
from jax import lax
from jax.experimental import pallas as pl
from jax.experimental.pallas import tpu as pltpu
from jax.sharding import PartitionSpec as P

BLK = 128
AXES = ("group", "row", "col")
ANY = pl.BlockSpec(memory_space=pl.ANY)
SMEM = pl.BlockSpec(memory_space=pltpu.SMEM)
VMEM = pl.BlockSpec(memory_space=pltpu.VMEM)
DEPTH = (((1,), (1,)), ((), ()))


def params(mib):
    return pltpu.CompilerParams(vmem_limit_bytes=mib << 20)


def move(array, target):
    groups, rows, cols = (lax.axis_size(axis) for axis in AXES)
    pairs = []
    for g in range(groups):
        for r in range(rows):
            for c in range(cols):
                tg, tr, tc = target(g, r, c)
                if tg >= 0:
                    pairs.append(((g * rows + r) * cols + c, (tg * rows + tr) * cols + tc))
    return lax.ppermute(array, AXES, pairs)


def plan_kernel(map_ref, mask_ref, out_ref):
    count = map_ref.shape[1]
    runs = lax.axis_size("row")
    span = count // runs
    group = lax.axis_index("group")
    child = jnp.minimum(group + 1, map_ref.shape[0] - 1)

    def coded(g, run):
        out = []
        for k in range(span):
            target = map_ref[g, run * span + k]
            live = mask_ref[g, run * span + k] == 1
            out.append((jnp.where(live, target // span, -1), target * span + k))
        return out

    def ends(codes, run):
        low, high = jnp.int32(1 << 20), jnp.int32(-1)
        for to, code in codes:
            hit = to == run
            low = jnp.minimum(low, jnp.where(hit, code, 1 << 20))
            high = jnp.maximum(high, jnp.where(hit, code, -1))
        return low, high

    for position, axis in enumerate(("row", "col")):
        me = lax.axis_index(axis)
        own = coded(group, me)
        for run in range(runs):
            for i, code in enumerate(ends(own, run)):
                out_ref[position * 2 * runs + 2 * run + i] = lax.rem(code, span)
        for d in range(runs):
            for i, code in enumerate(ends(coded(child, me ^ d), me)):
                out_ref[(position + 2) * 2 * runs + 2 * d + i] = code // span - me * span


def plan(child_map, child_mask):
    return pl.pallas_call(
        plan_kernel,
        out_shape=jax.ShapeDtypeStruct((32,), jnp.int32),
        in_specs=[SMEM, SMEM],
        out_specs=SMEM,
        name="plan",
    )(child_map, child_mask)


def load_factor(shards, rows_v, cols_v, sems):
    size = shards[0].shape[0]
    copies = []
    for axis, held, refs in (("col", rows_v, shards[:4]), ("row", cols_v, shards[4:])):
        me = lax.axis_index(axis)
        for d, ref in enumerate(refs):
            copies.append(
                pltpu.make_async_copy(ref, held.at[pl.ds((me ^ d) * size, size)], sems.at[len(copies)])
            )
    for copy in copies:
        copy.start()
    return copies


def picked_kernel(sending, idx, *refs):
    shards, frontal = refs[:8], refs[8]
    outs = refs[9:13]
    rows_v, cols_v, front_v, pick_v, sems = refs[13:]
    row, col = lax.axis_index("row"), lax.axis_index("col")
    copies = load_factor(shards, rows_v, cols_v, sems)
    row_at, col_at = [], []
    for d in range(4):
        for i in range(2):
            if sending:
                row_at.append(idx[2 * (row ^ d) + i])
                col_at.append(idx[8 + 2 * (col ^ d) + i])
            else:
                row_at.append(idx[16 + 2 * d + i])
                col_at.append(idx[24 + 2 * d + i])
    for a in range(8):
        for b in range(8):
            pltpu.make_async_copy(
                frontal.at[
                    pl.ds(pl.multiple_of(row_at[a] * BLK, BLK), BLK),
                    pl.ds(pl.multiple_of(col_at[b] * BLK, BLK), BLK),
                ],
                front_v.at[a * 8 + b],
                sems.at[8],
            ).start()
    for copy in copies:
        copy.wait()
    for b in range(8):
        pick_v[b * BLK : (b + 1) * BLK, :] = cols_v[pl.ds(pl.multiple_of(col_at[b] * BLK, BLK), BLK), :]
    pltpu.make_async_copy(front_v, front_v, sems.at[8]).wait()
    for d in range(4):
        left = jnp.concatenate(
            [rows_v[pl.ds(pl.multiple_of(row_at[2 * d + i] * BLK, BLK), BLK), :] for i in range(2)], axis=0
        )
        product = lax.dot_general(left, pick_v[...], DEPTH, preferred_element_type=jnp.float32)
        for e in range(4):
            for i in range(2):
                for j in range(2):
                    at = ((e * 2 + i) * 2 + j) * BLK
                    b = 2 * e + j
                    value = front_v[(2 * d + i) * 8 + b].astype(jnp.float32)
                    value = value - product[i * BLK : (i + 1) * BLK, b * BLK : (b + 1) * BLK]
                    outs[d][at : at + BLK, :] = value.astype(outs[d].dtype)


def picked(idx, shards, frontal, sending):
    dtype = jnp.bfloat16 if sending else jnp.float32
    depth = shards[0].shape[1]
    return pl.pallas_call(
        functools.partial(picked_kernel, sending),
        out_shape=[jax.ShapeDtypeStruct((16 * BLK, BLK), dtype)] * 4,
        in_specs=[SMEM] + [ANY] * 9,
        out_specs=[VMEM] * 4,
        scratch_shapes=[
            pltpu.VMEM((frontal.shape[0], depth), jnp.bfloat16),
            pltpu.VMEM((frontal.shape[1], depth), jnp.bfloat16),
            pltpu.VMEM((64, BLK, BLK), jnp.bfloat16),
            pltpu.VMEM((8 * BLK, depth), jnp.bfloat16),
            pltpu.SemaphoreType.DMA((9,)),
        ],
        compiler_params=params(40),
        cost_estimate=pl.CostEstimate(flops=2 * 1024 * 1024 * 384, bytes_accessed=10 << 20, transcendentals=0),
        name="picked_send" if sending else "picked_own",
    )(idx, *shards, frontal)


def update_kernel(frontal, *refs):
    shards, out = refs[:8], refs[8]
    rows_v, cols_v, sems = refs[9:]
    step = pl.program_id(0)

    @pl.when(step == 0)
    def _():
        for copy in load_factor(shards, rows_v, cols_v, sems):
            copy.wait()

    high, wide = out.shape
    across = cols_v.shape[0] // wide
    left = rows_v[pl.ds(pl.multiple_of(step // across * high, high), high), :]
    right = cols_v[pl.ds(pl.multiple_of(lax.rem(step, across) * wide, wide), wide), :]
    product = lax.dot_general(left, right, DEPTH, preferred_element_type=jnp.float32)
    out[...] = (frontal[...].astype(jnp.float32) - product).astype(jnp.bfloat16)


def updated(shards, frontal):
    tile, depth = frontal.shape[0], shards[0].shape[1]
    high, wide = 512, 1024
    across = tile // wide
    block = pl.BlockSpec((high, wide), lambda s: (s // across, s % across))
    return pl.pallas_call(
        update_kernel,
        out_shape=jax.ShapeDtypeStruct((tile, tile), jnp.bfloat16),
        grid=(tile // high * across,),
        in_specs=[block] + [ANY] * 8,
        out_specs=block,
        scratch_shapes=[
            pltpu.VMEM((tile, depth), jnp.bfloat16),
            pltpu.VMEM((tile, depth), jnp.bfloat16),
            pltpu.SemaphoreType.DMA((8,)),
        ],
        compiler_params=params(40),
        cost_estimate=pl.CostEstimate(flops=2 * tile * tile * depth, bytes_accessed=20 << 20, transcendentals=0),
        name="update",
    )(frontal, *shards)


def place_kernel(d, idx, own, here, x1, x2, x3, _, out, block_v, sem):
    copies = []
    for e, ref in enumerate((here, x1, x2, x3)):
        for i in range(2):
            for j in range(2):
                k = (e * 2 + i) * 2 + j
                at = (i * 2 + j) * BLK
                block_v[k] = (own[k * BLK : (k + 1) * BLK, :] + ref[at : at + BLK, :].astype(jnp.float32)).astype(
                    jnp.bfloat16
                )
                pltpu.make_async_copy(
                    block_v.at[k],
                    out.at[
                        pl.ds(pl.multiple_of(idx[16 + 2 * d + i] * BLK, BLK), BLK),
                        pl.ds(pl.multiple_of(idx[24 + 2 * e + j] * BLK, BLK), BLK),
                    ],
                    sem,
                ).start()
    pltpu.make_async_copy(block_v, block_v, sem).wait()


def placed(idx, d, own, here, others, out):
    quarter = pl.BlockSpec((4 * BLK, BLK), lambda s: (0, 0))
    whole = pl.BlockSpec((16 * BLK, BLK), lambda s: (0, 0))
    return pl.pallas_call(
        functools.partial(place_kernel, d),
        out_shape=jax.ShapeDtypeStruct(out.shape, out.dtype),
        grid=(1,),
        in_specs=[SMEM, whole, quarter, quarter, quarter, quarter, ANY],
        out_specs=ANY,
        scratch_shapes=[pltpu.VMEM((16, BLK, BLK), jnp.bfloat16), pltpu.SemaphoreType.DMA],
        input_output_aliases={6: 0},
        compiler_params=params(16),
        cost_estimate=pl.CostEstimate(flops=1 << 18, bytes_accessed=2 << 20, transcendentals=0),
        name="place",
    )(idx, own, here, *others, out)


def on_device(frontal, panel_cols, inv_factor, child_map, child_mask):
    front = frontal[0]
    idx = plan(child_map, child_mask)
    factor = lax.dot_general(panel_cols[0], inv_factor[0], DEPTH, preferred_element_type=jnp.float32).astype(
        jnp.bfloat16
    )
    turned = move(factor, lambda g, r, c: (g, c, r))
    by_col = [factor] + [move(factor, lambda g, r, c, d=d: (g, r, c ^ d)) for d in (1, 2, 3)]
    far = move(turned, lambda g, r, c: (g, r ^ 2, c))
    by_row = [turned, move(turned, lambda g, r, c: (g, r ^ 1, c)), far, move(far, lambda g, r, c: (g, r ^ 1, c))]
    shards = by_col + by_row
    sent = picked(idx, shards, front, True)
    came = [move(sent[d], lambda g, r, c, d=d: (g - 1, r ^ d, c)) for d in range(4)]
    out = updated(shards, front)
    own = picked(idx, shards, front, False)
    quarter = 4 * BLK
    for d in range(4):
        others = [
            move(came[d][e * quarter : (e + 1) * quarter], lambda g, r, c, e=e: (g, r, c ^ e)) for e in (1, 2, 3)
        ]
        out = placed(idx, d, own[d], came[d], others, out)
    return out[None]


def solution(mesh):
    specs = (
        P("group", "row", "col"),
        P("group", ("row", "col"), None),
        P("group", None, None),
        P(),
        P(),
    )
    return jax.shard_map(
        on_device, mesh=mesh, in_specs=specs, out_specs=P("group", "row", "col"), check_vma=False
    )
```

time: 299 us -> 137 us (0.46)
  the two profiles are of different devices: /device:TPU:72 before, /device:TPU:25 now
where the time goes in v1:
time: 137 us
  waiting for transfers between devices  53.2 us (39%)
  starting transfers between devices  49.1 us (36%)
  Pallas kernels  27.5 us (20%)
  local copies, waits for them, and re-layouts  5.14 us (4%)
  matrix products  1.37 us (1%)
    ppermute x23, waiting for transfers between devices, move(): return lax.ppermute(array, AXES, pairs)  53.2 us
    ppermute x23, starting transfers between devices, move(): return lax.ppermute(array, AXES, pairs)  49.1 us
    pallas_call x1, Pallas kernels, updated(): pl.pallas_call(update_kernel, out_shape=jax.ShapeDtypeStruct((tile, tile)...  9.63 us
    pallas_call x2, Pallas kernels, picked(): pl.pallas_call(functools.partial(picked_kernel, sending), out_shape=[jax....  9.19 us
    pallas_call x4, Pallas kernels, placed(): pl.pallas_call(functools.partial(place_kernel, d), out_shape=jax.ShapeDty...  5.34 us
    unnamed x6, local copies, waits for them, and re-layouts  5.03 us
    pallas_call x1, Pallas kernels, plan(): pl.pallas_call(plan_kernel, out_shape=jax.ShapeDtypeStruct((32,), jnp.int...  3.33 us
  transfers between devices with their start and end apart: 23, of which 10 were waited for; matrix products, arithmetic and copies ran while one was open for 0% of the time, Pallas kernels for 16%

profile of v1, /device:TPU:25, one launch (start us, length us, event | category | flops | bytes accessed | tf_op | source)
XLA Modules:
  0.0 136.6 jit_solution(2803481670662422989)
XLA Ops:
  0.0 0.0 copy-start
  0.0 1.0 copy-done
  1.0 1.4 %convolution_convert_fusion.refs_0_ = bf16[512,384]{1,0:T(8,128)(2,1)S(1)} fusion(bf16[1,512,384]{2,1,0:T(8,128)(2,1)S(1)} %copy-done, bf16[1,384,384]{2,1,0:T(8,128)(2,1)} %param.7), kind=kOutput, calls=%fused_computation | convolution fusion | flops 151191552 | bytes 1081344 | tf_op jit(solution)/shard_map/dot_general | solution.py:239
  2.4 3.7 %collective-permute-start.3 = (bf16[512,384]{1,0:T(8,128)(2,1)S(1)}, bf16[512,384]{1,0:T(8,128)(2,1)S(1)}, u32[]{:S(2)}, u32[]{:S(2)}) collective-permute-start(bf16[512,384]{1,0:T(8,128)(2,1)S(1)} %convolution_convert_fusion.refs_0_), channel_id=1, source_target_pairs={{0,0},{1,4},{2,8},{3,12},{4,1},{5,5},{6,9},{7,13},{8,2},{9,6},{10,... | collective-permute-start | bytes 1179656 | tf_op jit(solution)/shard_map/ppermute | solution.py:31
  6.1 5.4 %collective-permute-done.3.refs_4_ = bf16[512,384]{1,0:T(8,128)(2,1)S(1)} collective-permute-done((bf16[512,384]{1,0:T(8,128)(2,1)S(1)}, bf16[512,384]{1,0:T(8,128)(2,1)S(1)}, u32[]{:S(2)}, u32[]{:S(2)}) %collective-permute-start.3) | collective-permute-done | bytes 393248 | tf_op jit(solution)/shard_map/ppermute | solution.py:31
  11.5 7.9 %collective-permute-start.5 = (bf16[512,384]{1,0:T(8,128)(2,1)S(1)}, bf16[512,384]{1,0:T(8,128)(2,1)S(1)}, u32[]{:S(2)}, u32[]{:S(2)}) collective-permute-start(bf16[512,384]{1,0:T(8,128)(2,1)S(1)} %collective-permute-done.3.refs_4_), channel_id=1, source_target_pairs={{0,8},{1,9},{2,10},{3,11},{4,12},{5,13},{6,14},{7,15},{8,0},{9,1},... | collective-permute-start | bytes 1179656 | tf_op jit(solution)/shard_map/ppermute | solution.py:31
  19.4 0.0 collective-permute-start
  19.4 0.0 collective-permute-start.1
  19.4 3.9 %collective-permute-start.2 = (bf16[512,384]{1,0:T(8,128)(2,1)S(1)}, bf16[512,384]{1,0:T(8,128)(2,1)S(1)}, u32[]{:S(2)}, u32[]{:S(2)}) collective-permute-start(bf16[512,384]{1,0:T(8,128)(2,1)S(1)} %convolution_convert_fusion.refs_0_), channel_id=1, source_target_pairs={{0,3},{1,2},{2,1},{3,0},{4,7},{5,6},{6,5},{7,4},{8,11},{9,10},{10,... | collective-permute-start | bytes 1179656 | tf_op jit(solution)/shard_map/ppermute | solution.py:31
  23.3 0.1 collective-permute-start.4
  23.4 3.3 %collective-permute-done.5.refs_6_ = bf16[512,384]{1,0:T(8,128)(2,1)S(1)} collective-permute-done((bf16[512,384]{1,0:T(8,128)(2,1)S(1)}, bf16[512,384]{1,0:T(8,128)(2,1)S(1)}, u32[]{:S(2)}, u32[]{:S(2)}) %collective-permute-start.5) | collective-permute-done | bytes 393248 | tf_op jit(solution)/shard_map/ppermute | solution.py:31
  26.7 0.0 collective-permute-start.6
  26.7 3.3 %plan.1.idx = s32[32]{0:T(128)} custom-call(s32[8,64]{1,0:T(8,128)} %map_ref.1, s32[8,64]{1,0:T(8,128)} %mask_ref.1), custom_call_target="tpu_custom_call" | custom-call | tf_op jit(solution)/shard_map/plan/pallas_call | solution.py:69
  30.1 0.5 collective-permute-done.refs_1_
  30.6 4.7 %collective-permute-done.1.refs_2_ = bf16[512,384]{1,0:T(8,128)(2,1)S(1)} collective-permute-done((bf16[512,384]{1,0:T(8,128)(2,1)S(1)}, bf16[512,384]{1,0:T(8,128)(2,1)S(1)}, u32[]{:S(2)}, u32[]{:S(2)}) %collective-permute-start.1) | collective-permute-done | bytes 393248 | tf_op jit(solution)/shard_map/ppermute | solution.py:31
  35.3 5.1 %collective-permute-done.2.refs_3_ = bf16[512,384]{1,0:T(8,128)(2,1)S(1)} collective-permute-done((bf16[512,384]{1,0:T(8,128)(2,1)S(1)}, bf16[512,384]{1,0:T(8,128)(2,1)S(1)}, u32[]{:S(2)}, u32[]{:S(2)}) %collective-permute-start.2) | collective-permute-done | bytes 393248 | tf_op jit(solution)/shard_map/ppermute | solution.py:31
  40.3 0.0 collective-permute-done.4.refs_5_
  40.3 0.0 collective-permute-done.6.refs_7_
  40.3 0.0 copy-start.1
  40.3 3.4 %copy-done.1 = bf16[1,2048,2048]{2,1,0:T(8,128)(2,1)S(1)} copy-done((bf16[1,2048,2048]{2,1,0:T(8,128)(2,1)S(1)}, bf16[1,2048,2048]{2,1,0:T(8,128)(2,1)}, u32[]{:S(2)}) %copy-start.1) | copy-done | bytes 8388632
  43.7 0.0 copy-start.2
  43.7 0.7 copy-done.2
  44.4 4.2 %picked_send.1 = (bf16[2048,128]{1,0:T(8,128)(2,1)S(1)}, bf16[2048,128]{1,0:T(8,128)(2,1)S(1)}, bf16[2048,128]{1,0:T(8,128)(2,1)S(1)}, bf16[2048,128]{1,0:T(8,128)(2,1)S(1)}) custom-call(s32[32]{0:T(128)S(1)} %copy-done.2, bf16[512,384]{1,0:T(8,128)(2,1)S(1)} %convolution_convert_fusion.refs_0_, bf16[512,384]{1,0:T(8,128)(2,1)S(1)} %collective-permute-done.refs_1_, ...), custom_call_target="tpu_custom_call" | custom-call | flops 805306368 | bytes 10485760 | tf_op jit(solution)/shard_map/picked_send/pallas_call | solution.py:140
  48.6 2.4 %collective-permute-start.19 = (bf16[2048,128]{1,0:T(8,128)(2,1)S(1)}, bf16[2048,128]{1,0:T(8,128)(2,1)S(1)}, u32[]{:S(2)}, u32[]{:S(2)}) collective-permute-start(bf16[2048,128]{1,0:T(8,128)(2,1)S(1)} %get-tuple-element.20), channel_id=1, source_target_pairs={{16,0},{17,1},{18,2},{19,3},{20,4},{21,5},{22,6},{23,7},{24,8},{25... | collective-permute-start | bytes 1572872 | tf_op jit(solution)/shard_map/ppermute | solution.py:31
  51.0 3.7 %collective-permute-start.15 = (bf16[2048,128]{1,0:T(8,128)(2,1)S(1)}, bf16[2048,128]{1,0:T(8,128)(2,1)S(1)}, u32[]{:S(2)}, u32[]{:S(2)}) collective-permute-start(bf16[2048,128]{1,0:T(8,128)(2,1)S(1)} %get-tuple-element.18), channel_id=1, source_target_pairs={{16,4},{17,5},{18,6},{19,7},{20,0},{21,1},{22,2},{23,3},{24,12},{2... | collective-permute-start | bytes 1572872 | tf_op jit(solution)/shard_map/ppermute | solution.py:31
  54.7 2.0 %collective-permute-start.11 = (bf16[2048,128]{1,0:T(8,128)(2,1)S(1)}, bf16[2048,128]{1,0:T(8,128)(2,1)S(1)}, u32[]{:S(2)}, u32[]{:S(2)}) collective-permute-start(bf16[2048,128]{1,0:T(8,128)(2,1)S(1)} %get-tuple-element.16), channel_id=1, source_target_pairs={{16,8},{17,9},{18,10},{19,11},{20,12},{21,13},{22,14},{23,15},{24,... | collective-permute-start | bytes 1572872 | tf_op jit(solution)/shard_map/ppermute | solution.py:31
  56.7 3.2 %collective-permute-start.7 = (bf16[2048,128]{1,0:T(8,128)(2,1)S(1)}, bf16[2048,128]{1,0:T(8,128)(2,1)S(1)}, u32[]{:S(2)}, u32[]{:S(2)}) collective-permute-start(bf16[2048,128]{1,0:T(8,128)(2,1)S(1)} %get-tuple-element.14), channel_id=1, source_target_pairs={{16,12},{17,13},{18,14},{19,15},{20,8},{21,9},{22,10},{23,11},{24,... | collective-permute-start | bytes 1572872 | tf_op jit(solution)/shard_map/ppermute | solution.py:31
  59.9 6.2 %collective-permute-done.19.here = bf16[2048,128]{1,0:T(8,128)(2,1)S(1)} collective-permute-done((bf16[2048,128]{1,0:T(8,128)(2,1)S(1)}, bf16[2048,128]{1,0:T(8,128)(2,1)S(1)}, u32[]{:S(2)}, u32[]{:S(2)}) %collective-permute-start.19) | collective-permute-done | bytes 524320 | tf_op jit(solution)/shard_map/ppermute | solution.py:31
  66.1 0.1 collective-permute-start.20
  66.2 5.4 %collective-permute-start.21 = (bf16[512,128]{1,0:T(8,128)(2,1)S(1)}, bf16[512,128]{1,0:T(8,128)(2,1)S(1)}, u32[]{:S(2)}, u32[]{:S(2)}) collective-permute-start(bf16[512,128]{1,0:T(8,128)(2,1)S(1)} %get-tuple-element.22), channel_id=1, source_target_pairs={{0,2},{1,3},{2,0},{3,1},{4,6},{5,7},{6,4},{7,5},{8,10},{9,11},{10,... | collective-permute-start | bytes 393224 | tf_op jit(solution)/shard_map/ppermute | solution.py:31
  71.6 11.0 %collective-permute-done.15.here = bf16[2048,128]{1,0:T(8,128)(2,1)S(1)} collective-permute-done((bf16[2048,128]{1,0:T(8,128)(2,1)S(1)}, bf16[2048,128]{1,0:T(8,128)(2,1)S(1)}, u32[]{:S(2)}, u32[]{:S(2)}) %collective-permute-start.15) | collective-permute-done | bytes 524320 | tf_op jit(solution)/shard_map/ppermute | solution.py:31
  82.6 2.6 %collective-permute-start.22 = (bf16[512,128]{1,0:T(8,128)(2,1)S(1)}, bf16[512,128]{1,0:T(8,128)(2,1)S(1)}, u32[]{:S(2)}, u32[]{:S(2)}) collective-permute-start(bf16[512,128]{1,0:T(8,128)(2,1)S(1)} %get-tuple-element.21), channel_id=1, source_target_pairs={{0,3},{1,2},{2,1},{3,0},{4,7},{5,6},{6,5},{7,4},{8,11},{9,10},{10,... | collective-permute-start | bytes 393224 | tf_op jit(solution)/shard_map/ppermute | solution.py:31
  85.2 2.2 %collective-permute-done.11.here = bf16[2048,128]{1,0:T(8,128)(2,1)S(1)} collective-permute-done((bf16[2048,128]{1,0:T(8,128)(2,1)S(1)}, bf16[2048,128]{1,0:T(8,128)(2,1)S(1)}, u32[]{:S(2)}, u32[]{:S(2)}) %collective-permute-start.11) | collective-permute-done | bytes 524320 | tf_op jit(solution)/shard_map/ppermute | solution.py:31
  87.4 0.0 collective-permute-start.16
  87.5 14.0 %collective-permute-done.7.here = bf16[2048,128]{1,0:T(8,128)(2,1)S(1)} collective-permute-done((bf16[2048,128]{1,0:T(8,128)(2,1)S(1)}, bf16[2048,128]{1,0:T(8,128)(2,1)S(1)}, u32[]{:S(2)}, u32[]{:S(2)}) %collective-permute-start.7) | collective-permute-done | bytes 524320 | tf_op jit(solution)/shard_map/ppermute | solution.py:31
  101.5 0.0 collective-permute-start.17
  101.5 0.0 collective-permute-done.20.x1
  101.5 3.4 %collective-permute-start.18 = (bf16[512,128]{1,0:T(8,128)(2,1)S(1)}, bf16[512,128]{1,0:T(8,128)(2,1)S(1)}, u32[]{:S(2)}, u32[]{:S(2)}) collective-permute-start(bf16[512,128]{1,0:T(8,128)(2,1)S(1)} %get-tuple-element.24), channel_id=1, source_target_pairs={{0,3},{1,2},{2,1},{3,0},{4,7},{5,6},{6,5},{7,4},{8,11},{9,10},{10,... | collective-permute-start | bytes 393224 | tf_op jit(solution)/shard_map/ppermute | solution.py:31
  104.9 0.0 collective-permute-done.21.x2
  104.9 0.7 collective-permute-start.12
  105.6 0.0 collective-permute-done.22.x3
  105.6 1.8 %collective-permute-start.13 = (bf16[512,128]{1,0:T(8,128)(2,1)S(1)}, bf16[512,128]{1,0:T(8,128)(2,1)S(1)}, u32[]{:S(2)}, u32[]{:S(2)}) collective-permute-start(bf16[512,128]{1,0:T(8,128)(2,1)S(1)} %get-tuple-element.28), channel_id=1, source_target_pairs={{0,2},{1,3},{2,0},{3,1},{4,6},{5,7},{6,4},{7,5},{8,10},{9,11},{10,... | collective-permute-start | bytes 393224 | tf_op jit(solution)/shard_map/ppermute | solution.py:31
  107.4 0.0 collective-permute-done.16.x1
  107.4 1.5 %collective-permute-start.14 = (bf16[512,128]{1,0:T(8,128)(2,1)S(1)}, bf16[512,128]{1,0:T(8,128)(2,1)S(1)}, u32[]{:S(2)}, u32[]{:S(2)}) collective-permute-start(bf16[512,128]{1,0:T(8,128)(2,1)S(1)} %get-tuple-element.27), channel_id=1, source_target_pairs={{0,3},{1,2},{2,1},{3,0},{4,7},{5,6},{6,5},{7,4},{8,11},{9,10},{10,... | collective-permute-start | bytes 393224 | tf_op jit(solution)/shard_map/ppermute | solution.py:31
  108.9 0.0 collective-permute-done.17.x2
  108.9 2.8 %collective-permute-start.10 = (bf16[512,128]{1,0:T(8,128)(2,1)S(1)}, bf16[512,128]{1,0:T(8,128)(2,1)S(1)}, u32[]{:S(2)}, u32[]{:S(2)}) collective-permute-start(bf16[512,128]{1,0:T(8,128)(2,1)S(1)} %get-tuple-element.30), channel_id=1, source_target_pairs={{0,3},{1,2},{2,1},{3,0},{4,7},{5,6},{6,5},{7,4},{8,11},{9,10},{10,... | collective-permute-start | bytes 393224 | tf_op jit(solution)/shard_map/ppermute | solution.py:31
  111.6 0.0 collective-permute-done.18.x3
  111.6 0.0 collective-permute-start.8
  111.6 0.7 collective-permute-done.12.x1
  112.3 4.0 %collective-permute-start.9 = (bf16[512,128]{1,0:T(8,128)(2,1)S(1)}, bf16[512,128]{1,0:T(8,128)(2,1)S(1)}, u32[]{:S(2)}, u32[]{:S(2)}) collective-permute-start(bf16[512,128]{1,0:T(8,128)(2,1)S(1)} %get-tuple-element.31), channel_id=1, source_target_pairs={{0,2},{1,3},{2,0},{3,1},{4,6},{5,7},{6,4},{7,5},{8,10},{9,11},{10,... | collective-permute-start | bytes 393224 | tf_op jit(solution)/shard_map/ppermute | solution.py:31
  116.4 9.6 %update.1._ = bf16[2048,2048]{1,0:T(8,128)(2,1)} custom-call(bf16[2048,2048]{1,0:T(8,128)(2,1)S(1)} %bitcast.10, bf16[512,384]{1,0:T(8,128)(2,1)S(1)} %convolution_convert_fusion.refs_0_, bf16[512,384]{1,0:T(8,128)(2,1)S(1)} %collective-permute-done.refs_1_, bf16[512,384]{1,0:T(8,128)(2,1)S(1)} %collective-permute-done.1.refs_2_, ...), custom_call_target="tpu_custom_call" | custom-call | flops 3221225472 | bytes 20971520 | tf_op jit(solution)/shard_map/update/pallas_call | solution.py:181
  126.0 5.0 %picked_own.1 = (f32[2048,128]{1,0:T(8,128)S(1)}, f32[2048,128]{1,0:T(8,128)S(1)}, f32[2048,128]{1,0:T(8,128)S(1)}, f32[2048,128]{1,0:T(8,128)S(1)}) custom-call(s32[32]{0:T(128)S(1)} %copy-done.2, bf16[512,384]{1,0:T(8,128)(2,1)S(1)} %convolution_convert_fusion.refs_0_, bf16[512,384]{1,0:T(8,128)(2,1)S(1)} %collective-permute-done.refs_1_, ...), custom_call_target="tpu_custom_call" | custom-call | flops 805306368 | bytes 10485760 | tf_op jit(solution)/shard_map/picked_own/pallas_call | solution.py:140
  131.0 1.3 place.4._
  132.3 1.3 place.5._
  133.7 0.0 collective-permute-done.13.x2
  133.7 0.0 collective-permute-done.14.x3
  133.7 1.3 place.6._
  135.0 0.0 collective-permute-done.10.x3
  135.0 0.0 collective-permute-done.8.x1
  135.1 0.0 collective-permute-done.9.x2
  135.1 1.3 place.7
  (4 shorter events, 0.1 us)
Async XLA Ops:
  0.0 1.0 copy-start
  2.4 9.1 %collective-permute-start.3 = (bf16[512,384]{1,0:T(8,128)(2,1)S(1)}, bf16[512,384]{1,0:T(8,128)(2,1)S(1)}, u32[]{:S(2)}, u32[]{:S(2)}) collective-permute-start(bf16[512,384]{1,0:T(8,128)(2,1)S(1)} %convolution_convert_fusion.refs_0_), channel_id=1, source_target_pairs={{0,0},{1,4},{2,8},{3,12},{4,1},{5,5},{6,9},{7,13},{8,2},{9,6},{10,... | collective-permute-start | bytes 1179656 | tf_op jit(solution)/shard_map/ppermute | solution.py:31
  11.5 15.2 %collective-permute-start.5 = (bf16[512,384]{1,0:T(8,128)(2,1)S(1)}, bf16[512,384]{1,0:T(8,128)(2,1)S(1)}, u32[]{:S(2)}, u32[]{:S(2)}) collective-permute-start(bf16[512,384]{1,0:T(8,128)(2,1)S(1)} %collective-permute-done.3.refs_4_), channel_id=1, source_target_pairs={{0,8},{1,9},{2,10},{3,11},{4,12},{5,13},{6,14},{7,15},{8,0},{9,1},... | collective-permute-start | bytes 1179656 | tf_op jit(solution)/shard_map/ppermute | solution.py:31
  19.4 11.1 %collective-permute-start = (bf16[512,384]{1,0:T(8,128)(2,1)S(1)}, bf16[512,384]{1,0:T(8,128)(2,1)S(1)}, u32[]{:S(2)}, u32[]{:S(2)}) collective-permute-start(bf16[512,384]{1,0:T(8,128)(2,1)S(1)} %convolution_convert_fusion.refs_0_), channel_id=1, source_target_pairs={{0,1},{1,0},{2,3},{3,2},{4,5},{5,4},{6,7},{7,6},{8,9},{9,8},{10,11... | collective-permute-start | bytes 1179656 | tf_op jit(solution)/shard_map/ppermute | solution.py:31
  19.4 15.8 %collective-permute-start.1 = (bf16[512,384]{1,0:T(8,128)(2,1)S(1)}, bf16[512,384]{1,0:T(8,128)(2,1)S(1)}, u32[]{:S(2)}, u32[]{:S(2)}) collective-permute-start(bf16[512,384]{1,0:T(8,128)(2,1)S(1)} %convolution_convert_fusion.refs_0_), channel_id=1, source_target_pairs={{0,2},{1,3},{2,0},{3,1},{4,6},{5,7},{6,4},{7,5},{8,10},{9,11},{10,... | collective-permute-start | bytes 1179656 | tf_op jit(solution)/shard_map/ppermute | solution.py:31
  19.4 20.9 %collective-permute-start.2 = (bf16[512,384]{1,0:T(8,128)(2,1)S(1)}, bf16[512,384]{1,0:T(8,128)(2,1)S(1)}, u32[]{:S(2)}, u32[]{:S(2)}) collective-permute-start(bf16[512,384]{1,0:T(8,128)(2,1)S(1)} %convolution_convert_fusion.refs_0_), channel_id=1, source_target_pairs={{0,3},{1,2},{2,1},{3,0},{4,7},{5,6},{6,5},{7,4},{8,11},{9,10},{10,... | collective-permute-start | bytes 1179656 | tf_op jit(solution)/shard_map/ppermute | solution.py:31
  23.3 17.0 %collective-permute-start.4 = (bf16[512,384]{1,0:T(8,128)(2,1)S(1)}, bf16[512,384]{1,0:T(8,128)(2,1)S(1)}, u32[]{:S(2)}, u32[]{:S(2)}) collective-permute-start(bf16[512,384]{1,0:T(8,128)(2,1)S(1)} %collective-permute-done.3.refs_4_), channel_id=1, source_target_pairs={{0,4},{1,5},{2,6},{3,7},{4,0},{5,1},{6,2},{7,3},{8,12},{9,13},{10,... | collective-permute-start | bytes 1179656 | tf_op jit(solution)/shard_map/ppermute | solution.py:31
  26.7 13.6 %collective-permute-start.6 = (bf16[512,384]{1,0:T(8,128)(2,1)S(1)}, bf16[512,384]{1,0:T(8,128)(2,1)S(1)}, u32[]{:S(2)}, u32[]{:S(2)}) collective-permute-start(bf16[512,384]{1,0:T(8,128)(2,1)S(1)} %collective-permute-done.5.refs_6_), channel_id=1, source_target_pairs={{0,4},{1,5},{2,6},{3,7},{4,0},{5,1},{6,2},{7,3},{8,12},{9,13},{10,... | collective-permute-start | bytes 1179656 | tf_op jit(solution)/shard_map/ppermute | solution.py:31
  40.3 3.4 %copy-start.1 = (bf16[1,2048,2048]{2,1,0:T(8,128)(2,1)S(1)}, bf16[1,2048,2048]{2,1,0:T(8,128)(2,1)}, u32[]{:S(2)}) copy-start(bf16[1,2048,2048]{2,1,0:T(8,128)(2,1)} %param.5) | copy-start | bytes 25165828
  43.7 0.7 copy-start.2
  48.6 17.5 %collective-permute-start.19 = (bf16[2048,128]{1,0:T(8,128)(2,1)S(1)}, bf16[2048,128]{1,0:T(8,128)(2,1)S(1)}, u32[]{:S(2)}, u32[]{:S(2)}) collective-permute-start(bf16[2048,128]{1,0:T(8,128)(2,1)S(1)} %get-tuple-element.20), channel_id=1, source_target_pairs={{16,0},{17,1},{18,2},{19,3},{20,4},{21,5},{22,6},{23,7},{24,8},{25... | collective-permute-start | bytes 1572872 | tf_op jit(solution)/shard_map/ppermute | solution.py:31
  51.0 31.6 %collective-permute-start.15 = (bf16[2048,128]{1,0:T(8,128)(2,1)S(1)}, bf16[2048,128]{1,0:T(8,128)(2,1)S(1)}, u32[]{:S(2)}, u32[]{:S(2)}) collective-permute-start(bf16[2048,128]{1,0:T(8,128)(2,1)S(1)} %get-tuple-element.18), channel_id=1, source_target_pairs={{16,4},{17,5},{18,6},{19,7},{20,0},{21,1},{22,2},{23,3},{24,12},{2... | collective-permute-start | bytes 1572872 | tf_op jit(solution)/shard_map/ppermute | solution.py:31
  54.7 32.8 %collective-permute-start.11 = (bf16[2048,128]{1,0:T(8,128)(2,1)S(1)}, bf16[2048,128]{1,0:T(8,128)(2,1)S(1)}, u32[]{:S(2)}, u32[]{:S(2)}) collective-permute-start(bf16[2048,128]{1,0:T(8,128)(2,1)S(1)} %get-tuple-element.16), channel_id=1, source_target_pairs={{16,8},{17,9},{18,10},{19,11},{20,12},{21,13},{22,14},{23,15},{24,... | collective-permute-start | bytes 1572872 | tf_op jit(solution)/shard_map/ppermute | solution.py:31
  56.7 44.8 %collective-permute-start.7 = (bf16[2048,128]{1,0:T(8,128)(2,1)S(1)}, bf16[2048,128]{1,0:T(8,128)(2,1)S(1)}, u32[]{:S(2)}, u32[]{:S(2)}) collective-permute-start(bf16[2048,128]{1,0:T(8,128)(2,1)S(1)} %get-tuple-element.14), channel_id=1, source_target_pairs={{16,12},{17,13},{18,14},{19,15},{20,8},{21,9},{22,10},{23,11},{24,... | collective-permute-start | bytes 1572872 | tf_op jit(solution)/shard_map/ppermute | solution.py:31
  66.1 35.4 %collective-permute-start.20 = (bf16[512,128]{1,0:T(8,128)(2,1)S(1)}, bf16[512,128]{1,0:T(8,128)(2,1)S(1)}, u32[]{:S(2)}, u32[]{:S(2)}) collective-permute-start(bf16[512,128]{1,0:T(8,128)(2,1)S(1)} %get-tuple-element.23), channel_id=1, source_target_pairs={{0,1},{1,0},{2,3},{3,2},{4,5},{5,4},{6,7},{7,6},{8,9},{9,8},{10,11... | collective-permute-start | bytes 393224 | tf_op jit(solution)/shard_map/ppermute | solution.py:31
  66.2 38.7 %collective-permute-start.21 = (bf16[512,128]{1,0:T(8,128)(2,1)S(1)}, bf16[512,128]{1,0:T(8,128)(2,1)S(1)}, u32[]{:S(2)}, u32[]{:S(2)}) collective-permute-start(bf16[512,128]{1,0:T(8,128)(2,1)S(1)} %get-tuple-element.22), channel_id=1, source_target_pairs={{0,2},{1,3},{2,0},{3,1},{4,6},{5,7},{6,4},{7,5},{8,10},{9,11},{10,... | collective-permute-start | bytes 393224 | tf_op jit(solution)/shard_map/ppermute | solution.py:31
  82.6 23.0 %collective-permute-start.22 = (bf16[512,128]{1,0:T(8,128)(2,1)S(1)}, bf16[512,128]{1,0:T(8,128)(2,1)S(1)}, u32[]{:S(2)}, u32[]{:S(2)}) collective-permute-start(bf16[512,128]{1,0:T(8,128)(2,1)S(1)} %get-tuple-element.21), channel_id=1, source_target_pairs={{0,3},{1,2},{2,1},{3,0},{4,7},{5,6},{6,5},{7,4},{8,11},{9,10},{10,... | collective-permute-start | bytes 393224 | tf_op jit(solution)/shard_map/ppermute | solution.py:31
  87.4 19.9 %collective-permute-start.16 = (bf16[512,128]{1,0:T(8,128)(2,1)S(1)}, bf16[512,128]{1,0:T(8,128)(2,1)S(1)}, u32[]{:S(2)}, u32[]{:S(2)}) collective-permute-start(bf16[512,128]{1,0:T(8,128)(2,1)S(1)} %get-tuple-element.26), channel_id=1, source_target_pairs={{0,1},{1,0},{2,3},{3,2},{4,5},{5,4},{6,7},{7,6},{8,9},{9,8},{10,11... | collective-permute-start | bytes 393224 | tf_op jit(solution)/shard_map/ppermute | solution.py:31
  101.5 7.4 %collective-permute-start.17 = (bf16[512,128]{1,0:T(8,128)(2,1)S(1)}, bf16[512,128]{1,0:T(8,128)(2,1)S(1)}, u32[]{:S(2)}, u32[]{:S(2)}) collective-permute-start(bf16[512,128]{1,0:T(8,128)(2,1)S(1)} %get-tuple-element.25), channel_id=1, source_target_pairs={{0,2},{1,3},{2,0},{3,1},{4,6},{5,7},{6,4},{7,5},{8,10},{9,11},{10,... | collective-permute-start | bytes 393224 | tf_op jit(solution)/shard_map/ppermute | solution.py:31
  101.5 10.2 %collective-permute-start.18 = (bf16[512,128]{1,0:T(8,128)(2,1)S(1)}, bf16[512,128]{1,0:T(8,128)(2,1)S(1)}, u32[]{:S(2)}, u32[]{:S(2)}) collective-permute-start(bf16[512,128]{1,0:T(8,128)(2,1)S(1)} %get-tuple-element.24), channel_id=1, source_target_pairs={{0,3},{1,2},{2,1},{3,0},{4,7},{5,6},{6,5},{7,4},{8,11},{9,10},{10,... | collective-permute-start | bytes 393224 | tf_op jit(solution)/shard_map/ppermute | solution.py:31
  104.9 7.5 %collective-permute-start.12 = (bf16[512,128]{1,0:T(8,128)(2,1)S(1)}, bf16[512,128]{1,0:T(8,128)(2,1)S(1)}, u32[]{:S(2)}, u32[]{:S(2)}) collective-permute-start(bf16[512,128]{1,0:T(8,128)(2,1)S(1)} %get-tuple-element.29), channel_id=1, source_target_pairs={{0,1},{1,0},{2,3},{3,2},{4,5},{5,4},{6,7},{7,6},{8,9},{9,8},{10,11... | collective-permute-start | bytes 393224 | tf_op jit(solution)/shard_map/ppermute | solution.py:31
  105.6 28.1 %collective-permute-start.13 = (bf16[512,128]{1,0:T(8,128)(2,1)S(1)}, bf16[512,128]{1,0:T(8,128)(2,1)S(1)}, u32[]{:S(2)}, u32[]{:S(2)}) collective-permute-start(bf16[512,128]{1,0:T(8,128)(2,1)S(1)} %get-tuple-element.28), channel_id=1, source_target_pairs={{0,2},{1,3},{2,0},{3,1},{4,6},{5,7},{6,4},{7,5},{8,10},{9,11},{10,... | collective-permute-start | bytes 393224 | tf_op jit(solution)/shard_map/ppermute | solution.py:31
  107.4 26.3 %collective-permute-start.14 = (bf16[512,128]{1,0:T(8,128)(2,1)S(1)}, bf16[512,128]{1,0:T(8,128)(2,1)S(1)}, u32[]{:S(2)}, u32[]{:S(2)}) collective-permute-start(bf16[512,128]{1,0:T(8,128)(2,1)S(1)} %get-tuple-element.27), channel_id=1, source_target_pairs={{0,3},{1,2},{2,1},{3,0},{4,7},{5,6},{6,5},{7,4},{8,11},{9,10},{10,... | collective-permute-start | bytes 393224 | tf_op jit(solution)/shard_map/ppermute | solution.py:31
  108.9 26.2 %collective-permute-start.10 = (bf16[512,128]{1,0:T(8,128)(2,1)S(1)}, bf16[512,128]{1,0:T(8,128)(2,1)S(1)}, u32[]{:S(2)}, u32[]{:S(2)}) collective-permute-start(bf16[512,128]{1,0:T(8,128)(2,1)S(1)} %get-tuple-element.30), channel_id=1, source_target_pairs={{0,3},{1,2},{2,1},{3,0},{4,7},{5,6},{6,5},{7,4},{8,11},{9,10},{10,... | collective-permute-start | bytes 393224 | tf_op jit(solution)/shard_map/ppermute | solution.py:31
  111.6 23.4 %collective-permute-start.8 = (bf16[512,128]{1,0:T(8,128)(2,1)S(1)}, bf16[512,128]{1,0:T(8,128)(2,1)S(1)}, u32[]{:S(2)}, u32[]{:S(2)}) collective-permute-start(bf16[512,128]{1,0:T(8,128)(2,1)S(1)} %get-tuple-element.32), channel_id=1, source_target_pairs={{0,1},{1,0},{2,3},{3,2},{4,5},{5,4},{6,7},{7,6},{8,9},{9,8},{10,11... | collective-permute-start | bytes 393224 | tf_op jit(solution)/shard_map/ppermute | solution.py:31
  112.3 22.7 %collective-permute-start.9 = (bf16[512,128]{1,0:T(8,128)(2,1)S(1)}, bf16[512,128]{1,0:T(8,128)(2,1)S(1)}, u32[]{:S(2)}, u32[]{:S(2)}) collective-permute-start(bf16[512,128]{1,0:T(8,128)(2,1)S(1)} %get-tuple-element.31), channel_id=1, source_target_pairs={{0,2},{1,3},{2,0},{3,1},{4,6},{5,7},{6,4},{7,5},{8,10},{9,11},{10,... | collective-permute-start | bytes 393224 | tf_op jit(solution)/shard_map/ppermute | solution.py:31

commit v2 on v1

v2 whole, which is shorter than its diff:
```python
import functools

import jax
import jax.numpy as jnp
from jax import lax
from jax.experimental import pallas as pl
from jax.experimental.pallas import tpu as pltpu
from jax.sharding import PartitionSpec as P

BLK = 128
AXES = ("group", "row", "col")
ANY = pl.BlockSpec(memory_space=pl.ANY)
SMEM = pl.BlockSpec(memory_space=pltpu.SMEM)
VMEM = pl.BlockSpec(memory_space=pltpu.VMEM)
DEPTH = (((1,), (1,)), ((), ()))


def params(mib):
    return pltpu.CompilerParams(vmem_limit_bytes=mib << 20)


def move(array, target):
    groups, rows, cols = (lax.axis_size(axis) for axis in AXES)
    pairs = []
    for g in range(groups):
        for r in range(rows):
            for c in range(cols):
                to = target(g, r, c)
                if to is not None and to[0] >= 0:
                    tg, tr, tc = to
                    pairs.append(((g * rows + r) * cols + c, (tg * rows + tr) * cols + tc))
    return lax.ppermute(array, AXES, pairs)


def codes(map_ref, mask_ref, group, run, span):
    out = []
    for k in range(span):
        target = map_ref[group, run * span + k]
        live = mask_ref[group, run * span + k] == 1
        out.append((jnp.where(live, target // span, -1), target * span + k))
    return out


def ends(coded, run):
    low, high = jnp.int32(1 << 20), jnp.int32(-1)
    for to, code in coded:
        hit = to == run
        low = jnp.minimum(low, jnp.where(hit, code, 1 << 20))
        high = jnp.maximum(high, jnp.where(hit, code, -1))
    return low, high


def plan_kernel(map_ref, mask_ref, out_ref):
    count = map_ref.shape[1]
    runs = lax.axis_size("row")
    span = count // runs
    group = lax.axis_index("group")
    child = jnp.minimum(group + 1, map_ref.shape[0] - 1)
    for position, axis in enumerate(("row", "col")):
        me = lax.axis_index(axis)
        own = codes(map_ref, mask_ref, group, me, span)
        for run in range(runs):
            for i, code in enumerate(ends(own, run)):
                out_ref[position * 2 * runs + 2 * run + i] = lax.rem(code, span)
        for d in range(runs):
            for i, code in enumerate(ends(codes(map_ref, mask_ref, child, me ^ d, span), me)):
                out_ref[(position + 2) * 2 * runs + 2 * d + i] = code // span - me * span


def plan(child_map, child_mask):
    return pl.pallas_call(
        plan_kernel,
        out_shape=jax.ShapeDtypeStruct((32,), jnp.int32),
        in_specs=[SMEM, SMEM],
        out_specs=SMEM,
        compiler_params=params(16),
        name="plan",
    )(child_map, child_mask)


def load_factor(shards, rows_v, cols_v):
    size = shards[0].shape[0]
    half = size // 2
    row, col = lax.axis_index("row"), lax.axis_index("col")
    alike = lax.rem(row + col, 2) == 0
    places = [((col ^ d) * size, size) for d in (0, 1, 3)] + [((col ^ 2) * size + n * half, half) for n in range(2)]
    for ref, (start, count) in zip(shards[:5], places):
        rows_v[pl.ds(pl.multiple_of(start, half), count), :] = ref[...]
    for d in range(4):
        place = pl.ds(pl.multiple_of((col ^ d) * size, size), size)

        @pl.when(alike)
        def _():
            cols_v[place, :] = shards[5 + 2 * d][...]

        @pl.when(jnp.logical_not(alike))
        def _():
            cols_v[place, :] = shards[6 + 2 * d][...]


def pack_kernel(idx, frontal, out, sem):
    row, col = lax.axis_index("row"), lax.axis_index("col")
    row_at = [pl.multiple_of(idx[2 * (row ^ d) + i] * BLK, BLK) for d in range(4) for i in range(2)]
    col_at = [pl.multiple_of(idx[8 + 2 * (col ^ e) + j] * BLK, BLK) for e in range(4) for j in range(2)]
    for a in range(8):
        for b in range(8):
            pltpu.make_async_copy(
                frontal.at[pl.ds(row_at[a], BLK), pl.ds(col_at[b], BLK)], out.at[a * 8 + b], sem
            ).start()
    pltpu.make_async_copy(out, out, sem).wait()


def pack(idx, frontal):
    return pl.pallas_call(
        pack_kernel,
        out_shape=jax.ShapeDtypeStruct((64, BLK, BLK), frontal.dtype),
        in_specs=[SMEM, ANY],
        out_specs=VMEM,
        scratch_shapes=[pltpu.SemaphoreType.DMA],
        compiler_params=params(16),
        cost_estimate=pl.CostEstimate(flops=0, bytes_accessed=4 << 20, transcendentals=0),
        name="pack",
    )(idx, frontal)


def picked_kernel(idx, *refs):
    shards, packed = refs[:13], refs[13]
    outs = refs[14:21]
    rows_v, cols_v, pick_v = refs[21:]
    row, col = lax.axis_index("row"), lax.axis_index("col")
    load_factor(shards, rows_v, cols_v)
    row_at = [pl.multiple_of(idx[2 * (row ^ d) + i] * BLK, BLK) for d in range(4) for i in range(2)]
    col_at = [pl.multiple_of(idx[8 + 2 * (col ^ e) + j] * BLK, BLK) for e in range(4) for j in range(2)]
    for b in range(8):
        pick_v[b * BLK : (b + 1) * BLK, :] = cols_v[pl.ds(col_at[b], BLK), :]
    for d in range(4):
        left = jnp.concatenate([rows_v[pl.ds(row_at[2 * d + i], BLK), :] for i in range(2)], axis=0)
        product = lax.dot_general(left, pick_v[...], DEPTH, preferred_element_type=jnp.float32)
        for e in range(4):
            for i in range(2):
                for j in range(2):
                    b = 2 * e + j
                    value = packed[(2 * d + i) * 8 + b].astype(jnp.float32)
                    value = value - product[i * BLK : (i + 1) * BLK, b * BLK : (b + 1) * BLK]
                    if d < 3:
                        ref, at = outs[d], (e * 2 + i) * 2 + j
                    else:
                        ref, at = outs[3 + e], i * 2 + j
                    ref[at * BLK : (at + 1) * BLK, :] = value.astype(jnp.bfloat16)


def picked(idx, shards, packed):
    size, depth = shards[0].shape
    return pl.pallas_call(
        picked_kernel,
        out_shape=[jax.ShapeDtypeStruct((blocks * BLK, BLK), jnp.bfloat16) for blocks in (16, 16, 16, 4, 4, 4, 4)],
        in_specs=[SMEM] + [VMEM] * 14,
        out_specs=[VMEM] * 7,
        scratch_shapes=[
            pltpu.VMEM((4 * size, depth), jnp.bfloat16),
            pltpu.VMEM((4 * size, depth), jnp.bfloat16),
            pltpu.VMEM((8 * BLK, depth), jnp.bfloat16),
        ],
        compiler_params=params(24),
        cost_estimate=pl.CostEstimate(flops=2 * 1024 * 1024 * 384, bytes_accessed=8 << 20, transcendentals=0),
        name="picked",
    )(idx, *shards, packed)


def update_kernel(idx, frontal, *refs):
    shards, out, owns = refs[:13], refs[13], refs[14:18]
    rows_v, cols_v, whole_v = refs[18:]
    step = pl.program_id(0)

    @pl.when(step == 0)
    def _():
        load_factor(shards, rows_v, cols_v)

    high = out.shape[0]
    left = rows_v[pl.ds(pl.multiple_of(step * high, high), high), :]
    product = lax.dot_general(left, cols_v[...], DEPTH, preferred_element_type=jnp.float32)
    value = frontal[...].astype(jnp.float32) - product
    out[...] = value.astype(jnp.bfloat16)
    whole_v[...] = value
    per = high // BLK
    for d in range(4):
        for i in range(2):
            at = idx[16 + 2 * d + i]

            @pl.when(at // per == step)
            def _():
                strip = pl.ds(pl.multiple_of(lax.rem(at, per) * BLK, BLK), BLK)
                for e in range(4):
                    for j in range(2):
                        k = ((e * 2 + i) * 2 + j) * BLK
                        wide = pl.ds(pl.multiple_of(idx[24 + 2 * e + j] * BLK, BLK), BLK)
                        owns[d][k : k + BLK, :] = whole_v[strip, wide]


def updated(idx, shards, frontal):
    tile, depth = frontal.shape[0], shards[0].shape[1]
    high = 512
    block = pl.BlockSpec((high, tile), lambda s: (s, 0))
    return pl.pallas_call(
        update_kernel,
        out_shape=[jax.ShapeDtypeStruct((tile, tile), jnp.bfloat16)]
        + [jax.ShapeDtypeStruct((16 * BLK, BLK), jnp.float32)] * 4,
        grid=(tile // high,),
        in_specs=[SMEM, block] + [VMEM] * 13,
        out_specs=[block] + [VMEM] * 4,
        scratch_shapes=[
            pltpu.VMEM((tile, depth), jnp.bfloat16),
            pltpu.VMEM((tile, depth), jnp.bfloat16),
            pltpu.VMEM((high, tile), jnp.float32),
        ],
        compiler_params=params(40),
        cost_estimate=pl.CostEstimate(flops=2 * tile * tile * depth, bytes_accessed=24 << 20, transcendentals=0),
        name="update",
    )(idx, frontal, *shards)


def place_kernel(first, count, split, idx, *refs):
    owns, parts = refs[:count], refs[count : count + split]
    out, block_v, sem = refs[count + split + 1 :]
    for n in range(count):
        for e in range(4):
            for i in range(2):
                for j in range(2):
                    k = (e * 2 + i) * 2 + j
                    if split == count:
                        ref, at = parts[n], k
                    elif e == 0:
                        ref, at = parts[n], i * 2 + j
                    else:
                        ref, at = parts[count + e - 1], (n * 2 + i) * 2 + j
                    value = owns[n][k * BLK : (k + 1) * BLK, :]
                    value = value + ref[at * BLK : (at + 1) * BLK, :].astype(jnp.float32)
                    block_v[n * 16 + k] = value.astype(jnp.bfloat16)
                    pltpu.make_async_copy(
                        block_v.at[n * 16 + k],
                        out.at[
                            pl.ds(pl.multiple_of(idx[16 + 2 * (first + n) + i] * BLK, BLK), BLK),
                            pl.ds(pl.multiple_of(idx[24 + 2 * e + j] * BLK, BLK), BLK),
                        ],
                        sem,
                    ).start()
    pltpu.make_async_copy(block_v, block_v, sem).wait()


def placed(idx, first, own, parts, out):
    count, split = len(own), len(parts)

    return pl.pallas_call(
        functools.partial(place_kernel, first, count, split),
        out_shape=jax.ShapeDtypeStruct(out.shape, out.dtype),
        in_specs=[SMEM] + [VMEM] * (count + split) + [ANY],
        out_specs=ANY,
        scratch_shapes=[pltpu.VMEM((16 * count, BLK, BLK), jnp.bfloat16), pltpu.SemaphoreType.DMA],
        input_output_aliases={count + split + 1: 0},
        compiler_params=params(12),
        cost_estimate=pl.CostEstimate(flops=1 << 18, bytes_accessed=count << 21, transcendentals=0),
        name="place",
    )(idx, *own, *parts, out)


def after(array, *done):
    return lax.optimization_barrier((array, *done))[0]


def on_device(frontal, panel_cols, inv_factor, child_map, child_mask):
    front = frontal[0]
    quarter = 4 * BLK

    def hop(d, array):
        return move(array, lambda g, r, c: (g - 1, r ^ d, c))

    def flip_row(d, array):
        return move(array, lambda g, r, c: (g, r ^ d, c))

    def flip_col(d, array):
        return move(array, lambda g, r, c: (g, r, c ^ d))

    factor = lax.dot_general(panel_cols[0], inv_factor[0], DEPTH, preferred_element_type=jnp.float32).astype(
        jnp.bfloat16
    )
    across = flip_row(2, factor)
    near = [flip_col(1, factor), flip_col(3, factor)]
    idx = plan(child_map, child_mask)
    packed = pack(idx, front)
    row, col = lax.axis_index("row"), lax.axis_index("col")
    same = row // 2 == col // 2
    alike = (row + col) % 2 == 0
    across = after(across, packed, *near)
    low, high = jnp.where(same, factor, across), jnp.where(same, across, factor)
    half = factor.shape[0] // 2
    by_col = [factor, *near, flip_col(1, near[1][:half]), flip_col(3, near[0][half:])]
    third = move(high, lambda g, r, c: (g, r, c ^ 3) if (r + c) % 2 else None)
    one = move(
        jnp.where(alike, high, low), lambda g, r, c: (g, r ^ 1, c ^ 1) if (r + c) % 2 else (g, r, c ^ 2)
    )

    def swap(array):
        return move(array, lambda g, r, c: None if (r + c) % 2 else (g, r ^ 1, c))

    other = flip_row(1, after(one, *by_col[3:]))
    shards = by_col + [low, swap(low), other, one, one, other, third, swap(after(third, *by_col[3:]))]
    sent = picked(idx, shards, packed)
    came = [hop(d, sent[d]) for d in range(3)]
    crossed = [sent[3]] + [flip_col(e, sent[3 + e]) for e in (1, 2, 3)]
    came.append(hop(3, jnp.concatenate(crossed)))
    out, *own = updated(idx, shards, after(front, came[0]))
    for changes in ((0, 1), (2,)):
        parts = [came[d] for d in changes]
        for e in (1, 2, 3):
            blocks = [came[d][e * quarter : (e + 1) * quarter] for d in changes]
            blocks = jnp.concatenate(blocks) if len(blocks) > 1 else blocks[0]
            parts.append(flip_col(e, after(blocks, own[0])))
        out = placed(idx, changes[0], [own[d] for d in changes], parts, out)
    return placed(idx, 3, own[3:], came[3:], out)[None]


def solution(mesh):
    specs = (
        P("group", "row", "col"),
        P("group", ("row", "col"), None),
        P("group", None, None),
        P(),
        P(),
    )
    return jax.shard_map(
        on_device, mesh=mesh, in_specs=specs, out_specs=P("group", "row", "col"), check_vma=False
    )
```

time: 137 us -> 99.7 us (0.73)
  the two profiles are of different devices: /device:TPU:25 before, /device:TPU:72 now
where the time goes in v2:
time: 99.7 us; the launch traced here: 98.2 us
  starting transfers between devices  41.4 us (42%)
  waiting for transfers between devices  27.7 us (28%)
  Pallas kernels  21.3 us (21%)
  local copies, waits for them, and re-layouts  5.87 us (6%)
  matrix products  1.36 us (1%)
    ppermute x23, starting transfers between devices, move(): return lax.ppermute(array, AXES, pairs)  41.4 us
    ppermute x23, waiting for transfers between devices, move(): return lax.ppermute(array, AXES, pairs)  27.7 us
    pallas_call x1, Pallas kernels, updated(): pl.pallas_call(update_kernel, out_shape=[jax.ShapeDtypeStruct((tile, tile...  10.4 us
    unnamed x8, local copies, waits for them, and re-layouts  5.75 us
    pallas_call x3, Pallas kernels, placed(): pl.pallas_call(functools.partial(place_kernel, first, count, split), out_...  4.16 us
    pallas_call x1, Pallas kernels, plan(): pl.pallas_call(plan_kernel, out_shape=jax.ShapeDtypeStruct((32,), jnp.int...  3.28 us
    pallas_call x1, Pallas kernels, picked(): pl.pallas_call(picked_kernel, out_shape=[jax.ShapeDtypeStruct((blocks * B...  2.16 us
  transfers between devices with their start and end apart: 23, of which 8 were waited for; matrix products, arithmetic and copies ran while one was open for 0% of the time, Pallas kernels for 18%

profile of v2, /device:TPU:72, one launch (start us, length us, event | category | flops | bytes accessed | tf_op | source)
XLA Modules:
  0.0 98.2 jit_solution(12396559798269639583)
XLA Ops:
  0.0 0.0 copy-start
  0.0 1.0 %copy-done = bf16[1,512,384]{2,1,0:T(8,128)(2,1)S(1)} copy-done((bf16[1,512,384]{2,1,0:T(8,128)(2,1)S(1)}, bf16[1,512,384]{2,1,0:T(8,128)(2,1)}, u32[]{:S(2)}) %copy-start) | copy-done | bytes 393240
  1.0 1.4 %convolution_convert_fusion.refs_0_ = bf16[512,384]{1,0:T(8,128)(2,1)S(1)} fusion(bf16[1,512,384]{2,1,0:T(8,128)(2,1)S(1)} %copy-done, bf16[1,384,384]{2,1,0:T(8,128)(2,1)} %param.7), kind=kOutput, calls=%fused_computation | convolution fusion | flops 151191552 | bytes 1081344 | tf_op jit(solution)/shard_map/dot_general | solution.py:283
  2.4 1.6 %collective-permute-start = (bf16[512,384]{1,0:T(8,128)(2,1)S(1)}, bf16[512,384]{1,0:T(8,128)(2,1)S(1)}, u32[]{:S(2)}, u32[]{:S(2)}) collective-permute-start(bf16[512,384]{1,0:T(8,128)(2,1)S(1)} %convolution_convert_fusion.refs_0_), channel_id=1, source_target_pairs={{0,1},{1,0},{2,3},{3,2},{4,5},{5,4},{6,7},{7,6},{8,9},{9,8},{10,11... | collective-permute-start | bytes 1179656 | tf_op jit(solution)/shard_map/ppermute | solution.py:32
  3.9 2.1 %collective-permute-start.1 = (bf16[512,384]{1,0:T(8,128)(2,1)S(1)}, bf16[512,384]{1,0:T(8,128)(2,1)S(1)}, u32[]{:S(2)}, u32[]{:S(2)}) collective-permute-start(bf16[512,384]{1,0:T(8,128)(2,1)S(1)} %convolution_convert_fusion.refs_0_), channel_id=1, source_target_pairs={{0,3},{1,2},{2,1},{3,0},{4,7},{5,6},{6,5},{7,4},{8,11},{9,10},{10,... | collective-permute-start | bytes 1179656 | tf_op jit(solution)/shard_map/ppermute | solution.py:32
  6.0 1.6 %collective-permute-start.4 = (bf16[512,384]{1,0:T(8,128)(2,1)S(1)}, bf16[512,384]{1,0:T(8,128)(2,1)S(1)}, u32[]{:S(2)}, u32[]{:S(2)}) collective-permute-start(bf16[512,384]{1,0:T(8,128)(2,1)S(1)} %convolution_convert_fusion.refs_0_), channel_id=1, source_target_pairs={{0,8},{1,9},{2,10},{3,11},{4,12},{5,13},{6,14},{7,15},{8,0},{9,1},... | collective-permute-start | bytes 1179656 | tf_op jit(solution)/shard_map/ppermute | solution.py:32
  7.7 0.0 copy-start.2
  7.7 0.7 copy-done.2
  8.3 0.0 copy-start.3
  8.3 0.7 copy-done.3
  9.0 3.3 %plan.1.idx = s32[32]{0:T(128)S(1)} custom-call(s32[8,64]{1,0:T(8,128)S(1)} %copy-done.2, s32[8,64]{1,0:T(8,128)S(1)} %copy-done.3), custom_call_target="tpu_custom_call" | custom-call | tf_op jit(solution)/shard_map/plan/pallas_call | solution.py:71
  12.3 0.0 copy-start.1
  12.3 3.4 %copy-done.1 = bf16[1,2048,2048]{2,1,0:T(8,128)(2,1)S(1)} copy-done((bf16[1,2048,2048]{2,1,0:T(8,128)(2,1)S(1)}, bf16[1,2048,2048]{2,1,0:T(8,128)(2,1)}, u32[]{:S(2)}) %copy-start.1) | copy-done | bytes 8388632
  15.7 1.3 %pack.1.refs_13_ = bf16[64,128,128]{2,1,0:T(8,128)(2,1)S(1)} custom-call(s32[32]{0:T(128)S(1)} %plan.1.idx, bf16[2048,2048]{1,0:T(8,128)(2,1)S(1)} %bitcast.9), custom_call_target="tpu_custom_call" | custom-call | bytes 4194304 | tf_op jit(solution)/shard_map/pack/pallas_call | solution.py:114
  17.0 0.0 collective-permute-done.refs_1_
  17.0 0.0 collective-permute-done.1.refs_2_
  17.0 0.0 collective-permute-done.4
  17.0 0.1 broadcast_select_fusion
  17.1 1.3 %collective-permute-start.8 = (bf16[512,384]{1,0:T(8,128)(2,1)S(1)}, bf16[512,384]{1,0:T(8,128)(2,1)S(1)}, u32[]{:S(2)}, u32[]{:S(2)}) collective-permute-start(bf16[512,384]{1,0:T(8,128)(2,1)S(1)} %get-tuple-element.50), channel_id=1, source_target_pairs={{1,2},{3,0},{4,7},{6,5},{9,10},{11,8},{12,15},{14,13},{17,18},{19,... | collective-permute-start | bytes 1179656 | tf_op jit(solution)/shard_map/ppermute | solution.py:32
  18.4 0.7 collective-permute-start.6
  19.2 1.6 %collective-permute-start.2 = (bf16[256,384]{1,0:T(8,128)(2,1)S(1)}, bf16[256,384]{1,0:T(8,128)(2,1)S(1)}, u32[]{:S(2)}, u32[]{:S(2)}) collective-permute-start(bf16[256,384]{1,0:T(8,128)(2,1)S(1)} %slice.44), channel_id=1, source_target_pairs={{0,1},{1,0},{2,3},{3,2},{4,5},{5,4},{6,7},{7,6},{8,9},{9,8},{10,11... | collective-permute-start | bytes 589832 | tf_op jit(solution)/shard_map/ppermute | solution.py:32
  20.8 2.0 %collective-permute-start.3 = (bf16[256,384]{1,0:T(8,128)(2,1)S(1)}, bf16[256,384]{1,0:T(8,128)(2,1)S(1)}, u32[]{:S(2)}, u32[]{:S(2)}) collective-permute-start(bf16[256,384]{1,0:T(8,128)(2,1)S(1)} %slice.45), channel_id=1, source_target_pairs={{0,3},{1,2},{2,1},{3,0},{4,7},{5,6},{6,5},{7,4},{8,11},{9,10},{10,... | collective-permute-start | bytes 589832 | tf_op jit(solution)/shard_map/ppermute | solution.py:32
  22.8 3.3 %collective-permute-start.5 = (bf16[512,384]{1,0:T(8,128)(2,1)S(1)}, bf16[512,384]{1,0:T(8,128)(2,1)S(1)}, u32[]{:S(2)}, u32[]{:S(2)}) collective-permute-start(bf16[512,384]{1,0:T(8,128)(2,1)S(1)} %get-tuple-element.51.refs_5_), channel_id=1, source_target_pairs={{0,4},{2,6},{5,1},{7,3},{8,12},{10,14},{13,9},{15,11},{16,20},{18,... | collective-permute-start | bytes 1179656 | tf_op jit(solution)/shard_map/ppermute | solution.py:32
  26.1 6.8 %collective-permute-done.2.refs_3_ = bf16[256,384]{1,0:T(8,128)(2,1)S(1)} collective-permute-done((bf16[256,384]{1,0:T(8,128)(2,1)S(1)}, bf16[256,384]{1,0:T(8,128)(2,1)S(1)}, u32[]{:S(2)}, u32[]{:S(2)}) %collective-permute-start.2) | collective-permute-done | bytes 196640 | tf_op jit(solution)/shard_map/ppermute | solution.py:32
  32.9 3.4 %collective-permute-done.3.refs_4_ = bf16[256,384]{1,0:T(8,128)(2,1)S(1)} collective-permute-done((bf16[256,384]{1,0:T(8,128)(2,1)S(1)}, bf16[256,384]{1,0:T(8,128)(2,1)S(1)}, u32[]{:S(2)}, u32[]{:S(2)}) %collective-permute-start.3) | collective-permute-done | bytes 196640 | tf_op jit(solution)/shard_map/ppermute | solution.py:32
  36.2 0.0 collective-permute-done.8.refs_11_
  36.2 1.3 %collective-permute-start.9 = (bf16[512,384]{1,0:T(8,128)(2,1)S(1)}, bf16[512,384]{1,0:T(8,128)(2,1)S(1)}, u32[]{:S(2)}, u32[]{:S(2)}) collective-permute-start(bf16[512,384]{1,0:T(8,128)(2,1)S(1)} %collective-permute-done.8.refs_11_), channel_id=1, source_target_pairs={{0,4},{2,6},{5,1},{7,3},{8,12},{10,14},{13,9},{15,11},{16,20},{18,... | collective-permute-start | bytes 1179656 | tf_op jit(solution)/shard_map/ppermute | solution.py:32
  37.5 0.0 collective-permute-done.6.refs_8_.refs_9_
  37.5 0.1 collective-permute-start.7
  37.6 0.0 collective-permute-done.5.refs_6_
  37.7 1.2 %collective-permute-done.9.refs_12_ = bf16[512,384]{1,0:T(8,128)(2,1)S(1)} collective-permute-done((bf16[512,384]{1,0:T(8,128)(2,1)S(1)}, bf16[512,384]{1,0:T(8,128)(2,1)S(1)}, u32[]{:S(2)}, u32[]{:S(2)}) %collective-permute-start.9) | collective-permute-done | bytes 393248 | tf_op jit(solution)/shard_map/ppermute | solution.py:32
  38.8 0.6 collective-permute-done.7.refs_7_.refs_10_
  39.4 2.2 %picked.1 = (bf16[2048,128]{1,0:T(8,128)(2,1)S(1)}, bf16[2048,128]{1,0:T(8,128)(2,1)S(1)}, bf16[2048,128]{1,0:T(8,128)(2,1)S(1)}, bf16[512,128]{1,0:T(8,128)(2,1...) custom-call(s32[32]{0:T(128)S(1)} %plan.1.idx, ...), custom_call_target="tpu_custom_call" | custom-call | flops 805306368 | bytes 8388608 | tf_op jit(solution)/shard_map/picked/pallas_call | solution.py:154
  41.6 2.4 %collective-permute-start.10 = (bf16[2048,128]{1,0:T(8,128)(2,1)S(1)}, bf16[2048,128]{1,0:T(8,128)(2,1)S(1)}, u32[]{:S(2)}, u32[]{:S(2)}) collective-permute-start(bf16[2048,128]{1,0:T(8,128)(2,1)S(1)} %get-tuple-element.30), channel_id=1, source_target_pairs={{16,0},{17,1},{18,2},{19,3},{20,4},{21,5},{22,6},{23,7},{24,8},{25... | collective-permute-start | bytes 1572872 | tf_op jit(solution)/shard_map/ppermute | solution.py:32
  44.0 0.2 collective-permute-start.11
  44.1 1.9 %collective-permute-start.12 = (bf16[512,128]{1,0:T(8,128)(2,1)S(1)}, bf16[512,128]{1,0:T(8,128)(2,1)S(1)}, u32[]{:S(2)}, u32[]{:S(2)}) collective-permute-start(bf16[512,128]{1,0:T(8,128)(2,1)S(1)} %get-tuple-element.35), channel_id=1, source_target_pairs={{0,2},{1,3},{2,0},{3,1},{4,6},{5,7},{6,4},{7,5},{8,10},{9,11},{10,... | collective-permute-start | bytes 393224 | tf_op jit(solution)/shard_map/ppermute | solution.py:32
  46.0 2.7 %collective-permute-start.13 = (bf16[512,128]{1,0:T(8,128)(2,1)S(1)}, bf16[512,128]{1,0:T(8,128)(2,1)S(1)}, u32[]{:S(2)}, u32[]{:S(2)}) collective-permute-start(bf16[512,128]{1,0:T(8,128)(2,1)S(1)} %get-tuple-element.36), channel_id=1, source_target_pairs={{0,3},{1,2},{2,1},{3,0},{4,7},{5,6},{6,5},{7,4},{8,11},{9,10},{10,... | collective-permute-start | bytes 393224 | tf_op jit(solution)/shard_map/ppermute | solution.py:32
  48.7 3.1 %collective-permute-start.19 = (bf16[2048,128]{1,0:T(8,128)(2,1)S(1)}, bf16[2048,128]{1,0:T(8,128)(2,1)S(1)}, u32[]{:S(2)}, u32[]{:S(2)}) collective-permute-start(bf16[2048,128]{1,0:T(8,128)(2,1)S(1)} %get-tuple-element.44), channel_id=1, source_target_pairs={{16,4},{17,5},{18,6},{19,7},{20,0},{21,1},{22,2},{23,3},{24,12},{2... | collective-permute-start | bytes 1572872 | tf_op jit(solution)/shard_map/ppermute | solution.py:32
  51.9 0.0 collective-permute-done.11
  51.9 4.1 %collective-permute-start.15 = (bf16[2048,128]{1,0:T(8,128)(2,1)S(1)}, bf16[2048,128]{1,0:T(8,128)(2,1)S(1)}, u32[]{:S(2)}, u32[]{:S(2)}) collective-permute-start(bf16[2048,128]{1,0:T(8,128)(2,1)S(1)} %get-tuple-element.38), channel_id=1, source_target_pairs={{16,8},{17,9},{18,10},{19,11},{20,12},{21,13},{22,14},{23,15},{24,... | collective-permute-start | bytes 1572872 | tf_op jit(solution)/shard_map/ppermute | solution.py:32
  56.0 0.0 collective-permute-done.12
  56.0 0.0 collective-permute-done.13
  56.0 2.6 %collective-permute-start.14 = (bf16[2048,128]{1,0:T(8,128)(2,1)S(1)}, bf16[2048,128]{1,0:T(8,128)(2,1)S(1)}, u32[]{:S(2)}, u32[]{:S(2)}) collective-permute-start(bf16[2048,128]{1,0:T(8,128)(2,1)S(1)} %pad_maximum_fusion), channel_id=1, source_target_pairs={{16,12},{17,13},{18,14},{19,15},{20,8},{21,9},{22,10},{23,11},{24,... | collective-permute-start | bytes 1572872 | tf_op jit(solution)/shard_map/ppermute | solution.py:32
  58.6 0.0 collective-permute-done.10.refs_2_
  58.7 10.4 %update.1 = (bf16[2048,2048]{1,0:T(8,128)(2,1)}, f32[2048,128]{1,0:T(8,128)S(1)}, f32[2048,128]{1,0:T(8,128)S(1)}, f32[2048,128]{1,0:T(8,128)S(1)}, f32[2048,128]{1,0:T(8,128)S(1)}) custom-call(s32[32]{0:T(128)S(1)} %plan.1.idx, bf16[2048,2048]{1,0:T(8,128)(2,1)} %bitcast.8, bf16[512,384]{1,0:T(8,128)(2,1)S(1)} %convolution_convert_fusion.refs_0_, ...), custom_call_target="tpu_custom_call" | custom-call | flops 3221225472 | bytes 25165824 | tf_op jit(solution)/shard_map/update/pallas_call | solution.py:204
  69.1 0.0 collective-permute-done.19.refs_3_
  69.2 3.1 %collective-permute-start.22 = (bf16[1024,128]{1,0:T(8,128)(2,1)S(1)}, bf16[1024,128]{1,0:T(8,128)(2,1)S(1)}, u32[]{:S(2)}, u32[]{:S(2)}) collective-permute-start(bf16[1024,128]{1,0:T(8,128)(2,1)S(1)} %pad_maximum_fusion.3), channel_id=1, source_target_pairs={{0,3},{1,2},{2,1},{3,0},{4,7},{5,6},{6,5},{7,4},{8,11},{9,10},{10,... | collective-permute-start | bytes 786440 | tf_op jit(solution)/shard_map/ppermute | solution.py:32
  72.3 0.1 collective-permute-start.21
  72.4 1.0 %collective-permute-start.20 = (bf16[1024,128]{1,0:T(8,128)(2,1)S(1)}, bf16[1024,128]{1,0:T(8,128)(2,1)S(1)}, u32[]{:S(2)}, u32[]{:S(2)}) collective-permute-start(bf16[1024,128]{1,0:T(8,128)(2,1)S(1)} %get-tuple-element.45), channel_id=1, source_target_pairs={{0,1},{1,0},{2,3},{3,2},{4,5},{5,4},{6,7},{7,6},{8,9},{9,8},{10,11... | collective-permute-start | bytes 786440 | tf_op jit(solution)/shard_map/ppermute | solution.py:32
  73.5 7.6 %collective-permute-done.15.refs_1_ = bf16[2048,128]{1,0:T(8,128)(2,1)S(1)} collective-permute-done((bf16[2048,128]{1,0:T(8,128)(2,1)S(1)}, bf16[2048,128]{1,0:T(8,128)(2,1)S(1)}, u32[]{:S(2)}, u32[]{:S(2)}) %collective-permute-start.15) | collective-permute-done | bytes 524320 | tf_op jit(solution)/shard_map/ppermute | solution.py:32
  81.1 0.6 collective-permute-start.18
  81.7 3.4 %collective-permute-done.22.refs_6_ = bf16[1024,128]{1,0:T(8,128)(2,1)S(1)} collective-permute-done((bf16[1024,128]{1,0:T(8,128)(2,1)S(1)}, bf16[1024,128]{1,0:T(8,128)(2,1)S(1)}, u32[]{:S(2)}, u32[]{:S(2)}) %collective-permute-start.22) | collective-permute-done | bytes 262176 | tf_op jit(solution)/shard_map/ppermute | solution.py:32
  85.2 0.0 collective-permute-start.17
  85.2 0.0 collective-permute-done.21.refs_5_
  85.2 4.0 %collective-permute-start.16 = (bf16[512,128]{1,0:T(8,128)(2,1)S(1)}, bf16[512,128]{1,0:T(8,128)(2,1)S(1)}, u32[]{:S(2)}, u32[]{:S(2)}) collective-permute-start(bf16[512,128]{1,0:T(8,128)(2,1)S(1)} %get-tuple-element.40), channel_id=1, source_target_pairs={{0,1},{1,0},{2,3},{3,2},{4,5},{5,4},{6,7},{7,6},{8,9},{9,8},{10,11... | collective-permute-start | bytes 393224 | tf_op jit(solution)/shard_map/ppermute | solution.py:32
  89.2 0.0 collective-permute-done.20.refs_4_
  89.2 1.5 %place.3.refs_5_ = bf16[2048,2048]{1,0:T(8,128)(2,1)} custom-call(s32[32]{0:T(128)S(1)} %plan.1.idx, f32[2048,128]{1,0:T(8,128)S(1)} %get-tuple-element.39.refs_0_, f32[2048,128]{1,0:T(8,128)S(1)} %get-tuple-element.43.refs_1_, bf16[2048,128]{1,0:T(8,128)(2,1)S(1)} %collective-permute-done.10.refs_2_, ...), custom_call_target="tpu_custom_call", output_to_operand_aliasing={{}: (8, {})} | custom-call | flops 262144 | bytes 4194304 | tf_op jit(solution)/shard_map/place/pallas_call | solution.py:253
  90.7 0.0 collective-permute-done.18.refs_4_
  90.7 2.3 %collective-permute-done.17.refs_3_ = bf16[512,128]{1,0:T(8,128)(2,1)S(1)} collective-permute-done((bf16[512,128]{1,0:T(8,128)(2,1)S(1)}, bf16[512,128]{1,0:T(8,128)(2,1)S(1)}, u32[]{:S(2)}, u32[]{:S(2)}) %collective-permute-start.17) | collective-permute-done | bytes 131104 | tf_op jit(solution)/shard_map/ppermute | solution.py:32
  93.0 2.5 %collective-permute-done.16.refs_2_ = bf16[512,128]{1,0:T(8,128)(2,1)S(1)} collective-permute-done((bf16[512,128]{1,0:T(8,128)(2,1)S(1)}, bf16[512,128]{1,0:T(8,128)(2,1)S(1)}, u32[]{:S(2)}, u32[]{:S(2)}) %collective-permute-start.16) | collective-permute-done | bytes 131104 | tf_op jit(solution)/shard_map/ppermute | solution.py:32
  95.5 1.3 %place.4.refs_2_ = bf16[2048,2048]{1,0:T(8,128)(2,1)} custom-call(s32[32]{0:T(128)S(1)} %plan.1.idx, f32[2048,128]{1,0:T(8,128)S(1)} %get-tuple-element.37.refs_0_, bf16[2048,128]{1,0:T(8,128)(2,1)S(1)} %collective-permute-done.15.refs_1_, bf16[512,128]{1,0:T(8,128)(2,1)S(1)} %collective-permute-done.16.refs_2_, ...), custom_call_target="tpu_custom_call", output_to_operand_aliasing={{}: (6, {})} | custom-call | flops 262144 | bytes 2097152 | tf_op jit(solution)/shard_map/place/pallas_call | solution.py:253
  96.8 0.0 collective-permute-done.14.refs_1_
  96.8 1.3 %place.5 = bf16[2048,2048]{1,0:T(8,128)(2,1)} custom-call(s32[32]{0:T(128)S(1)} %plan.1.idx, f32[2048,128]{1,0:T(8,128)S(1)} %get-tuple-element.32.refs_0_, bf16[2048,128]{1,0:T(8,128)(2,1)S(1)} %collective-permute-done.14.refs_1_, bf16[2048,2048]{1,0:T(8,128)(2,1)} %place.4.refs_2_), custom_call_target="tpu_custom_call", output_to_operand_aliasing={{}: (3, {})} | custom-call | flops 262144 | bytes 2097152 | tf_op jit(solution)/shard_map/place/pallas_call | solution.py:253
  (8 shorter events, 0.2 us)
Async XLA Ops:
  0.0 1.0 %copy-start = (bf16[1,512,384]{2,1,0:T(8,128)(2,1)S(1)}, bf16[1,512,384]{2,1,0:T(8,128)(2,1)}, u32[]{:S(2)}) copy-start(bf16[1,512,384]{2,1,0:T(8,128)(2,1)} %param.6) | copy-start | bytes 1179652
  2.4 14.6 %collective-permute-start = (bf16[512,384]{1,0:T(8,128)(2,1)S(1)}, bf16[512,384]{1,0:T(8,128)(2,1)S(1)}, u32[]{:S(2)}, u32[]{:S(2)}) collective-permute-start(bf16[512,384]{1,0:T(8,128)(2,1)S(1)} %convolution_convert_fusion.refs_0_), channel_id=1, source_target_pairs={{0,1},{1,0},{2,3},{3,2},{4,5},{5,4},{6,7},{7,6},{8,9},{9,8},{10,11... | collective-permute-start | bytes 1179656 | tf_op jit(solution)/shard_map/ppermute | solution.py:32
  3.9 13.0 %collective-permute-start.1 = (bf16[512,384]{1,0:T(8,128)(2,1)S(1)}, bf16[512,384]{1,0:T(8,128)(2,1)S(1)}, u32[]{:S(2)}, u32[]{:S(2)}) collective-permute-start(bf16[512,384]{1,0:T(8,128)(2,1)S(1)} %convolution_convert_fusion.refs_0_), channel_id=1, source_target_pairs={{0,3},{1,2},{2,1},{3,0},{4,7},{5,6},{6,5},{7,4},{8,11},{9,10},{10,... | collective-permute-start | bytes 1179656 | tf_op jit(solution)/shard_map/ppermute | solution.py:32
  6.0 11.0 %collective-permute-start.4 = (bf16[512,384]{1,0:T(8,128)(2,1)S(1)}, bf16[512,384]{1,0:T(8,128)(2,1)S(1)}, u32[]{:S(2)}, u32[]{:S(2)}) collective-permute-start(bf16[512,384]{1,0:T(8,128)(2,1)S(1)} %convolution_convert_fusion.refs_0_), channel_id=1, source_target_pairs={{0,8},{1,9},{2,10},{3,11},{4,12},{5,13},{6,14},{7,15},{8,0},{9,1},... | collective-permute-start | bytes 1179656 | tf_op jit(solution)/shard_map/ppermute | solution.py:32
  7.7 0.7 copy-start.2
  8.3 0.7 copy-start.3
  12.3 3.4 %copy-start.1 = (bf16[1,2048,2048]{2,1,0:T(8,128)(2,1)S(1)}, bf16[1,2048,2048]{2,1,0:T(8,128)(2,1)}, u32[]{:S(2)}) copy-start(bf16[1,2048,2048]{2,1,0:T(8,128)(2,1)} %param.5) | copy-start | bytes 25165828
  17.1 19.1 %collective-permute-start.8 = (bf16[512,384]{1,0:T(8,128)(2,1)S(1)}, bf16[512,384]{1,0:T(8,128)(2,1)S(1)}, u32[]{:S(2)}, u32[]{:S(2)}) collective-permute-start(bf16[512,384]{1,0:T(8,128)(2,1)S(1)} %get-tuple-element.50), channel_id=1, source_target_pairs={{1,2},{3,0},{4,7},{6,5},{9,10},{11,8},{12,15},{14,13},{17,18},{19,... | collective-permute-start | bytes 1179656 | tf_op jit(solution)/shard_map/ppermute | solution.py:32
  18.4 19.1 %collective-permute-start.6 = (bf16[512,384]{1,0:T(8,128)(2,1)S(1)}, bf16[512,384]{1,0:T(8,128)(2,1)S(1)}, u32[]{:S(2)}, u32[]{:S(2)}) collective-permute-start(bf16[512,384]{1,0:T(8,128)(2,1)S(1)} %get-tuple-element.49), channel_id=1, source_target_pairs={{0,2},{1,4},{2,0},{3,6},{4,1},{5,7},{6,3},{7,5},{8,10},{9,12},{10,... | collective-permute-start | bytes 1179656 | tf_op jit(solution)/shard_map/ppermute | solution.py:32
  19.2 13.7 %collective-permute-start.2 = (bf16[256,384]{1,0:T(8,128)(2,1)S(1)}, bf16[256,384]{1,0:T(8,128)(2,1)S(1)}, u32[]{:S(2)}, u32[]{:S(2)}) collective-permute-start(bf16[256,384]{1,0:T(8,128)(2,1)S(1)} %slice.44), channel_id=1, source_target_pairs={{0,1},{1,0},{2,3},{3,2},{4,5},{5,4},{6,7},{7,6},{8,9},{9,8},{10,11... | collective-permute-start | bytes 589832 | tf_op jit(solution)/shard_map/ppermute | solution.py:32
  20.8 15.5 %collective-permute-start.3 = (bf16[256,384]{1,0:T(8,128)(2,1)S(1)}, bf16[256,384]{1,0:T(8,128)(2,1)S(1)}, u32[]{:S(2)}, u32[]{:S(2)}) collective-permute-start(bf16[256,384]{1,0:T(8,128)(2,1)S(1)} %slice.45), channel_id=1, source_target_pairs={{0,3},{1,2},{2,1},{3,0},{4,7},{5,6},{6,5},{7,4},{8,11},{9,10},{10,... | collective-permute-start | bytes 589832 | tf_op jit(solution)/shard_map/ppermute | solution.py:32
  22.8 14.8 %collective-permute-start.5 = (bf16[512,384]{1,0:T(8,128)(2,1)S(1)}, bf16[512,384]{1,0:T(8,128)(2,1)S(1)}, u32[]{:S(2)}, u32[]{:S(2)}) collective-permute-start(bf16[512,384]{1,0:T(8,128)(2,1)S(1)} %get-tuple-element.51.refs_5_), channel_id=1, source_target_pairs={{0,4},{2,6},{5,1},{7,3},{8,12},{10,14},{13,9},{15,11},{16,20},{18,... | collective-permute-start | bytes 1179656 | tf_op jit(solution)/shard_map/ppermute | solution.py:32
  36.2 2.6 %collective-permute-start.9 = (bf16[512,384]{1,0:T(8,128)(2,1)S(1)}, bf16[512,384]{1,0:T(8,128)(2,1)S(1)}, u32[]{:S(2)}, u32[]{:S(2)}) collective-permute-start(bf16[512,384]{1,0:T(8,128)(2,1)S(1)} %collective-permute-done.8.refs_11_), channel_id=1, source_target_pairs={{0,4},{2,6},{5,1},{7,3},{8,12},{10,14},{13,9},{15,11},{16,20},{18,... | collective-permute-start | bytes 1179656 | tf_op jit(solution)/shard_map/ppermute | solution.py:32
  37.5 1.9 %collective-permute-start.7 = (bf16[512,384]{1,0:T(8,128)(2,1)S(1)}, bf16[512,384]{1,0:T(8,128)(2,1)S(1)}, u32[]{:S(2)}, u32[]{:S(2)}) collective-permute-start(bf16[512,384]{1,0:T(8,128)(2,1)S(1)} %collective-permute-done.6.refs_8_.refs_9_), channel_id=1, source_target_pairs={{0,4},{1,5},{2,6},{3,7},{4,0},{5,1},{6,2},{7,3},{8,12},{9,13},{10,... | collective-permute-start | bytes 1179656 | tf_op jit(solution)/shard_map/ppermute | solution.py:32
  41.6 17.1 %collective-permute-start.10 = (bf16[2048,128]{1,0:T(8,128)(2,1)S(1)}, bf16[2048,128]{1,0:T(8,128)(2,1)S(1)}, u32[]{:S(2)}, u32[]{:S(2)}) collective-permute-start(bf16[2048,128]{1,0:T(8,128)(2,1)S(1)} %get-tuple-element.30), channel_id=1, source_target_pairs={{16,0},{17,1},{18,2},{19,3},{20,4},{21,5},{22,6},{23,7},{24,8},{25... | collective-permute-start | bytes 1572872 | tf_op jit(solution)/shard_map/ppermute | solution.py:32
  44.0 7.9 %collective-permute-start.11 = (bf16[512,128]{1,0:T(8,128)(2,1)S(1)}, bf16[512,128]{1,0:T(8,128)(2,1)S(1)}, u32[]{:S(2)}, u32[]{:S(2)}) collective-permute-start(bf16[512,128]{1,0:T(8,128)(2,1)S(1)} %get-tuple-element.34), channel_id=1, source_target_pairs={{0,1},{1,0},{2,3},{3,2},{4,5},{5,4},{6,7},{7,6},{8,9},{9,8},{10,11... | collective-permute-start | bytes 393224 | tf_op jit(solution)/shard_map/ppermute | solution.py:32
  44.1 11.8 %collective-permute-start.12 = (bf16[512,128]{1,0:T(8,128)(2,1)S(1)}, bf16[512,128]{1,0:T(8,128)(2,1)S(1)}, u32[]{:S(2)}, u32[]{:S(2)}) collective-permute-start(bf16[512,128]{1,0:T(8,128)(2,1)S(1)} %get-tuple-element.35), channel_id=1, source_target_pairs={{0,2},{1,3},{2,0},{3,1},{4,6},{5,7},{6,4},{7,5},{8,10},{9,11},{10,... | collective-permute-start | bytes 393224 | tf_op jit(solution)/shard_map/ppermute | solution.py:32
  46.0 10.0 %collective-permute-start.13 = (bf16[512,128]{1,0:T(8,128)(2,1)S(1)}, bf16[512,128]{1,0:T(8,128)(2,1)S(1)}, u32[]{:S(2)}, u32[]{:S(2)}) collective-permute-start(bf16[512,128]{1,0:T(8,128)(2,1)S(1)} %get-tuple-element.36), channel_id=1, source_target_pairs={{0,3},{1,2},{2,1},{3,0},{4,7},{5,6},{6,5},{7,4},{8,11},{9,10},{10,... | collective-permute-start | bytes 393224 | tf_op jit(solution)/shard_map/ppermute | solution.py:32
  48.7 20.4 %collective-permute-start.19 = (bf16[2048,128]{1,0:T(8,128)(2,1)S(1)}, bf16[2048,128]{1,0:T(8,128)(2,1)S(1)}, u32[]{:S(2)}, u32[]{:S(2)}) collective-permute-start(bf16[2048,128]{1,0:T(8,128)(2,1)S(1)} %get-tuple-element.44), channel_id=1, source_target_pairs={{16,4},{17,5},{18,6},{19,7},{20,0},{21,1},{22,2},{23,3},{24,12},{2... | collective-permute-start | bytes 1572872 | tf_op jit(solution)/shard_map/ppermute | solution.py:32
  51.9 29.2 %collective-permute-start.15 = (bf16[2048,128]{1,0:T(8,128)(2,1)S(1)}, bf16[2048,128]{1,0:T(8,128)(2,1)S(1)}, u32[]{:S(2)}, u32[]{:S(2)}) collective-permute-start(bf16[2048,128]{1,0:T(8,128)(2,1)S(1)} %get-tuple-element.38), channel_id=1, source_target_pairs={{16,8},{17,9},{18,10},{19,11},{20,12},{21,13},{22,14},{23,15},{24,... | collective-permute-start | bytes 1572872 | tf_op jit(solution)/shard_map/ppermute | solution.py:32
  56.0 40.8 %collective-permute-start.14 = (bf16[2048,128]{1,0:T(8,128)(2,1)S(1)}, bf16[2048,128]{1,0:T(8,128)(2,1)S(1)}, u32[]{:S(2)}, u32[]{:S(2)}) collective-permute-start(bf16[2048,128]{1,0:T(8,128)(2,1)S(1)} %pad_maximum_fusion), channel_id=1, source_target_pairs={{16,12},{17,13},{18,14},{19,15},{20,8},{21,9},{22,10},{23,11},{24,... | collective-permute-start | bytes 1572872 | tf_op jit(solution)/shard_map/ppermute | solution.py:32
  69.2 16.0 %collective-permute-start.22 = (bf16[1024,128]{1,0:T(8,128)(2,1)S(1)}, bf16[1024,128]{1,0:T(8,128)(2,1)S(1)}, u32[]{:S(2)}, u32[]{:S(2)}) collective-permute-start(bf16[1024,128]{1,0:T(8,128)(2,1)S(1)} %pad_maximum_fusion.3), channel_id=1, source_target_pairs={{0,3},{1,2},{2,1},{3,0},{4,7},{5,6},{6,5},{7,4},{8,11},{9,10},{10,... | collective-permute-start | bytes 786440 | tf_op jit(solution)/shard_map/ppermute | solution.py:32
  72.3 12.8 %collective-permute-start.21 = (bf16[1024,128]{1,0:T(8,128)(2,1)S(1)}, bf16[1024,128]{1,0:T(8,128)(2,1)S(1)}, u32[]{:S(2)}, u32[]{:S(2)}) collective-permute-start(bf16[1024,128]{1,0:T(8,128)(2,1)S(1)} %get-tuple-element.46), channel_id=1, source_target_pairs={{0,2},{1,3},{2,0},{3,1},{4,6},{5,7},{6,4},{7,5},{8,10},{9,11},{10,... | collective-permute-start | bytes 786440 | tf_op jit(solution)/shard_map/ppermute | solution.py:32
  72.4 16.7 %collective-permute-start.20 = (bf16[1024,128]{1,0:T(8,128)(2,1)S(1)}, bf16[1024,128]{1,0:T(8,128)(2,1)S(1)}, u32[]{:S(2)}, u32[]{:S(2)}) collective-permute-start(bf16[1024,128]{1,0:T(8,128)(2,1)S(1)} %get-tuple-element.45), channel_id=1, source_target_pairs={{0,1},{1,0},{2,3},{3,2},{4,5},{5,4},{6,7},{7,6},{8,9},{9,8},{10,11... | collective-permute-start | bytes 786440 | tf_op jit(solution)/shard_map/ppermute | solution.py:32
  81.1 9.6 %collective-permute-start.18 = (bf16[512,128]{1,0:T(8,128)(2,1)S(1)}, bf16[512,128]{1,0:T(8,128)(2,1)S(1)}, u32[]{:S(2)}, u32[]{:S(2)}) collective-permute-start(bf16[512,128]{1,0:T(8,128)(2,1)S(1)} %get-tuple-element.42), channel_id=1, source_target_pairs={{0,3},{1,2},{2,1},{3,0},{4,7},{5,6},{6,5},{7,4},{8,11},{9,10},{10,... | collective-permute-start | bytes 393224 | tf_op jit(solution)/shard_map/ppermute | solution.py:32
  85.2 7.8 %collective-permute-start.17 = (bf16[512,128]{1,0:T(8,128)(2,1)S(1)}, bf16[512,128]{1,0:T(8,128)(2,1)S(1)}, u32[]{:S(2)}, u32[]{:S(2)}) collective-permute-start(bf16[512,128]{1,0:T(8,128)(2,1)S(1)} %get-tuple-element.41), channel_id=1, source_target_pairs={{0,2},{1,3},{2,0},{3,1},{4,6},{5,7},{6,4},{7,5},{8,10},{9,11},{10,... | collective-permute-start | bytes 393224 | tf_op jit(solution)/shard_map/ppermute | solution.py:32
  85.2 10.3 %collective-permute-start.16 = (bf16[512,128]{1,0:T(8,128)(2,1)S(1)}, bf16[512,128]{1,0:T(8,128)(2,1)S(1)}, u32[]{:S(2)}, u32[]{:S(2)}) collective-permute-start(bf16[512,128]{1,0:T(8,128)(2,1)S(1)} %get-tuple-element.40), channel_id=1, source_target_pairs={{0,1},{1,0},{2,3},{3,2},{4,5},{5,4},{6,7},{7,6},{8,9},{9,8},{10,11... | collective-permute-start | bytes 393224 | tf_op jit(solution)/shard_map/ppermute | solution.py:32

commit v3 on v2

--- a/solution.py
+++ b/solution.py
@@ -219,20 +219,19 @@
     )(idx, frontal, *shards)
 
 
-def place_kernel(first, count, split, idx, *refs):
-    owns, parts = refs[:count], refs[count : count + split]
-    out, block_v, sem = refs[count + split + 1 :]
+def place_kernel(first, split, idx, *refs):
+    count = len(split)
+    owns, parts = refs[:count], list(refs[count : count + sum(split)])
+    out, block_v, sem = refs[-3:]
     for n in range(count):
+        mine, parts = parts[: split[n]], parts[split[n] :]
         for e in range(4):
             for i in range(2):
                 for j in range(2):
                     k = (e * 2 + i) * 2 + j
-                    if split == count:
-                        ref, at = parts[n], k
-                    elif e == 0:
-                        ref, at = parts[n], i * 2 + j
-                    else:
-                        ref, at = parts[count + e - 1], (n * 2 + i) * 2 + j
+                    ref, at = (mine[0], k) if split[n] == 1 else (mine[e], i * 2 + j)
+                    if e > 0 and ref.shape[0] == 8 * BLK:
+                        at += n * 4
                     value = owns[n][k * BLK : (k + 1) * BLK, :]
                     value = value + ref[at * BLK : (at + 1) * BLK, :].astype(jnp.float32)
                     block_v[n * 16 + k] = value.astype(jnp.bfloat16)
@@ -248,19 +247,19 @@
 
 
 def placed(idx, first, own, parts, out):
-    count, split = len(own), len(parts)
-
-    return pl.pallas_call(
-        functools.partial(place_kernel, first, count, split),
+    count = len(own)
+    arrays = [array for piece in parts for array in piece]
+    return pl.pallas_call(
+        functools.partial(place_kernel, first, [len(piece) for piece in parts]),
         out_shape=jax.ShapeDtypeStruct(out.shape, out.dtype),
-        in_specs=[SMEM] + [VMEM] * (count + split) + [ANY],
+        in_specs=[SMEM] + [VMEM] * (count + len(arrays)) + [ANY],
         out_specs=ANY,
         scratch_shapes=[pltpu.VMEM((16 * count, BLK, BLK), jnp.bfloat16), pltpu.SemaphoreType.DMA],
-        input_output_aliases={count + split + 1: 0},
+        input_output_aliases={count + len(arrays) + 1: 0},
         compiler_params=params(12),
         cost_estimate=pl.CostEstimate(flops=1 << 18, bytes_accessed=count << 21, transcendentals=0),
         name="place",
-    )(idx, *own, *parts, out)
+    )(idx, *own, *arrays, out)
 
 
 def after(array, *done):
@@ -290,7 +289,7 @@
     row, col = lax.axis_index("row"), lax.axis_index("col")
     same = row // 2 == col // 2
     alike = (row + col) % 2 == 0
-    across = after(across, packed, *near)
+    across = after(across, idx)
     low, high = jnp.where(same, factor, across), jnp.where(same, across, factor)
     half = factor.shape[0] // 2
     by_col = [factor, *near, flip_col(1, near[1][:half]), flip_col(3, near[0][half:])]
@@ -303,20 +302,22 @@
         return move(array, lambda g, r, c: None if (r + c) % 2 else (g, r ^ 1, c))
 
     other = flip_row(1, after(one, *by_col[3:]))
-    shards = by_col + [low, swap(low), other, one, one, other, third, swap(after(third, *by_col[3:]))]
+    shards = by_col + [low, swap(after(low, packed)), other, one, one, other, third, swap(after(third, *by_col[3:]))]
     sent = picked(idx, shards, packed)
     came = [hop(d, sent[d]) for d in range(3)]
     crossed = [sent[3]] + [flip_col(e, sent[3 + e]) for e in (1, 2, 3)]
     came.append(hop(3, jnp.concatenate(crossed)))
     out, *own = updated(idx, shards, after(front, came[0]))
+    others = []
     for changes in ((0, 1), (2,)):
-        parts = [came[d] for d in changes]
+        others.append([])
         for e in (1, 2, 3):
             blocks = [came[d][e * quarter : (e + 1) * quarter] for d in changes]
             blocks = jnp.concatenate(blocks) if len(blocks) > 1 else blocks[0]
-            parts.append(flip_col(e, after(blocks, own[0])))
-        out = placed(idx, changes[0], [own[d] for d in changes], parts, out)
-    return placed(idx, 3, own[3:], came[3:], out)[None]
+            others[-1].append(flip_col(e, after(blocks, own[0])))
+    parts = [[came[0], *others[0]], [came[1], *others[0]], [came[2], *others[1]], [came[3]]]
+    out = placed(idx, 0, own[:2], parts[:2], out)
+    return placed(idx, 2, own[2:], parts[2:], out)[None]
 
 
 def solution(mesh):

time: 99.7 us -> 96.4 us (0.967)
  waiting for transfers between devices: 27.7 us -> 24.3 us
  starting transfers between devices: 41.4 us -> 42.9 us
  Pallas kernels: 21.3 us -> 20.2 us
    ppermute x23, waiting for transfers between devices: 27.7 us -> 24.3 us  [move(): return lax.ppermute(array, AXES, pairs)]
    ppermute x23, starting transfers between devices: 41.4 us -> 42.9 us  [move(): return lax.ppermute(array, AXES, pairs)]
    pallas_call x3 -> x2, Pallas kernels: 4.16 us -> 2.99 us  [placed(): pl.pallas_call(functools.partial(place_kernel, first, [len(piece) for pie...]
  transfers between devices with their start and end apart: 23 -> 23, of which waited for: 8 -> 9; matrix products, arithmetic and copies ran while one was open for 0% -> 0% of each run, Pallas kernels for 18% -> 17%
where the time goes in v3:
time: 96.4 us; the launch traced here: 95 us
  starting transfers between devices  42.9 us (45%)
  waiting for transfers between devices  24.3 us (25%)
  Pallas kernels  20.2 us (21%)
  local copies, waits for them, and re-layouts  5.87 us (6%)
  matrix products  1.36 us (1%)
    ppermute x23, starting transfers between devices, move(): return lax.ppermute(array, AXES, pairs)  42.9 us
    ppermute x23, waiting for transfers between devices, move(): return lax.ppermute(array, AXES, pairs)  24.3 us
    pallas_call x1, Pallas kernels, updated(): pl.pallas_call(update_kernel, out_shape=[jax.ShapeDtypeStruct((tile, tile...  10.5 us
    unnamed x8, local copies, waits for them, and re-layouts  5.75 us
    pallas_call x1, Pallas kernels, plan(): pl.pallas_call(plan_kernel, out_shape=jax.ShapeDtypeStruct((32,), jnp.int...  3.28 us
    pallas_call x2, Pallas kernels, placed(): pl.pallas_call(functools.partial(place_kernel, first, [len(piece) for pie...  2.99 us
    pallas_call x1, Pallas kernels, picked(): pl.pallas_call(picked_kernel, out_shape=[jax.ShapeDtypeStruct((blocks * B...  2.16 us
  transfers between devices with their start and end apart: 23, of which 9 were waited for; matrix products, arithmetic and copies ran while one was open for 0% of the time, Pallas kernels for 17%

profile of v3, /device:TPU:72, one launch (start us, length us, event | category | flops | bytes accessed | tf_op | source)
XLA Modules:
  0.0 95.0 jit_solution(4146664795582367246)
XLA Ops:
  0.0 0.0 copy-start
  0.0 1.0 %copy-done = bf16[1,512,384]{2,1,0:T(8,128)(2,1)S(1)} copy-done((bf16[1,512,384]{2,1,0:T(8,128)(2,1)S(1)}, bf16[1,512,384]{2,1,0:T(8,128)(2,1)}, u32[]{:S(2)}) %copy-start) | copy-done | bytes 393240
  1.0 1.4 %convolution_convert_fusion.refs_0_ = bf16[512,384]{1,0:T(8,128)(2,1)S(1)} fusion(bf16[1,512,384]{2,1,0:T(8,128)(2,1)S(1)} %copy-done, bf16[1,384,384]{2,1,0:T(8,128)(2,1)} %param.7), kind=kOutput, calls=%fused_computation | convolution fusion | flops 151191552 | bytes 1081344 | tf_op jit(solution)/shard_map/dot_general | solution.py:282
  2.4 1.7 %collective-permute-start.4 = (bf16[512,384]{1,0:T(8,128)(2,1)S(1)}, bf16[512,384]{1,0:T(8,128)(2,1)S(1)}, u32[]{:S(2)}, u32[]{:S(2)}) collective-permute-start(bf16[512,384]{1,0:T(8,128)(2,1)S(1)} %convolution_convert_fusion.refs_0_), channel_id=1, source_target_pairs={{0,8},{1,9},{2,10},{3,11},{4,12},{5,13},{6,14},{7,15},{8,0},{9,1},... | collective-permute-start | bytes 1179656 | tf_op jit(solution)/shard_map/ppermute | solution.py:32
  4.1 2.8 %collective-permute-start.1 = (bf16[512,384]{1,0:T(8,128)(2,1)S(1)}, bf16[512,384]{1,0:T(8,128)(2,1)S(1)}, u32[]{:S(2)}, u32[]{:S(2)}) collective-permute-start(bf16[512,384]{1,0:T(8,128)(2,1)S(1)} %convolution_convert_fusion.refs_0_), channel_id=1, source_target_pairs={{0,3},{1,2},{2,1},{3,0},{4,7},{5,6},{6,5},{7,4},{8,11},{9,10},{10,... | collective-permute-start | bytes 1179656 | tf_op jit(solution)/shard_map/ppermute | solution.py:32
  6.8 0.2 collective-permute-start
  7.1 0.0 copy-start.2
  7.1 0.7 copy-done.2
  7.7 0.0 copy-start.3
  7.7 0.7 copy-done.3
  8.4 3.3 %plan.1.idx = s32[32]{0:T(128)S(1)} custom-call(s32[8,64]{1,0:T(8,128)S(1)} %copy-done.2, s32[8,64]{1,0:T(8,128)S(1)} %copy-done.3), custom_call_target="tpu_custom_call" | custom-call | tf_op jit(solution)/shard_map/plan/pallas_call | solution.py:71
  11.7 1.6 %collective-permute-done.4 = bf16[512,384]{1,0:T(8,128)(2,1)S(1)} collective-permute-done((bf16[512,384]{1,0:T(8,128)(2,1)S(1)}, bf16[512,384]{1,0:T(8,128)(2,1)S(1)}, u32[]{:S(2)}, u32[]{:S(2)}) %collective-permute-start.4) | collective-permute-done | bytes 393248 | tf_op jit(solution)/shard_map/ppermute | solution.py:32
  13.3 0.1 broadcast_select_fusion
  13.4 3.1 %collective-permute-start.6 = (bf16[512,384]{1,0:T(8,128)(2,1)S(1)}, bf16[512,384]{1,0:T(8,128)(2,1)S(1)}, u32[]{:S(2)}, u32[]{:S(2)}) collective-permute-start(bf16[512,384]{1,0:T(8,128)(2,1)S(1)} %get-tuple-element.51), channel_id=1, source_target_pairs={{0,2},{1,4},{2,0},{3,6},{4,1},{5,7},{6,3},{7,5},{8,10},{9,12},{10,... | collective-permute-start | bytes 1179656 | tf_op jit(solution)/shard_map/ppermute | solution.py:32
  16.5 1.3 %collective-permute-start.8 = (bf16[512,384]{1,0:T(8,128)(2,1)S(1)}, bf16[512,384]{1,0:T(8,128)(2,1)S(1)}, u32[]{:S(2)}, u32[]{:S(2)}) collective-permute-start(bf16[512,384]{1,0:T(8,128)(2,1)S(1)} %get-tuple-element.52), channel_id=1, source_target_pairs={{1,2},{3,0},{4,7},{6,5},{9,10},{11,8},{12,15},{14,13},{17,18},{19,... | collective-permute-start | bytes 1179656 | tf_op jit(solution)/shard_map/ppermute | solution.py:32
  17.8 0.0 collective-permute-done.1.refs_2_
  17.9 1.2 %collective-permute-start.2 = (bf16[256,384]{1,0:T(8,128)(2,1)S(1)}, bf16[256,384]{1,0:T(8,128)(2,1)S(1)}, u32[]{:S(2)}, u32[]{:S(2)}) collective-permute-start(bf16[256,384]{1,0:T(8,128)(2,1)S(1)} %slice.44), channel_id=1, source_target_pairs={{0,1},{1,0},{2,3},{3,2},{4,5},{5,4},{6,7},{7,6},{8,9},{9,8},{10,11... | collective-permute-start | bytes 589832 | tf_op jit(solution)/shard_map/ppermute | solution.py:32
  19.0 0.0 collective-permute-done.refs_1_
  19.1 2.9 %collective-permute-start.3 = (bf16[256,384]{1,0:T(8,128)(2,1)S(1)}, bf16[256,384]{1,0:T(8,128)(2,1)S(1)}, u32[]{:S(2)}, u32[]{:S(2)}) collective-permute-start(bf16[256,384]{1,0:T(8,128)(2,1)S(1)} %slice.45), channel_id=1, source_target_pairs={{0,3},{1,2},{2,1},{3,0},{4,7},{5,6},{6,5},{7,4},{8,11},{9,10},{10,... | collective-permute-start | bytes 589832 | tf_op jit(solution)/shard_map/ppermute | solution.py:32
  21.9 0.0 copy-start.1
  22.0 3.4 %copy-done.1 = bf16[1,2048,2048]{2,1,0:T(8,128)(2,1)S(1)} copy-done((bf16[1,2048,2048]{2,1,0:T(8,128)(2,1)S(1)}, bf16[1,2048,2048]{2,1,0:T(8,128)(2,1)}, u32[]{:S(2)}) %copy-start.1) | copy-done | bytes 8388632
  25.3 1.3 %pack.1.refs_13_ = bf16[64,128,128]{2,1,0:T(8,128)(2,1)S(1)} custom-call(s32[32]{0:T(128)S(1)} %plan.1.idx, bf16[2048,2048]{1,0:T(8,128)(2,1)S(1)} %bitcast.9), custom_call_target="tpu_custom_call" | custom-call | bytes 4194304 | tf_op jit(solution)/shard_map/pack/pallas_call | solution.py:114
  26.6 1.3 %collective-permute-start.5 = (bf16[512,384]{1,0:T(8,128)(2,1)S(1)}, bf16[512,384]{1,0:T(8,128)(2,1)S(1)}, u32[]{:S(2)}, u32[]{:S(2)}) collective-permute-start(bf16[512,384]{1,0:T(8,128)(2,1)S(1)} %get-tuple-element.29.refs_5_), channel_id=1, source_target_pairs={{0,4},{2,6},{5,1},{7,3},{8,12},{10,14},{13,9},{15,11},{16,20},{18,... | collective-permute-start | bytes 1179656 | tf_op jit(solution)/shard_map/ppermute | solution.py:32
  27.9 1.8 %collective-permute-done.2.refs_3_ = bf16[256,384]{1,0:T(8,128)(2,1)S(1)} collective-permute-done((bf16[256,384]{1,0:T(8,128)(2,1)S(1)}, bf16[256,384]{1,0:T(8,128)(2,1)S(1)}, u32[]{:S(2)}, u32[]{:S(2)}) %collective-permute-start.2) | collective-permute-done | bytes 196640 | tf_op jit(solution)/shard_map/ppermute | solution.py:32
  29.8 3.1 %collective-permute-done.3.refs_4_ = bf16[256,384]{1,0:T(8,128)(2,1)S(1)} collective-permute-done((bf16[256,384]{1,0:T(8,128)(2,1)S(1)}, bf16[256,384]{1,0:T(8,128)(2,1)S(1)}, u32[]{:S(2)}, u32[]{:S(2)}) %collective-permute-start.3) | collective-permute-done | bytes 196640 | tf_op jit(solution)/shard_map/ppermute | solution.py:32
  32.9 0.0 collective-permute-done.6.refs_8_.refs_9_
  32.9 0.0 collective-permute-start.7
  32.9 0.0 collective-permute-done.8.refs_11_
  32.9 2.4 %collective-permute-start.9 = (bf16[512,384]{1,0:T(8,128)(2,1)S(1)}, bf16[512,384]{1,0:T(8,128)(2,1)S(1)}, u32[]{:S(2)}, u32[]{:S(2)}) collective-permute-start(bf16[512,384]{1,0:T(8,128)(2,1)S(1)} %collective-permute-done.8.refs_11_), channel_id=1, source_target_pairs={{0,4},{2,6},{5,1},{7,3},{8,12},{10,14},{13,9},{15,11},{16,20},{18,... | collective-permute-start | bytes 1179656 | tf_op jit(solution)/shard_map/ppermute | solution.py:32
  35.3 0.0 collective-permute-done.5.refs_6_
  35.3 0.0 collective-permute-done.7.refs_7_.refs_10_
  35.4 1.3 %collective-permute-done.9.refs_12_ = bf16[512,384]{1,0:T(8,128)(2,1)S(1)} collective-permute-done((bf16[512,384]{1,0:T(8,128)(2,1)S(1)}, bf16[512,384]{1,0:T(8,128)(2,1)S(1)}, u32[]{:S(2)}, u32[]{:S(2)}) %collective-permute-start.9) | collective-permute-done | bytes 393248 | tf_op jit(solution)/shard_map/ppermute | solution.py:32
  36.6 2.2 %picked.1 = (bf16[2048,128]{1,0:T(8,128)(2,1)S(1)}, bf16[2048,128]{1,0:T(8,128)(2,1)S(1)}, bf16[2048,128]{1,0:T(8,128)(2,1)S(1)}, bf16[512,128]{1,0:T(8,128)(2,1...) custom-call(s32[32]{0:T(128)S(1)} %plan.1.idx, ...), custom_call_target="tpu_custom_call" | custom-call | flops 805306368 | bytes 8388608 | tf_op jit(solution)/shard_map/picked/pallas_call | solution.py:154
  38.8 2.4 %collective-permute-start.10 = (bf16[2048,128]{1,0:T(8,128)(2,1)S(1)}, bf16[2048,128]{1,0:T(8,128)(2,1)S(1)}, u32[]{:S(2)}, u32[]{:S(2)}) collective-permute-start(bf16[2048,128]{1,0:T(8,128)(2,1)S(1)} %get-tuple-element.32), channel_id=1, source_target_pairs={{16,0},{17,1},{18,2},{19,3},{20,4},{21,5},{22,6},{23,7},{24,8},{25... | collective-permute-start | bytes 1572872 | tf_op jit(solution)/shard_map/ppermute | solution.py:32
  41.2 0.1 collective-permute-start.15
  41.3 1.9 %collective-permute-start.16 = (bf16[512,128]{1,0:T(8,128)(2,1)S(1)}, bf16[512,128]{1,0:T(8,128)(2,1)S(1)}, u32[]{:S(2)}, u32[]{:S(2)}) collective-permute-start(bf16[512,128]{1,0:T(8,128)(2,1)S(1)} %get-tuple-element.43), channel_id=1, source_target_pairs={{0,2},{1,3},{2,0},{3,1},{4,6},{5,7},{6,4},{7,5},{8,10},{9,11},{10,... | collective-permute-start | bytes 393224 | tf_op jit(solution)/shard_map/ppermute | solution.py:32
  43.2 2.8 %collective-permute-start.17 = (bf16[512,128]{1,0:T(8,128)(2,1)S(1)}, bf16[512,128]{1,0:T(8,128)(2,1)S(1)}, u32[]{:S(2)}, u32[]{:S(2)}) collective-permute-start(bf16[512,128]{1,0:T(8,128)(2,1)S(1)} %get-tuple-element.44), channel_id=1, source_target_pairs={{0,3},{1,2},{2,1},{3,0},{4,7},{5,6},{6,5},{7,4},{8,11},{9,10},{10,... | collective-permute-start | bytes 393224 | tf_op jit(solution)/shard_map/ppermute | solution.py:32
  46.0 3.1 %collective-permute-start.19 = (bf16[2048,128]{1,0:T(8,128)(2,1)S(1)}, bf16[2048,128]{1,0:T(8,128)(2,1)S(1)}, u32[]{:S(2)}, u32[]{:S(2)}) collective-permute-start(bf16[2048,128]{1,0:T(8,128)(2,1)S(1)} %get-tuple-element.46), channel_id=1, source_target_pairs={{16,4},{17,5},{18,6},{19,7},{20,0},{21,1},{22,2},{23,3},{24,12},{2... | collective-permute-start | bytes 1572872 | tf_op jit(solution)/shard_map/ppermute | solution.py:32
  49.1 0.0 collective-permute-done.15
  49.1 4.8 %collective-permute-start.11 = (bf16[2048,128]{1,0:T(8,128)(2,1)S(1)}, bf16[2048,128]{1,0:T(8,128)(2,1)S(1)}, u32[]{:S(2)}, u32[]{:S(2)}) collective-permute-start(bf16[2048,128]{1,0:T(8,128)(2,1)S(1)} %get-tuple-element.36), channel_id=1, source_target_pairs={{16,8},{17,9},{18,10},{19,11},{20,12},{21,13},{22,14},{23,15},{24,... | collective-permute-start | bytes 1572872 | tf_op jit(solution)/shard_map/ppermute | solution.py:32
  53.9 0.0 collective-permute-done.16
  53.9 0.0 collective-permute-done.17
  54.0 3.5 %collective-permute-start.18 = (bf16[2048,128]{1,0:T(8,128)(2,1)S(1)}, bf16[2048,128]{1,0:T(8,128)(2,1)S(1)}, u32[]{:S(2)}, u32[]{:S(2)}) collective-permute-start(bf16[2048,128]{1,0:T(8,128)(2,1)S(1)} %pad_maximum_fusion), channel_id=1, source_target_pairs={{16,12},{17,13},{18,14},{19,15},{20,8},{21,9},{22,10},{23,11},{24,... | collective-permute-start | bytes 1572872 | tf_op jit(solution)/shard_map/ppermute | solution.py:32
  57.5 0.0 collective-permute-done.10.refs_2_
  57.5 10.5 %update.1 = (bf16[2048,2048]{1,0:T(8,128)(2,1)}, f32[2048,128]{1,0:T(8,128)S(1)}, f32[2048,128]{1,0:T(8,128)S(1)}, f32[2048,128]{1,0:T(8,128)S(1)}, f32[2048,128]{1,0:T(8,128)S(1)}) custom-call(s32[32]{0:T(128)S(1)} %plan.1.idx, bf16[2048,2048]{1,0:T(8,128)(2,1)} %bitcast.8, bf16[512,384]{1,0:T(8,128)(2,1)S(1)} %convolution_convert_fusion.refs_0_, ...), custom_call_target="tpu_custom_call" | custom-call | flops 3221225472 | bytes 25165824 | tf_op jit(solution)/shard_map/update/pallas_call | solution.py:204
  68.0 0.0 collective-permute-done.19.refs_6_
  68.1 2.2 %collective-permute-start.22 = (bf16[1024,128]{1,0:T(8,128)(2,1)S(1)}, bf16[1024,128]{1,0:T(8,128)(2,1)S(1)}, u32[]{:S(2)}, u32[]{:S(2)}) collective-permute-start(bf16[1024,128]{1,0:T(8,128)(2,1)S(1)} %pad_maximum_fusion.3), channel_id=1, source_target_pairs={{0,3},{1,2},{2,1},{3,0},{4,7},{5,6},{6,5},{7,4},{8,11},{9,10},{10,... | collective-permute-start | bytes 786440 | tf_op jit(solution)/shard_map/ppermute | solution.py:32
  70.3 0.1 collective-permute-start.21
  70.4 1.9 %collective-permute-start.20 = (bf16[1024,128]{1,0:T(8,128)(2,1)S(1)}, bf16[1024,128]{1,0:T(8,128)(2,1)S(1)}, u32[]{:S(2)}, u32[]{:S(2)}) collective-permute-start(bf16[1024,128]{1,0:T(8,128)(2,1)S(1)} %get-tuple-element.47), channel_id=1, source_target_pairs={{0,1},{1,0},{2,3},{3,2},{4,5},{5,4},{6,7},{7,6},{8,9},{9,8},{10,11... | collective-permute-start | bytes 786440 | tf_op jit(solution)/shard_map/ppermute | solution.py:32
  72.4 6.6 %collective-permute-done.11.refs_2_ = bf16[2048,128]{1,0:T(8,128)(2,1)S(1)} collective-permute-done((bf16[2048,128]{1,0:T(8,128)(2,1)S(1)}, bf16[2048,128]{1,0:T(8,128)(2,1)S(1)}, u32[]{:S(2)}, u32[]{:S(2)}) %collective-permute-start.11) | collective-permute-done | bytes 524320 | tf_op jit(solution)/shard_map/ppermute | solution.py:32
  79.0 0.2 collective-permute-start.14
  79.2 4.9 %collective-permute-done.22.refs_5_.refs_9_ = bf16[1024,128]{1,0:T(8,128)(2,1)S(1)} collective-permute-done((bf16[1024,128]{1,0:T(8,128)(2,1)S(1)}, bf16[1024,128]{1,0:T(8,128)(2,1)S(1)}, u32[]{:S(2)}, u32[]{:S(2)}) %collective-permute-start.22) | collective-permute-done | bytes 262176 | tf_op jit(solution)/shard_map/ppermute | solution.py:32
  84.1 0.0 collective-permute-start.13
  84.1 0.0 collective-permute-done.21.refs_4_.refs_8_
  84.1 3.0 %collective-permute-start.12 = (bf16[512,128]{1,0:T(8,128)(2,1)S(1)}, bf16[512,128]{1,0:T(8,128)(2,1)S(1)}, u32[]{:S(2)}, u32[]{:S(2)}) collective-permute-start(bf16[512,128]{1,0:T(8,128)(2,1)S(1)} %get-tuple-element.38), channel_id=1, source_target_pairs={{0,1},{1,0},{2,3},{3,2},{4,5},{5,4},{6,7},{7,6},{8,9},{9,8},{10,11... | collective-permute-start | bytes 393224 | tf_op jit(solution)/shard_map/ppermute | solution.py:32
  87.2 0.0 collective-permute-done.20.refs_3_.refs_7_
  87.2 1.5 %place.2.refs_7_ = bf16[2048,2048]{1,0:T(8,128)(2,1)} custom-call(s32[32]{0:T(128)S(1)} %plan.1.idx, f32[2048,128]{1,0:T(8,128)S(1)} %get-tuple-element.37.refs_0_, f32[2048,128]{1,0:T(8,128)S(1)} %get-tuple-element.45.refs_1_, bf16[2048,128]{1,0:T(8,128)(2,1)S(1)} %collective-permute-done.10.refs_2_, ...), custom_call_target="tpu_custom_call", output_to_operand_aliasing={{}: (11, {})} | custom-call | flops 262144 | bytes 4194304 | tf_op jit(solution)/shard_map/place/pallas_call | solution.py:252
  88.7 0.5 collective-permute-done.18.refs_6_
  89.1 0.0 collective-permute-done.14.refs_5_
  89.1 2.9 %collective-permute-done.13.refs_4_ = bf16[512,128]{1,0:T(8,128)(2,1)S(1)} collective-permute-done((bf16[512,128]{1,0:T(8,128)(2,1)S(1)}, bf16[512,128]{1,0:T(8,128)(2,1)S(1)}, u32[]{:S(2)}, u32[]{:S(2)}) %collective-permute-start.13) | collective-permute-done | bytes 131104 | tf_op jit(solution)/shard_map/ppermute | solution.py:32
  92.1 1.4 %collective-permute-done.12.refs_3_ = bf16[512,128]{1,0:T(8,128)(2,1)S(1)} collective-permute-done((bf16[512,128]{1,0:T(8,128)(2,1)S(1)}, bf16[512,128]{1,0:T(8,128)(2,1)S(1)}, u32[]{:S(2)}, u32[]{:S(2)}) %collective-permute-start.12) | collective-permute-done | bytes 131104 | tf_op jit(solution)/shard_map/ppermute | solution.py:32
  93.5 1.5 %place.3 = bf16[2048,2048]{1,0:T(8,128)(2,1)} custom-call(s32[32]{0:T(128)S(1)} %plan.1.idx, f32[2048,128]{1,0:T(8,128)S(1)} %get-tuple-element.34.refs_0_, f32[2048,128]{1,0:T(8,128)S(1)} %get-tuple-element.35.refs_1_, bf16[2048,128]{1,0:T(8,128)(2,1)S(1)} %collective-permute-done.11.refs_2_, ...), custom_call_target="tpu_custom_call", output_to_operand_aliasing={{}: (8, {})} | custom-call | flops 262144 | bytes 4194304 | tf_op jit(solution)/shard_map/place/pallas_call | solution.py:252
  (8 shorter events, 0.2 us)
Async XLA Ops:
  0.0 1.0 %copy-start = (bf16[1,512,384]{2,1,0:T(8,128)(2,1)S(1)}, bf16[1,512,384]{2,1,0:T(8,128)(2,1)}, u32[]{:S(2)}) copy-start(bf16[1,512,384]{2,1,0:T(8,128)(2,1)} %param.6) | copy-start | bytes 1179652
  2.4 10.9 %collective-permute-start.4 = (bf16[512,384]{1,0:T(8,128)(2,1)S(1)}, bf16[512,384]{1,0:T(8,128)(2,1)S(1)}, u32[]{:S(2)}, u32[]{:S(2)}) collective-permute-start(bf16[512,384]{1,0:T(8,128)(2,1)S(1)} %convolution_convert_fusion.refs_0_), channel_id=1, source_target_pairs={{0,8},{1,9},{2,10},{3,11},{4,12},{5,13},{6,14},{7,15},{8,0},{9,1},... | collective-permute-start | bytes 1179656 | tf_op jit(solution)/shard_map/ppermute | solution.py:32
  4.1 13.8 %collective-permute-start.1 = (bf16[512,384]{1,0:T(8,128)(2,1)S(1)}, bf16[512,384]{1,0:T(8,128)(2,1)S(1)}, u32[]{:S(2)}, u32[]{:S(2)}) collective-permute-start(bf16[512,384]{1,0:T(8,128)(2,1)S(1)} %convolution_convert_fusion.refs_0_), channel_id=1, source_target_pairs={{0,3},{1,2},{2,1},{3,0},{4,7},{5,6},{6,5},{7,4},{8,11},{9,10},{10,... | collective-permute-start | bytes 1179656 | tf_op jit(solution)/shard_map/ppermute | solution.py:32
  6.8 12.2 %collective-permute-start = (bf16[512,384]{1,0:T(8,128)(2,1)S(1)}, bf16[512,384]{1,0:T(8,128)(2,1)S(1)}, u32[]{:S(2)}, u32[]{:S(2)}) collective-permute-start(bf16[512,384]{1,0:T(8,128)(2,1)S(1)} %convolution_convert_fusion.refs_0_), channel_id=1, source_target_pairs={{0,1},{1,0},{2,3},{3,2},{4,5},{5,4},{6,7},{7,6},{8,9},{9,8},{10,11... | collective-permute-start | bytes 1179656 | tf_op jit(solution)/shard_map/ppermute | solution.py:32
  7.1 0.7 copy-start.2
  7.7 0.7 copy-start.3
  13.4 19.5 %collective-permute-start.6 = (bf16[512,384]{1,0:T(8,128)(2,1)S(1)}, bf16[512,384]{1,0:T(8,128)(2,1)S(1)}, u32[]{:S(2)}, u32[]{:S(2)}) collective-permute-start(bf16[512,384]{1,0:T(8,128)(2,1)S(1)} %get-tuple-element.51), channel_id=1, source_target_pairs={{0,2},{1,4},{2,0},{3,6},{4,1},{5,7},{6,3},{7,5},{8,10},{9,12},{10,... | collective-permute-start | bytes 1179656 | tf_op jit(solution)/shard_map/ppermute | solution.py:32
  16.5 16.4 %collective-permute-start.8 = (bf16[512,384]{1,0:T(8,128)(2,1)S(1)}, bf16[512,384]{1,0:T(8,128)(2,1)S(1)}, u32[]{:S(2)}, u32[]{:S(2)}) collective-permute-start(bf16[512,384]{1,0:T(8,128)(2,1)S(1)} %get-tuple-element.52), channel_id=1, source_target_pairs={{1,2},{3,0},{4,7},{6,5},{9,10},{11,8},{12,15},{14,13},{17,18},{19,... | collective-permute-start | bytes 1179656 | tf_op jit(solution)/shard_map/ppermute | solution.py:32
  17.9 11.9 %collective-permute-start.2 = (bf16[256,384]{1,0:T(8,128)(2,1)S(1)}, bf16[256,384]{1,0:T(8,128)(2,1)S(1)}, u32[]{:S(2)}, u32[]{:S(2)}) collective-permute-start(bf16[256,384]{1,0:T(8,128)(2,1)S(1)} %slice.44), channel_id=1, source_target_pairs={{0,1},{1,0},{2,3},{3,2},{4,5},{5,4},{6,7},{7,6},{8,9},{9,8},{10,11... | collective-permute-start | bytes 589832 | tf_op jit(solution)/shard_map/ppermute | solution.py:32
  19.1 13.8 %collective-permute-start.3 = (bf16[256,384]{1,0:T(8,128)(2,1)S(1)}, bf16[256,384]{1,0:T(8,128)(2,1)S(1)}, u32[]{:S(2)}, u32[]{:S(2)}) collective-permute-start(bf16[256,384]{1,0:T(8,128)(2,1)S(1)} %slice.45), channel_id=1, source_target_pairs={{0,3},{1,2},{2,1},{3,0},{4,7},{5,6},{6,5},{7,4},{8,11},{9,10},{10,... | collective-permute-start | bytes 589832 | tf_op jit(solution)/shard_map/ppermute | solution.py:32
  21.9 3.4 %copy-start.1 = (bf16[1,2048,2048]{2,1,0:T(8,128)(2,1)S(1)}, bf16[1,2048,2048]{2,1,0:T(8,128)(2,1)}, u32[]{:S(2)}) copy-start(bf16[1,2048,2048]{2,1,0:T(8,128)(2,1)} %param.5) | copy-start | bytes 25165828
  26.6 8.7 %collective-permute-start.5 = (bf16[512,384]{1,0:T(8,128)(2,1)S(1)}, bf16[512,384]{1,0:T(8,128)(2,1)S(1)}, u32[]{:S(2)}, u32[]{:S(2)}) collective-permute-start(bf16[512,384]{1,0:T(8,128)(2,1)S(1)} %get-tuple-element.29.refs_5_), channel_id=1, source_target_pairs={{0,4},{2,6},{5,1},{7,3},{8,12},{10,14},{13,9},{15,11},{16,20},{18,... | collective-permute-start | bytes 1179656 | tf_op jit(solution)/shard_map/ppermute | solution.py:32
  32.9 2.5 %collective-permute-start.7 = (bf16[512,384]{1,0:T(8,128)(2,1)S(1)}, bf16[512,384]{1,0:T(8,128)(2,1)S(1)}, u32[]{:S(2)}, u32[]{:S(2)}) collective-permute-start(bf16[512,384]{1,0:T(8,128)(2,1)S(1)} %collective-permute-done.6.refs_8_.refs_9_), channel_id=1, source_target_pairs={{0,4},{1,5},{2,6},{3,7},{4,0},{5,1},{6,2},{7,3},{8,12},{9,13},{10,... | collective-permute-start | bytes 1179656 | tf_op jit(solution)/shard_map/ppermute | solution.py:32
  32.9 3.7 %collective-permute-start.9 = (bf16[512,384]{1,0:T(8,128)(2,1)S(1)}, bf16[512,384]{1,0:T(8,128)(2,1)S(1)}, u32[]{:S(2)}, u32[]{:S(2)}) collective-permute-start(bf16[512,384]{1,0:T(8,128)(2,1)S(1)} %collective-permute-done.8.refs_11_), channel_id=1, source_target_pairs={{0,4},{2,6},{5,1},{7,3},{8,12},{10,14},{13,9},{15,11},{16,20},{18,... | collective-permute-start | bytes 1179656 | tf_op jit(solution)/shard_map/ppermute | solution.py:32
  38.8 18.6 %collective-permute-start.10 = (bf16[2048,128]{1,0:T(8,128)(2,1)S(1)}, bf16[2048,128]{1,0:T(8,128)(2,1)S(1)}, u32[]{:S(2)}, u32[]{:S(2)}) collective-permute-start(bf16[2048,128]{1,0:T(8,128)(2,1)S(1)} %get-tuple-element.32), channel_id=1, source_target_pairs={{16,0},{17,1},{18,2},{19,3},{20,4},{21,5},{22,6},{23,7},{24,8},{25... | collective-permute-start | bytes 1572872 | tf_op jit(solution)/shard_map/ppermute | solution.py:32
  41.2 7.9 %collective-permute-start.15 = (bf16[512,128]{1,0:T(8,128)(2,1)S(1)}, bf16[512,128]{1,0:T(8,128)(2,1)S(1)}, u32[]{:S(2)}, u32[]{:S(2)}) collective-permute-start(bf16[512,128]{1,0:T(8,128)(2,1)S(1)} %get-tuple-element.42), channel_id=1, source_target_pairs={{0,1},{1,0},{2,3},{3,2},{4,5},{5,4},{6,7},{7,6},{8,9},{9,8},{10,11... | collective-permute-start | bytes 393224 | tf_op jit(solution)/shard_map/ppermute | solution.py:32
  41.3 12.6 %collective-permute-start.16 = (bf16[512,128]{1,0:T(8,128)(2,1)S(1)}, bf16[512,128]{1,0:T(8,128)(2,1)S(1)}, u32[]{:S(2)}, u32[]{:S(2)}) collective-permute-start(bf16[512,128]{1,0:T(8,128)(2,1)S(1)} %get-tuple-element.43), channel_id=1, source_target_pairs={{0,2},{1,3},{2,0},{3,1},{4,6},{5,7},{6,4},{7,5},{8,10},{9,11},{10,... | collective-permute-start | bytes 393224 | tf_op jit(solution)/shard_map/ppermute | solution.py:32
  43.2 10.7 %collective-permute-start.17 = (bf16[512,128]{1,0:T(8,128)(2,1)S(1)}, bf16[512,128]{1,0:T(8,128)(2,1)S(1)}, u32[]{:S(2)}, u32[]{:S(2)}) collective-permute-start(bf16[512,128]{1,0:T(8,128)(2,1)S(1)} %get-tuple-element.44), channel_id=1, source_target_pairs={{0,3},{1,2},{2,1},{3,0},{4,7},{5,6},{6,5},{7,4},{8,11},{9,10},{10,... | collective-permute-start | bytes 393224 | tf_op jit(solution)/shard_map/ppermute | solution.py:32
  46.0 22.0 %collective-permute-start.19 = (bf16[2048,128]{1,0:T(8,128)(2,1)S(1)}, bf16[2048,128]{1,0:T(8,128)(2,1)S(1)}, u32[]{:S(2)}, u32[]{:S(2)}) collective-permute-start(bf16[2048,128]{1,0:T(8,128)(2,1)S(1)} %get-tuple-element.46), channel_id=1, source_target_pairs={{16,4},{17,5},{18,6},{19,7},{20,0},{21,1},{22,2},{23,3},{24,12},{2... | collective-permute-start | bytes 1572872 | tf_op jit(solution)/shard_map/ppermute | solution.py:32
  49.1 29.9 %collective-permute-start.11 = (bf16[2048,128]{1,0:T(8,128)(2,1)S(1)}, bf16[2048,128]{1,0:T(8,128)(2,1)S(1)}, u32[]{:S(2)}, u32[]{:S(2)}) collective-permute-start(bf16[2048,128]{1,0:T(8,128)(2,1)S(1)} %get-tuple-element.36), channel_id=1, source_target_pairs={{16,8},{17,9},{18,10},{19,11},{20,12},{21,13},{22,14},{23,15},{24,... | collective-permute-start | bytes 1572872 | tf_op jit(solution)/shard_map/ppermute | solution.py:32
  54.0 35.2 %collective-permute-start.18 = (bf16[2048,128]{1,0:T(8,128)(2,1)S(1)}, bf16[2048,128]{1,0:T(8,128)(2,1)S(1)}, u32[]{:S(2)}, u32[]{:S(2)}) collective-permute-start(bf16[2048,128]{1,0:T(8,128)(2,1)S(1)} %pad_maximum_fusion), channel_id=1, source_target_pairs={{16,12},{17,13},{18,14},{19,15},{20,8},{21,9},{22,10},{23,11},{24,... | collective-permute-start | bytes 1572872 | tf_op jit(solution)/shard_map/ppermute | solution.py:32
  68.1 16.1 %collective-permute-start.22 = (bf16[1024,128]{1,0:T(8,128)(2,1)S(1)}, bf16[1024,128]{1,0:T(8,128)(2,1)S(1)}, u32[]{:S(2)}, u32[]{:S(2)}) collective-permute-start(bf16[1024,128]{1,0:T(8,128)(2,1)S(1)} %pad_maximum_fusion.3), channel_id=1, source_target_pairs={{0,3},{1,2},{2,1},{3,0},{4,7},{5,6},{6,5},{7,4},{8,11},{9,10},{10,... | collective-permute-start | bytes 786440 | tf_op jit(solution)/shard_map/ppermute | solution.py:32
  70.3 13.8 %collective-permute-start.21 = (bf16[1024,128]{1,0:T(8,128)(2,1)S(1)}, bf16[1024,128]{1,0:T(8,128)(2,1)S(1)}, u32[]{:S(2)}, u32[]{:S(2)}) collective-permute-start(bf16[1024,128]{1,0:T(8,128)(2,1)S(1)} %get-tuple-element.48), channel_id=1, source_target_pairs={{0,2},{1,3},{2,0},{3,1},{4,6},{5,7},{6,4},{7,5},{8,10},{9,11},{10,... | collective-permute-start | bytes 786440 | tf_op jit(solution)/shard_map/ppermute | solution.py:32
  70.4 16.7 %collective-permute-start.20 = (bf16[1024,128]{1,0:T(8,128)(2,1)S(1)}, bf16[1024,128]{1,0:T(8,128)(2,1)S(1)}, u32[]{:S(2)}, u32[]{:S(2)}) collective-permute-start(bf16[1024,128]{1,0:T(8,128)(2,1)S(1)} %get-tuple-element.47), channel_id=1, source_target_pairs={{0,1},{1,0},{2,3},{3,2},{4,5},{5,4},{6,7},{7,6},{8,9},{9,8},{10,11... | collective-permute-start | bytes 786440 | tf_op jit(solution)/shard_map/ppermute | solution.py:32
  79.0 10.1 %collective-permute-start.14 = (bf16[512,128]{1,0:T(8,128)(2,1)S(1)}, bf16[512,128]{1,0:T(8,128)(2,1)S(1)}, u32[]{:S(2)}, u32[]{:S(2)}) collective-permute-start(bf16[512,128]{1,0:T(8,128)(2,1)S(1)} %get-tuple-element.40), channel_id=1, source_target_pairs={{0,3},{1,2},{2,1},{3,0},{4,7},{5,6},{6,5},{7,4},{8,11},{9,10},{10,... | collective-permute-start | bytes 393224 | tf_op jit(solution)/shard_map/ppermute | solution.py:32
  84.1 7.9 %collective-permute-start.13 = (bf16[512,128]{1,0:T(8,128)(2,1)S(1)}, bf16[512,128]{1,0:T(8,128)(2,1)S(1)}, u32[]{:S(2)}, u32[]{:S(2)}) collective-permute-start(bf16[512,128]{1,0:T(8,128)(2,1)S(1)} %get-tuple-element.39), channel_id=1, source_target_pairs={{0,2},{1,3},{2,0},{3,1},{4,6},{5,7},{6,4},{7,5},{8,10},{9,11},{10,... | collective-permute-start | bytes 393224 | tf_op jit(solution)/shard_map/ppermute | solution.py:32
  84.1 9.3 %collective-permute-start.12 = (bf16[512,128]{1,0:T(8,128)(2,1)S(1)}, bf16[512,128]{1,0:T(8,128)(2,1)S(1)}, u32[]{:S(2)}, u32[]{:S(2)}) collective-permute-start(bf16[512,128]{1,0:T(8,128)(2,1)S(1)} %get-tuple-element.38), channel_id=1, source_target_pairs={{0,1},{1,0},{2,3},{3,2},{4,5},{5,4},{6,7},{7,6},{8,9},{9,8},{10,11... | collective-permute-start | bytes 393224 | tf_op jit(solution)/shard_map/ppermute | solution.py:32

commit v4 on v3

--- a/solution.py
+++ b/solution.py
@@ -123,17 +123,17 @@
     )(idx, frontal)
 
 
-def picked_kernel(idx, *refs):
+def picked_kernel(changes, idx, *refs):
     shards, packed = refs[:13], refs[13]
-    outs = refs[14:21]
-    rows_v, cols_v, pick_v = refs[21:]
+    outs = refs[14:-3]
+    rows_v, cols_v, pick_v = refs[-3:]
     row, col = lax.axis_index("row"), lax.axis_index("col")
     load_factor(shards, rows_v, cols_v)
     row_at = [pl.multiple_of(idx[2 * (row ^ d) + i] * BLK, BLK) for d in range(4) for i in range(2)]
     col_at = [pl.multiple_of(idx[8 + 2 * (col ^ e) + j] * BLK, BLK) for e in range(4) for j in range(2)]
     for b in range(8):
         pick_v[b * BLK : (b + 1) * BLK, :] = cols_v[pl.ds(col_at[b], BLK), :]
-    for d in range(4):
+    for d in changes:
         left = jnp.concatenate([rows_v[pl.ds(row_at[2 * d + i], BLK), :] for i in range(2)], axis=0)
         product = lax.dot_general(left, pick_v[...], DEPTH, preferred_element_type=jnp.float32)
         for e in range(4):
@@ -143,22 +143,23 @@
                     value = packed[(2 * d + i) * 8 + b].astype(jnp.float32)
                     value = value - product[i * BLK : (i + 1) * BLK, b * BLK : (b + 1) * BLK]
                     if d < 3:
-                        ref, at = outs[d], (e * 2 + i) * 2 + j
+                        ref, at = outs[d - changes[0]], (e * 2 + i) * 2 + j
                     else:
-                        ref, at = outs[3 + e], i * 2 + j
+                        ref, at = outs[3 - changes[0] + e], i * 2 + j
                     ref[at * BLK : (at + 1) * BLK, :] = value.astype(jnp.bfloat16)
 
 
-def picked(idx, shards, packed):
-    size, depth = shards[0].shape
-    return pl.pallas_call(
-        picked_kernel,
-        out_shape=[jax.ShapeDtypeStruct((blocks * BLK, BLK), jnp.bfloat16) for blocks in (16, 16, 16, 4, 4, 4, 4)],
+def picked(changes, idx, shards, packed):
+    shard, depth = shards[0].shape
+    sizes = [size for d in changes for size in ((16,) if d < 3 else (4,) * 4)]
+    return pl.pallas_call(
+        functools.partial(picked_kernel, changes),
+        out_shape=[jax.ShapeDtypeStruct((blocks * BLK, BLK), jnp.bfloat16) for blocks in sizes],
         in_specs=[SMEM] + [VMEM] * 14,
-        out_specs=[VMEM] * 7,
+        out_specs=[VMEM] * len(sizes),
         scratch_shapes=[
-            pltpu.VMEM((4 * size, depth), jnp.bfloat16),
-            pltpu.VMEM((4 * size, depth), jnp.bfloat16),
+            pltpu.VMEM((4 * shard, depth), jnp.bfloat16),
+            pltpu.VMEM((4 * shard, depth), jnp.bfloat16),
             pltpu.VMEM((8 * BLK, depth), jnp.bfloat16),
         ],
         compiler_params=params(24),
@@ -303,7 +304,8 @@
 
     other = flip_row(1, after(one, *by_col[3:]))
     shards = by_col + [low, swap(after(low, packed)), other, one, one, other, third, swap(after(third, *by_col[3:]))]
-    sent = picked(idx, shards, packed)
+    sent = picked((0,), idx, shards, packed)
+    sent += picked((1, 2, 3), idx, shards, after(packed, sent[0]))
     came = [hop(d, sent[d]) for d in range(3)]
     crossed = [sent[3]] + [flip_col(e, sent[3 + e]) for e in (1, 2, 3)]
     came.append(hop(3, jnp.concatenate(crossed)))

time: 96.4 us -> 96.5 us (level); the launches traced: 95 us -> 96.1 us
  Pallas kernels: 20.2 us -> 21.3 us
    pallas_call x1 -> x2, Pallas kernels: 2.16 us -> 3.23 us  [picked(): pl.pallas_call(functools.partial(picked_kernel, changes), out_shape=[jax....]
  transfers between devices with their start and end apart: 23 -> 23, of which waited for: 9 -> 8; matrix products, arithmetic and copies ran while one was open for 0% -> 0% of each run, Pallas kernels for 17% -> 19%
where the time goes in v4:
time: 96.5 us; the launch traced here: 96.1 us
  starting transfers between devices  42.8 us (44%)
  waiting for transfers between devices  24.3 us (25%)
  Pallas kernels  21.3 us (22%)
  local copies, waits for them, and re-layouts  5.87 us (6%)
  matrix products  1.36 us (1%)
    ppermute x23, starting transfers between devices, move(): return lax.ppermute(array, AXES, pairs)  42.8 us
    ppermute x23, waiting for transfers between devices, move(): return lax.ppermute(array, AXES, pairs)  24.3 us
    pallas_call x1, Pallas kernels, updated(): pl.pallas_call(update_kernel, out_shape=[jax.ShapeDtypeStruct((tile, tile...  10.5 us
    unnamed x8, local copies, waits for them, and re-layouts  5.75 us
    pallas_call x1, Pallas kernels, plan(): pl.pallas_call(plan_kernel, out_shape=jax.ShapeDtypeStruct((32,), jnp.int...  3.28 us
    pallas_call x2, Pallas kernels, picked(): pl.pallas_call(functools.partial(picked_kernel, changes), out_shape=[jax....  3.23 us
    pallas_call x2, Pallas kernels, placed(): pl.pallas_call(functools.partial(place_kernel, first, [len(piece) for pie...  2.99 us
  transfers between devices with their start and end apart: 23, of which 8 were waited for; matrix products, arithmetic and copies ran while one was open for 0% of the time, Pallas kernels for 19%

profile of v4, /device:TPU:72, one launch (start us, length us, event | category | flops | bytes accessed | tf_op | source)
XLA Modules:
  0.0 96.1 jit_solution(8946876800349156997)
XLA Ops:
  0.0 0.0 copy-start
  0.0 1.0 %copy-done = bf16[1,512,384]{2,1,0:T(8,128)(2,1)S(1)} copy-done((bf16[1,512,384]{2,1,0:T(8,128)(2,1)S(1)}, bf16[1,512,384]{2,1,0:T(8,128)(2,1)}, u32[]{:S(2)}) %copy-start) | copy-done | bytes 393240
  1.0 1.4 %convolution_convert_fusion.refs_0_ = bf16[512,384]{1,0:T(8,128)(2,1)S(1)} fusion(bf16[1,512,384]{2,1,0:T(8,128)(2,1)S(1)} %copy-done, bf16[1,384,384]{2,1,0:T(8,128)(2,1)} %param.7), kind=kOutput, calls=%fused_computation | convolution fusion | flops 151191552 | bytes 1081344 | tf_op jit(solution)/shard_map/dot_general | solution.py:283
  2.4 1.7 %collective-permute-start.4 = (bf16[512,384]{1,0:T(8,128)(2,1)S(1)}, bf16[512,384]{1,0:T(8,128)(2,1)S(1)}, u32[]{:S(2)}, u32[]{:S(2)}) collective-permute-start(bf16[512,384]{1,0:T(8,128)(2,1)S(1)} %convolution_convert_fusion.refs_0_), channel_id=1, source_target_pairs={{0,8},{1,9},{2,10},{3,11},{4,12},{5,13},{6,14},{7,15},{8,0},{9,1},... | collective-permute-start | bytes 1179656 | tf_op jit(solution)/shard_map/ppermute | solution.py:32
  4.1 2.8 %collective-permute-start.1 = (bf16[512,384]{1,0:T(8,128)(2,1)S(1)}, bf16[512,384]{1,0:T(8,128)(2,1)S(1)}, u32[]{:S(2)}, u32[]{:S(2)}) collective-permute-start(bf16[512,384]{1,0:T(8,128)(2,1)S(1)} %convolution_convert_fusion.refs_0_), channel_id=1, source_target_pairs={{0,3},{1,2},{2,1},{3,0},{4,7},{5,6},{6,5},{7,4},{8,11},{9,10},{10,... | collective-permute-start | bytes 1179656 | tf_op jit(solution)/shard_map/ppermute | solution.py:32
  6.8 0.2 collective-permute-start
  7.1 0.0 copy-start.2
  7.1 0.7 copy-done.2
  7.7 0.0 copy-start.3
  7.7 0.7 copy-done.3
  8.4 3.3 %plan.1.idx = s32[32]{0:T(128)S(1)} custom-call(s32[8,64]{1,0:T(8,128)S(1)} %copy-done.2, s32[8,64]{1,0:T(8,128)S(1)} %copy-done.3), custom_call_target="tpu_custom_call" | custom-call | tf_op jit(solution)/shard_map/plan/pallas_call | solution.py:71
  11.7 1.6 %collective-permute-done.4 = bf16[512,384]{1,0:T(8,128)(2,1)S(1)} collective-permute-done((bf16[512,384]{1,0:T(8,128)(2,1)S(1)}, bf16[512,384]{1,0:T(8,128)(2,1)S(1)}, u32[]{:S(2)}, u32[]{:S(2)}) %collective-permute-start.4) | collective-permute-done | bytes 393248 | tf_op jit(solution)/shard_map/ppermute | solution.py:32
  13.3 0.1 broadcast_select_fusion
  13.4 3.1 %collective-permute-start.6 = (bf16[512,384]{1,0:T(8,128)(2,1)S(1)}, bf16[512,384]{1,0:T(8,128)(2,1)S(1)}, u32[]{:S(2)}, u32[]{:S(2)}) collective-permute-start(bf16[512,384]{1,0:T(8,128)(2,1)S(1)} %get-tuple-element.51), channel_id=1, source_target_pairs={{0,2},{1,4},{2,0},{3,6},{4,1},{5,7},{6,3},{7,5},{8,10},{9,12},{10,... | collective-permute-start | bytes 1179656 | tf_op jit(solution)/shard_map/ppermute | solution.py:32
  16.5 1.3 %collective-permute-start.8 = (bf16[512,384]{1,0:T(8,128)(2,1)S(1)}, bf16[512,384]{1,0:T(8,128)(2,1)S(1)}, u32[]{:S(2)}, u32[]{:S(2)}) collective-permute-start(bf16[512,384]{1,0:T(8,128)(2,1)S(1)} %get-tuple-element.52), channel_id=1, source_target_pairs={{1,2},{3,0},{4,7},{6,5},{9,10},{11,8},{12,15},{14,13},{17,18},{19,... | collective-permute-start | bytes 1179656 | tf_op jit(solution)/shard_map/ppermute | solution.py:32
  17.8 0.0 collective-permute-done.1.refs_2_
  17.9 1.2 %collective-permute-start.2 = (bf16[256,384]{1,0:T(8,128)(2,1)S(1)}, bf16[256,384]{1,0:T(8,128)(2,1)S(1)}, u32[]{:S(2)}, u32[]{:S(2)}) collective-permute-start(bf16[256,384]{1,0:T(8,128)(2,1)S(1)} %slice.44), channel_id=1, source_target_pairs={{0,1},{1,0},{2,3},{3,2},{4,5},{5,4},{6,7},{7,6},{8,9},{9,8},{10,11... | collective-permute-start | bytes 589832 | tf_op jit(solution)/shard_map/ppermute | solution.py:32
  19.0 0.0 collective-permute-done.refs_1_
  19.1 2.9 %collective-permute-start.3 = (bf16[256,384]{1,0:T(8,128)(2,1)S(1)}, bf16[256,384]{1,0:T(8,128)(2,1)S(1)}, u32[]{:S(2)}, u32[]{:S(2)}) collective-permute-start(bf16[256,384]{1,0:T(8,128)(2,1)S(1)} %slice.45), channel_id=1, source_target_pairs={{0,3},{1,2},{2,1},{3,0},{4,7},{5,6},{6,5},{7,4},{8,11},{9,10},{10,... | collective-permute-start | bytes 589832 | tf_op jit(solution)/shard_map/ppermute | solution.py:32
  21.9 0.0 copy-start.1
  22.0 3.4 %copy-done.1 = bf16[1,2048,2048]{2,1,0:T(8,128)(2,1)S(1)} copy-done((bf16[1,2048,2048]{2,1,0:T(8,128)(2,1)S(1)}, bf16[1,2048,2048]{2,1,0:T(8,128)(2,1)}, u32[]{:S(2)}) %copy-start.1) | copy-done | bytes 8388632
  25.3 1.3 %pack.1.refs_13_ = bf16[64,128,128]{2,1,0:T(8,128)(2,1)S(1)} custom-call(s32[32]{0:T(128)S(1)} %plan.1.idx, bf16[2048,2048]{1,0:T(8,128)(2,1)S(1)} %bitcast.9), custom_call_target="tpu_custom_call" | custom-call | bytes 4194304 | tf_op jit(solution)/shard_map/pack/pallas_call | solution.py:114
  26.6 1.3 %collective-permute-start.5 = (bf16[512,384]{1,0:T(8,128)(2,1)S(1)}, bf16[512,384]{1,0:T(8,128)(2,1)S(1)}, u32[]{:S(2)}, u32[]{:S(2)}) collective-permute-start(bf16[512,384]{1,0:T(8,128)(2,1)S(1)} %get-tuple-element.29.refs_5_), channel_id=1, source_target_pairs={{0,4},{2,6},{5,1},{7,3},{8,12},{10,14},{13,9},{15,11},{16,20},{18,... | collective-permute-start | bytes 1179656 | tf_op jit(solution)/shard_map/ppermute | solution.py:32
  27.9 1.8 %collective-permute-done.2.refs_3_ = bf16[256,384]{1,0:T(8,128)(2,1)S(1)} collective-permute-done((bf16[256,384]{1,0:T(8,128)(2,1)S(1)}, bf16[256,384]{1,0:T(8,128)(2,1)S(1)}, u32[]{:S(2)}, u32[]{:S(2)}) %collective-permute-start.2) | collective-permute-done | bytes 196640 | tf_op jit(solution)/shard_map/ppermute | solution.py:32
  29.8 3.1 %collective-permute-done.3.refs_4_ = bf16[256,384]{1,0:T(8,128)(2,1)S(1)} collective-permute-done((bf16[256,384]{1,0:T(8,128)(2,1)S(1)}, bf16[256,384]{1,0:T(8,128)(2,1)S(1)}, u32[]{:S(2)}, u32[]{:S(2)}) %collective-permute-start.3) | collective-permute-done | bytes 196640 | tf_op jit(solution)/shard_map/ppermute | solution.py:32
  32.9 0.0 collective-permute-done.6.refs_8_.refs_9_
  32.9 0.0 collective-permute-start.7
  32.9 0.0 collective-permute-done.8.refs_11_
  32.9 2.4 %collective-permute-start.9 = (bf16[512,384]{1,0:T(8,128)(2,1)S(1)}, bf16[512,384]{1,0:T(8,128)(2,1)S(1)}, u32[]{:S(2)}, u32[]{:S(2)}) collective-permute-start(bf16[512,384]{1,0:T(8,128)(2,1)S(1)} %collective-permute-done.8.refs_11_), channel_id=1, source_target_pairs={{0,4},{2,6},{5,1},{7,3},{8,12},{10,14},{13,9},{15,11},{16,20},{18,... | collective-permute-start | bytes 1179656 | tf_op jit(solution)/shard_map/ppermute | solution.py:32
  35.3 0.0 collective-permute-done.5.refs_6_
  35.3 0.0 collective-permute-done.7.refs_7_.refs_10_
  35.4 1.3 %collective-permute-done.9.refs_12_ = bf16[512,384]{1,0:T(8,128)(2,1)S(1)} collective-permute-done((bf16[512,384]{1,0:T(8,128)(2,1)S(1)}, bf16[512,384]{1,0:T(8,128)(2,1)S(1)}, u32[]{:S(2)}, u32[]{:S(2)}) %collective-permute-start.9) | collective-permute-done | bytes 393248 | tf_op jit(solution)/shard_map/ppermute | solution.py:32
  36.6 1.3 %picked.2 = bf16[2048,128]{1,0:T(8,128)(2,1)S(1)} custom-call(s32[32]{0:T(128)S(1)} %plan.1.idx, bf16[512,384]{1,0:T(8,128)(2,1)S(1)} %convolution_convert_fusion.refs_0_, bf16[512,384]{1,0:T(8,128)(2,1)S(1)} %collective-permute-done.refs_1_, bf16[512,384]{1,0:T(8,128)(2,1)S(1)} %collective-permute-done.1.refs_2_, ...), custom_call_target="tpu_custom_call" | custom-call | flops 805306368 | bytes 8388608 | tf_op jit(solution)/shard_map/picked/pallas_call | solution.py:155
  38.0 2.4 %collective-permute-start.10 = (bf16[2048,128]{1,0:T(8,128)(2,1)S(1)}, bf16[2048,128]{1,0:T(8,128)(2,1)S(1)}, u32[]{:S(2)}, u32[]{:S(2)}) collective-permute-start(bf16[2048,128]{1,0:T(8,128)(2,1)S(1)} %picked.2), channel_id=1, source_target_pairs={{16,0},{17,1},{18,2},{19,3},{20,4},{21,5},{22,6},{23,7},{24,8},{25... | collective-permute-start | bytes 1572872 | tf_op jit(solution)/shard_map/ppermute | solution.py:32
  40.4 1.9 %picked.3 = (bf16[2048,128]{1,0:T(8,128)(2,1)S(1)}, bf16[2048,128]{1,0:T(8,128)(2,1)S(1)}, bf16[512,128]{1,0:T(8,128)(2,1)S(1)}, bf16[512,128]{1,0:T(8,128)(2,1)...) custom-call(s32[32]{0:T(128)S(1)} %plan.1.idx, bf16[512,384]{1,0:T(8,128)(2,1)S(1)} %convolution_convert_fusion.refs_0_, ...), custom_call_target="tpu_custom_call" | custom-call | flops 805306368 | bytes 8388608 | tf_op jit(solution)/shard_map/picked/pallas_call | solution.py:155
  42.3 0.1 collective-permute-start.15
  42.4 1.9 %collective-permute-start.16 = (bf16[512,128]{1,0:T(8,128)(2,1)S(1)}, bf16[512,128]{1,0:T(8,128)(2,1)S(1)}, u32[]{:S(2)}, u32[]{:S(2)}) collective-permute-start(bf16[512,128]{1,0:T(8,128)(2,1)S(1)} %get-tuple-element.43), channel_id=1, source_target_pairs={{0,2},{1,3},{2,0},{3,1},{4,6},{5,7},{6,4},{7,5},{8,10},{9,11},{10,... | collective-permute-start | bytes 393224 | tf_op jit(solution)/shard_map/ppermute | solution.py:32
  44.3 2.8 %collective-permute-start.17 = (bf16[512,128]{1,0:T(8,128)(2,1)S(1)}, bf16[512,128]{1,0:T(8,128)(2,1)S(1)}, u32[]{:S(2)}, u32[]{:S(2)}) collective-permute-start(bf16[512,128]{1,0:T(8,128)(2,1)S(1)} %get-tuple-element.44), channel_id=1, source_target_pairs={{0,3},{1,2},{2,1},{3,0},{4,7},{5,6},{6,5},{7,4},{8,11},{9,10},{10,... | collective-permute-start | bytes 393224 | tf_op jit(solution)/shard_map/ppermute | solution.py:32
  47.0 3.1 %collective-permute-start.19 = (bf16[2048,128]{1,0:T(8,128)(2,1)S(1)}, bf16[2048,128]{1,0:T(8,128)(2,1)S(1)}, u32[]{:S(2)}, u32[]{:S(2)}) collective-permute-start(bf16[2048,128]{1,0:T(8,128)(2,1)S(1)} %get-tuple-element.46), channel_id=1, source_target_pairs={{16,4},{17,5},{18,6},{19,7},{20,0},{21,1},{22,2},{23,3},{24,12},{2... | collective-permute-start | bytes 1572872 | tf_op jit(solution)/shard_map/ppermute | solution.py:32
  50.2 0.0 collective-permute-done.15
  50.2 4.8 %collective-permute-start.11 = (bf16[2048,128]{1,0:T(8,128)(2,1)S(1)}, bf16[2048,128]{1,0:T(8,128)(2,1)S(1)}, u32[]{:S(2)}, u32[]{:S(2)}) collective-permute-start(bf16[2048,128]{1,0:T(8,128)(2,1)S(1)} %get-tuple-element.36), channel_id=1, source_target_pairs={{16,8},{17,9},{18,10},{19,11},{20,12},{21,13},{22,14},{23,15},{24,... | collective-permute-start | bytes 1572872 | tf_op jit(solution)/shard_map/ppermute | solution.py:32
  55.0 0.0 collective-permute-done.16
  55.0 0.0 collective-permute-done.17
  55.0 3.5 %collective-permute-start.18 = (bf16[2048,128]{1,0:T(8,128)(2,1)S(1)}, bf16[2048,128]{1,0:T(8,128)(2,1)S(1)}, u32[]{:S(2)}, u32[]{:S(2)}) collective-permute-start(bf16[2048,128]{1,0:T(8,128)(2,1)S(1)} %pad_maximum_fusion), channel_id=1, source_target_pairs={{16,12},{17,13},{18,14},{19,15},{20,8},{21,9},{22,10},{23,11},{24,... | collective-permute-start | bytes 1572872 | tf_op jit(solution)/shard_map/ppermute | solution.py:32
  58.5 0.0 collective-permute-done.10.refs_2_
  58.5 10.5 %update.1 = (bf16[2048,2048]{1,0:T(8,128)(2,1)}, f32[2048,128]{1,0:T(8,128)S(1)}, f32[2048,128]{1,0:T(8,128)S(1)}, f32[2048,128]{1,0:T(8,128)S(1)}, f32[2048,128]{1,0:T(8,128)S(1)}) custom-call(s32[32]{0:T(128)S(1)} %plan.1.idx, bf16[2048,2048]{1,0:T(8,128)(2,1)} %bitcast.8, bf16[512,384]{1,0:T(8,128)(2,1)S(1)} %convolution_convert_fusion.refs_0_, ...), custom_call_target="tpu_custom_call" | custom-call | flops 3221225472 | bytes 25165824 | tf_op jit(solution)/shard_map/update/pallas_call | solution.py:205
  69.1 0.0 collective-permute-done.19.refs_6_
  69.1 2.2 %collective-permute-start.22 = (bf16[1024,128]{1,0:T(8,128)(2,1)S(1)}, bf16[1024,128]{1,0:T(8,128)(2,1)S(1)}, u32[]{:S(2)}, u32[]{:S(2)}) collective-permute-start(bf16[1024,128]{1,0:T(8,128)(2,1)S(1)} %pad_maximum_fusion.3), channel_id=1, source_target_pairs={{0,3},{1,2},{2,1},{3,0},{4,7},{5,6},{6,5},{7,4},{8,11},{9,10},{10,... | collective-permute-start | bytes 786440 | tf_op jit(solution)/shard_map/ppermute | solution.py:32
  71.4 0.1 collective-permute-start.21
  71.5 1.9 %collective-permute-start.20 = (bf16[1024,128]{1,0:T(8,128)(2,1)S(1)}, bf16[1024,128]{1,0:T(8,128)(2,1)S(1)}, u32[]{:S(2)}, u32[]{:S(2)}) collective-permute-start(bf16[1024,128]{1,0:T(8,128)(2,1)S(1)} %get-tuple-element.47), channel_id=1, source_target_pairs={{0,1},{1,0},{2,3},{3,2},{4,5},{5,4},{6,7},{7,6},{8,9},{9,8},{10,11... | collective-permute-start | bytes 786440 | tf_op jit(solution)/shard_map/ppermute | solution.py:32
  73.4 4.7 %collective-permute-done.11.refs_2_ = bf16[2048,128]{1,0:T(8,128)(2,1)S(1)} collective-permute-done((bf16[2048,128]{1,0:T(8,128)(2,1)S(1)}, bf16[2048,128]{1,0:T(8,128)(2,1)S(1)}, u32[]{:S(2)}, u32[]{:S(2)}) %collective-permute-start.11) | collective-permute-done | bytes 524320 | tf_op jit(solution)/shard_map/ppermute | solution.py:32
  78.2 0.2 collective-permute-start.14
  78.4 6.8 %collective-permute-done.22.refs_5_.refs_9_ = bf16[1024,128]{1,0:T(8,128)(2,1)S(1)} collective-permute-done((bf16[1024,128]{1,0:T(8,128)(2,1)S(1)}, bf16[1024,128]{1,0:T(8,128)(2,1)S(1)}, u32[]{:S(2)}, u32[]{:S(2)}) %collective-permute-start.22) | collective-permute-done | bytes 262176 | tf_op jit(solution)/shard_map/ppermute | solution.py:32
  85.2 0.0 collective-permute-start.13
  85.2 0.0 collective-permute-done.21.refs_4_.refs_8_
  85.2 3.0 %collective-permute-start.12 = (bf16[512,128]{1,0:T(8,128)(2,1)S(1)}, bf16[512,128]{1,0:T(8,128)(2,1)S(1)}, u32[]{:S(2)}, u32[]{:S(2)}) collective-permute-start(bf16[512,128]{1,0:T(8,128)(2,1)S(1)} %get-tuple-element.38), channel_id=1, source_target_pairs={{0,1},{1,0},{2,3},{3,2},{4,5},{5,4},{6,7},{7,6},{8,9},{9,8},{10,11... | collective-permute-start | bytes 393224 | tf_op jit(solution)/shard_map/ppermute | solution.py:32
  88.2 0.0 collective-permute-done.20.refs_3_.refs_7_
  88.2 1.5 %place.2.refs_7_ = bf16[2048,2048]{1,0:T(8,128)(2,1)} custom-call(s32[32]{0:T(128)S(1)} %plan.1.idx, f32[2048,128]{1,0:T(8,128)S(1)} %get-tuple-element.37.refs_0_, f32[2048,128]{1,0:T(8,128)S(1)} %get-tuple-element.45.refs_1_, bf16[2048,128]{1,0:T(8,128)(2,1)S(1)} %collective-permute-done.10.refs_2_, ...), custom_call_target="tpu_custom_call", output_to_operand_aliasing={{}: (11, {})} | custom-call | flops 262144 | bytes 4194304 | tf_op jit(solution)/shard_map/place/pallas_call | solution.py:253
  89.7 0.0 collective-permute-done.18.refs_6_
  89.7 0.0 collective-permute-done.14.refs_5_
  89.8 3.4 %collective-permute-done.13.refs_4_ = bf16[512,128]{1,0:T(8,128)(2,1)S(1)} collective-permute-done((bf16[512,128]{1,0:T(8,128)(2,1)S(1)}, bf16[512,128]{1,0:T(8,128)(2,1)S(1)}, u32[]{:S(2)}, u32[]{:S(2)}) %collective-permute-start.13) | collective-permute-done | bytes 131104 | tf_op jit(solution)/shard_map/ppermute | solution.py:32
  93.1 1.4 %collective-permute-done.12.refs_3_ = bf16[512,128]{1,0:T(8,128)(2,1)S(1)} collective-permute-done((bf16[512,128]{1,0:T(8,128)(2,1)S(1)}, bf16[512,128]{1,0:T(8,128)(2,1)S(1)}, u32[]{:S(2)}, u32[]{:S(2)}) %collective-permute-start.12) | collective-permute-done | bytes 131104 | tf_op jit(solution)/shard_map/ppermute | solution.py:32
  94.6 1.5 %place.3 = bf16[2048,2048]{1,0:T(8,128)(2,1)} custom-call(s32[32]{0:T(128)S(1)} %plan.1.idx, f32[2048,128]{1,0:T(8,128)S(1)} %get-tuple-element.33.refs_0_, f32[2048,128]{1,0:T(8,128)S(1)} %get-tuple-element.34.refs_1_, bf16[2048,128]{1,0:T(8,128)(2,1)S(1)} %collective-permute-done.11.refs_2_, ...), custom_call_target="tpu_custom_call", output_to_operand_aliasing={{}: (8, {})} | custom-call | flops 262144 | bytes 4194304 | tf_op jit(solution)/shard_map/place/pallas_call | solution.py:253
  (8 shorter events, 0.2 us)
Async XLA Ops:
  0.0 1.0 %copy-start = (bf16[1,512,384]{2,1,0:T(8,128)(2,1)S(1)}, bf16[1,512,384]{2,1,0:T(8,128)(2,1)}, u32[]{:S(2)}) copy-start(bf16[1,512,384]{2,1,0:T(8,128)(2,1)} %param.6) | copy-start | bytes 1179652
  2.4 10.9 %collective-permute-start.4 = (bf16[512,384]{1,0:T(8,128)(2,1)S(1)}, bf16[512,384]{1,0:T(8,128)(2,1)S(1)}, u32[]{:S(2)}, u32[]{:S(2)}) collective-permute-start(bf16[512,384]{1,0:T(8,128)(2,1)S(1)} %convolution_convert_fusion.refs_0_), channel_id=1, source_target_pairs={{0,8},{1,9},{2,10},{3,11},{4,12},{5,13},{6,14},{7,15},{8,0},{9,1},... | collective-permute-start | bytes 1179656 | tf_op jit(solution)/shard_map/ppermute | solution.py:32
  4.1 13.8 %collective-permute-start.1 = (bf16[512,384]{1,0:T(8,128)(2,1)S(1)}, bf16[512,384]{1,0:T(8,128)(2,1)S(1)}, u32[]{:S(2)}, u32[]{:S(2)}) collective-permute-start(bf16[512,384]{1,0:T(8,128)(2,1)S(1)} %convolution_convert_fusion.refs_0_), channel_id=1, source_target_pairs={{0,3},{1,2},{2,1},{3,0},{4,7},{5,6},{6,5},{7,4},{8,11},{9,10},{10,... | collective-permute-start | bytes 1179656 | tf_op jit(solution)/shard_map/ppermute | solution.py:32
  6.8 12.2 %collective-permute-start = (bf16[512,384]{1,0:T(8,128)(2,1)S(1)}, bf16[512,384]{1,0:T(8,128)(2,1)S(1)}, u32[]{:S(2)}, u32[]{:S(2)}) collective-permute-start(bf16[512,384]{1,0:T(8,128)(2,1)S(1)} %convolution_convert_fusion.refs_0_), channel_id=1, source_target_pairs={{0,1},{1,0},{2,3},{3,2},{4,5},{5,4},{6,7},{7,6},{8,9},{9,8},{10,11... | collective-permute-start | bytes 1179656 | tf_op jit(solution)/shard_map/ppermute | solution.py:32
  7.1 0.7 copy-start.2
  7.7 0.7 copy-start.3
  13.4 19.5 %collective-permute-start.6 = (bf16[512,384]{1,0:T(8,128)(2,1)S(1)}, bf16[512,384]{1,0:T(8,128)(2,1)S(1)}, u32[]{:S(2)}, u32[]{:S(2)}) collective-permute-start(bf16[512,384]{1,0:T(8,128)(2,1)S(1)} %get-tuple-element.51), channel_id=1, source_target_pairs={{0,2},{1,4},{2,0},{3,6},{4,1},{5,7},{6,3},{7,5},{8,10},{9,12},{10,... | collective-permute-start | bytes 1179656 | tf_op jit(solution)/shard_map/ppermute | solution.py:32
  16.5 16.4 %collective-permute-start.8 = (bf16[512,384]{1,0:T(8,128)(2,1)S(1)}, bf16[512,384]{1,0:T(8,128)(2,1)S(1)}, u32[]{:S(2)}, u32[]{:S(2)}) collective-permute-start(bf16[512,384]{1,0:T(8,128)(2,1)S(1)} %get-tuple-element.52), channel_id=1, source_target_pairs={{1,2},{3,0},{4,7},{6,5},{9,10},{11,8},{12,15},{14,13},{17,18},{19,... | collective-permute-start | bytes 1179656 | tf_op jit(solution)/shard_map/ppermute | solution.py:32
  17.9 11.9 %collective-permute-start.2 = (bf16[256,384]{1,0:T(8,128)(2,1)S(1)}, bf16[256,384]{1,0:T(8,128)(2,1)S(1)}, u32[]{:S(2)}, u32[]{:S(2)}) collective-permute-start(bf16[256,384]{1,0:T(8,128)(2,1)S(1)} %slice.44), channel_id=1, source_target_pairs={{0,1},{1,0},{2,3},{3,2},{4,5},{5,4},{6,7},{7,6},{8,9},{9,8},{10,11... | collective-permute-start | bytes 589832 | tf_op jit(solution)/shard_map/ppermute | solution.py:32
  19.1 13.8 %collective-permute-start.3 = (bf16[256,384]{1,0:T(8,128)(2,1)S(1)}, bf16[256,384]{1,0:T(8,128)(2,1)S(1)}, u32[]{:S(2)}, u32[]{:S(2)}) collective-permute-start(bf16[256,384]{1,0:T(8,128)(2,1)S(1)} %slice.45), channel_id=1, source_target_pairs={{0,3},{1,2},{2,1},{3,0},{4,7},{5,6},{6,5},{7,4},{8,11},{9,10},{10,... | collective-permute-start | bytes 589832 | tf_op jit(solution)/shard_map/ppermute | solution.py:32
  21.9 3.4 %copy-start.1 = (bf16[1,2048,2048]{2,1,0:T(8,128)(2,1)S(1)}, bf16[1,2048,2048]{2,1,0:T(8,128)(2,1)}, u32[]{:S(2)}) copy-start(bf16[1,2048,2048]{2,1,0:T(8,128)(2,1)} %param.5) | copy-start | bytes 25165828
  26.6 8.7 %collective-permute-start.5 = (bf16[512,384]{1,0:T(8,128)(2,1)S(1)}, bf16[512,384]{1,0:T(8,128)(2,1)S(1)}, u32[]{:S(2)}, u32[]{:S(2)}) collective-permute-start(bf16[512,384]{1,0:T(8,128)(2,1)S(1)} %get-tuple-element.29.refs_5_), channel_id=1, source_target_pairs={{0,4},{2,6},{5,1},{7,3},{8,12},{10,14},{13,9},{15,11},{16,20},{18,... | collective-permute-start | bytes 1179656 | tf_op jit(solution)/shard_map/ppermute | solution.py:32
  32.9 2.5 %collective-permute-start.7 = (bf16[512,384]{1,0:T(8,128)(2,1)S(1)}, bf16[512,384]{1,0:T(8,128)(2,1)S(1)}, u32[]{:S(2)}, u32[]{:S(2)}) collective-permute-start(bf16[512,384]{1,0:T(8,128)(2,1)S(1)} %collective-permute-done.6.refs_8_.refs_9_), channel_id=1, source_target_pairs={{0,4},{1,5},{2,6},{3,7},{4,0},{5,1},{6,2},{7,3},{8,12},{9,13},{10,... | collective-permute-start | bytes 1179656 | tf_op jit(solution)/shard_map/ppermute | solution.py:32
  32.9 3.7 %collective-permute-start.9 = (bf16[512,384]{1,0:T(8,128)(2,1)S(1)}, bf16[512,384]{1,0:T(8,128)(2,1)S(1)}, u32[]{:S(2)}, u32[]{:S(2)}) collective-permute-start(bf16[512,384]{1,0:T(8,128)(2,1)S(1)} %collective-permute-done.8.refs_11_), channel_id=1, source_target_pairs={{0,4},{2,6},{5,1},{7,3},{8,12},{10,14},{13,9},{15,11},{16,20},{18,... | collective-permute-start | bytes 1179656 | tf_op jit(solution)/shard_map/ppermute | solution.py:32
  38.0 20.6 %collective-permute-start.10 = (bf16[2048,128]{1,0:T(8,128)(2,1)S(1)}, bf16[2048,128]{1,0:T(8,128)(2,1)S(1)}, u32[]{:S(2)}, u32[]{:S(2)}) collective-permute-start(bf16[2048,128]{1,0:T(8,128)(2,1)S(1)} %picked.2), channel_id=1, source_target_pairs={{16,0},{17,1},{18,2},{19,3},{20,4},{21,5},{22,6},{23,7},{24,8},{25... | collective-permute-start | bytes 1572872 | tf_op jit(solution)/shard_map/ppermute | solution.py:32
  42.3 7.9 %collective-permute-start.15 = (bf16[512,128]{1,0:T(8,128)(2,1)S(1)}, bf16[512,128]{1,0:T(8,128)(2,1)S(1)}, u32[]{:S(2)}, u32[]{:S(2)}) collective-permute-start(bf16[512,128]{1,0:T(8,128)(2,1)S(1)} %get-tuple-element.42), channel_id=1, source_target_pairs={{0,1},{1,0},{2,3},{3,2},{4,5},{5,4},{6,7},{7,6},{8,9},{9,8},{10,11... | collective-permute-start | bytes 393224 | tf_op jit(solution)/shard_map/ppermute | solution.py:32
  42.4 12.6 %collective-permute-start.16 = (bf16[512,128]{1,0:T(8,128)(2,1)S(1)}, bf16[512,128]{1,0:T(8,128)(2,1)S(1)}, u32[]{:S(2)}, u32[]{:S(2)}) collective-permute-start(bf16[512,128]{1,0:T(8,128)(2,1)S(1)} %get-tuple-element.43), channel_id=1, source_target_pairs={{0,2},{1,3},{2,0},{3,1},{4,6},{5,7},{6,4},{7,5},{8,10},{9,11},{10,... | collective-permute-start | bytes 393224 | tf_op jit(solution)/shard_map/ppermute | solution.py:32
  44.3 10.7 %collective-permute-start.17 = (bf16[512,128]{1,0:T(8,128)(2,1)S(1)}, bf16[512,128]{1,0:T(8,128)(2,1)S(1)}, u32[]{:S(2)}, u32[]{:S(2)}) collective-permute-start(bf16[512,128]{1,0:T(8,128)(2,1)S(1)} %get-tuple-element.44), channel_id=1, source_target_pairs={{0,3},{1,2},{2,1},{3,0},{4,7},{5,6},{6,5},{7,4},{8,11},{9,10},{10,... | collective-permute-start | bytes 393224 | tf_op jit(solution)/shard_map/ppermute | solution.py:32
  47.0 22.0 %collective-permute-start.19 = (bf16[2048,128]{1,0:T(8,128)(2,1)S(1)}, bf16[2048,128]{1,0:T(8,128)(2,1)S(1)}, u32[]{:S(2)}, u32[]{:S(2)}) collective-permute-start(bf16[2048,128]{1,0:T(8,128)(2,1)S(1)} %get-tuple-element.46), channel_id=1, source_target_pairs={{16,4},{17,5},{18,6},{19,7},{20,0},{21,1},{22,2},{23,3},{24,12},{2... | collective-permute-start | bytes 1572872 | tf_op jit(solution)/shard_map/ppermute | solution.py:32
  50.2 28.0 %collective-permute-start.11 = (bf16[2048,128]{1,0:T(8,128)(2,1)S(1)}, bf16[2048,128]{1,0:T(8,128)(2,1)S(1)}, u32[]{:S(2)}, u32[]{:S(2)}) collective-permute-start(bf16[2048,128]{1,0:T(8,128)(2,1)S(1)} %get-tuple-element.36), channel_id=1, source_target_pairs={{16,8},{17,9},{18,10},{19,11},{20,12},{21,13},{22,14},{23,15},{24,... | collective-permute-start | bytes 1572872 | tf_op jit(solution)/shard_map/ppermute | solution.py:32
  55.0 34.7 %collective-permute-start.18 = (bf16[2048,128]{1,0:T(8,128)(2,1)S(1)}, bf16[2048,128]{1,0:T(8,128)(2,1)S(1)}, u32[]{:S(2)}, u32[]{:S(2)}) collective-permute-start(bf16[2048,128]{1,0:T(8,128)(2,1)S(1)} %pad_maximum_fusion), channel_id=1, source_target_pairs={{16,12},{17,13},{18,14},{19,15},{20,8},{21,9},{22,10},{23,11},{24,... | collective-permute-start | bytes 1572872 | tf_op jit(solution)/shard_map/ppermute | solution.py:32
  69.1 16.1 %collective-permute-start.22 = (bf16[1024,128]{1,0:T(8,128)(2,1)S(1)}, bf16[1024,128]{1,0:T(8,128)(2,1)S(1)}, u32[]{:S(2)}, u32[]{:S(2)}) collective-permute-start(bf16[1024,128]{1,0:T(8,128)(2,1)S(1)} %pad_maximum_fusion.3), channel_id=1, source_target_pairs={{0,3},{1,2},{2,1},{3,0},{4,7},{5,6},{6,5},{7,4},{8,11},{9,10},{10,... | collective-permute-start | bytes 786440 | tf_op jit(solution)/shard_map/ppermute | solution.py:32
  71.4 13.8 %collective-permute-start.21 = (bf16[1024,128]{1,0:T(8,128)(2,1)S(1)}, bf16[1024,128]{1,0:T(8,128)(2,1)S(1)}, u32[]{:S(2)}, u32[]{:S(2)}) collective-permute-start(bf16[1024,128]{1,0:T(8,128)(2,1)S(1)} %get-tuple-element.48), channel_id=1, source_target_pairs={{0,2},{1,3},{2,0},{3,1},{4,6},{5,7},{6,4},{7,5},{8,10},{9,11},{10,... | collective-permute-start | bytes 786440 | tf_op jit(solution)/shard_map/ppermute | solution.py:32
  71.5 16.7 %collective-permute-start.20 = (bf16[1024,128]{1,0:T(8,128)(2,1)S(1)}, bf16[1024,128]{1,0:T(8,128)(2,1)S(1)}, u32[]{:S(2)}, u32[]{:S(2)}) collective-permute-start(bf16[1024,128]{1,0:T(8,128)(2,1)S(1)} %get-tuple-element.47), channel_id=1, source_target_pairs={{0,1},{1,0},{2,3},{3,2},{4,5},{5,4},{6,7},{7,6},{8,9},{9,8},{10,11... | collective-permute-start | bytes 786440 | tf_op jit(solution)/shard_map/ppermute | solution.py:32
  78.2 11.6 %collective-permute-start.14 = (bf16[512,128]{1,0:T(8,128)(2,1)S(1)}, bf16[512,128]{1,0:T(8,128)(2,1)S(1)}, u32[]{:S(2)}, u32[]{:S(2)}) collective-permute-start(bf16[512,128]{1,0:T(8,128)(2,1)S(1)} %get-tuple-element.40), channel_id=1, source_target_pairs={{0,3},{1,2},{2,1},{3,0},{4,7},{5,6},{6,5},{7,4},{8,11},{9,10},{10,... | collective-permute-start | bytes 393224 | tf_op jit(solution)/shard_map/ppermute | solution.py:32
  85.2 7.9 %collective-permute-start.13 = (bf16[512,128]{1,0:T(8,128)(2,1)S(1)}, bf16[512,128]{1,0:T(8,128)(2,1)S(1)}, u32[]{:S(2)}, u32[]{:S(2)}) collective-permute-start(bf16[512,128]{1,0:T(8,128)(2,1)S(1)} %get-tuple-element.39), channel_id=1, source_target_pairs={{0,2},{1,3},{2,0},{3,1},{4,6},{5,7},{6,4},{7,5},{8,10},{9,11},{10,... | collective-permute-start | bytes 393224 | tf_op jit(solution)/shard_map/ppermute | solution.py:32
  85.2 9.3 %collective-permute-start.12 = (bf16[512,128]{1,0:T(8,128)(2,1)S(1)}, bf16[512,128]{1,0:T(8,128)(2,1)S(1)}, u32[]{:S(2)}, u32[]{:S(2)}) collective-permute-start(bf16[512,128]{1,0:T(8,128)(2,1)S(1)} %get-tuple-element.38), channel_id=1, source_target_pairs={{0,1},{1,0},{2,3},{3,2},{4,5},{5,4},{6,7},{7,6},{8,9},{9,8},{10,11... | collective-permute-start | bytes 393224 | tf_op jit(solution)/shard_map/ppermute | solution.py:32

commit v5 on v4

--- a/solution.py
+++ b/solution.py
@@ -305,7 +305,9 @@
     other = flip_row(1, after(one, *by_col[3:]))
     shards = by_col + [low, swap(after(low, packed)), other, one, one, other, third, swap(after(third, *by_col[3:]))]
     sent = picked((0,), idx, shards, packed)
-    sent += picked((1, 2, 3), idx, shards, after(packed, sent[0]))
+    last = picked((3,), idx, shards, after(packed, sent[0]))
+    sent += picked((1, 2), idx, shards, after(packed, last[0]))
+    sent += last
     came = [hop(d, sent[d]) for d in range(3)]
     crossed = [sent[3]] + [flip_col(e, sent[3 + e]) for e in (1, 2, 3)]
     came.append(hop(3, jnp.concatenate(crossed)))

time: 96.5 us -> 96.3 us (level)
  starting transfers between devices: 42.8 us -> 41.3 us
    ppermute x23, starting transfers between devices: 42.8 us -> 41.3 us  [move(): return lax.ppermute(array, AXES, pairs)]
    pallas_call x2 -> x3, Pallas kernels: 3.23 us -> 4.27 us  [picked(): pl.pallas_call(functools.partial(picked_kernel, changes), out_shape=[jax....]
  transfers between devices with their start and end apart: 23 -> 23, of which waited for: 8 -> 8; matrix products, arithmetic and copies ran while one was open for 0% -> 0% of each run, Pallas kernels for 19% -> 20%
where the time goes in v5:
time: 96.3 us; the launch traced here: 95.8 us
  starting transfers between devices  41.3 us (43%)
  waiting for transfers between devices  24.4 us (25%)
  Pallas kernels  22.2 us (23%)
  local copies, waits for them, and re-layouts  5.87 us (6%)
  matrix products  1.37 us (1%)
    ppermute x23, starting transfers between devices, move(): return lax.ppermute(array, AXES, pairs)  41.3 us
    ppermute x23, waiting for transfers between devices, move(): return lax.ppermute(array, AXES, pairs)  24.4 us
    pallas_call x1, Pallas kernels, updated(): pl.pallas_call(update_kernel, out_shape=[jax.ShapeDtypeStruct((tile, tile...  10.4 us
    unnamed x8, local copies, waits for them, and re-layouts  5.75 us
    pallas_call x3, Pallas kernels, picked(): pl.pallas_call(functools.partial(picked_kernel, changes), out_shape=[jax....  4.27 us
    pallas_call x1, Pallas kernels, plan(): pl.pallas_call(plan_kernel, out_shape=jax.ShapeDtypeStruct((32,), jnp.int...  3.28 us
    pallas_call x2, Pallas kernels, placed(): pl.pallas_call(functools.partial(place_kernel, first, [len(piece) for pie...  2.99 us
  transfers between devices with their start and end apart: 23, of which 8 were waited for; matrix products, arithmetic and copies ran while one was open for 0% of the time, Pallas kernels for 20%

profile of v5, /device:TPU:72, one launch (start us, length us, event | category | flops | bytes accessed | tf_op | source)
XLA Modules:
  0.0 95.8 jit_solution(10908517830687169430)
XLA Ops:
  0.0 0.0 copy-start
  0.0 1.0 %copy-done = bf16[1,512,384]{2,1,0:T(8,128)(2,1)S(1)} copy-done((bf16[1,512,384]{2,1,0:T(8,128)(2,1)S(1)}, bf16[1,512,384]{2,1,0:T(8,128)(2,1)}, u32[]{:S(2)}) %copy-start) | copy-done | bytes 393240
  1.0 1.4 %convolution_convert_fusion.refs_0_ = bf16[512,384]{1,0:T(8,128)(2,1)S(1)} fusion(bf16[1,512,384]{2,1,0:T(8,128)(2,1)S(1)} %copy-done, bf16[1,384,384]{2,1,0:T(8,128)(2,1)} %param.7), kind=kOutput, calls=%fused_computation | convolution fusion | flops 151191552 | bytes 1081344 | tf_op jit(solution)/shard_map/dot_general | solution.py:283
  2.4 1.7 %collective-permute-start.4 = (bf16[512,384]{1,0:T(8,128)(2,1)S(1)}, bf16[512,384]{1,0:T(8,128)(2,1)S(1)}, u32[]{:S(2)}, u32[]{:S(2)}) collective-permute-start(bf16[512,384]{1,0:T(8,128)(2,1)S(1)} %convolution_convert_fusion.refs_0_), channel_id=1, source_target_pairs={{0,8},{1,9},{2,10},{3,11},{4,12},{5,13},{6,14},{7,15},{8,0},{9,1},... | collective-permute-start | bytes 1179656 | tf_op jit(solution)/shard_map/ppermute | solution.py:32
  4.1 2.8 %collective-permute-start.1 = (bf16[512,384]{1,0:T(8,128)(2,1)S(1)}, bf16[512,384]{1,0:T(8,128)(2,1)S(1)}, u32[]{:S(2)}, u32[]{:S(2)}) collective-permute-start(bf16[512,384]{1,0:T(8,128)(2,1)S(1)} %convolution_convert_fusion.refs_0_), channel_id=1, source_target_pairs={{0,3},{1,2},{2,1},{3,0},{4,7},{5,6},{6,5},{7,4},{8,11},{9,10},{10,... | collective-permute-start | bytes 1179656 | tf_op jit(solution)/shard_map/ppermute | solution.py:32
  6.8 0.2 collective-permute-start
  7.1 0.0 copy-start.2
  7.1 0.7 copy-done.2
  7.7 0.0 copy-start.3
  7.8 0.7 copy-done.3
  8.4 3.3 %plan.1.idx = s32[32]{0:T(128)S(1)} custom-call(s32[8,64]{1,0:T(8,128)S(1)} %copy-done.2, s32[8,64]{1,0:T(8,128)S(1)} %copy-done.3), custom_call_target="tpu_custom_call" | custom-call | tf_op jit(solution)/shard_map/plan/pallas_call | solution.py:71
  11.7 1.6 %collective-permute-done.4 = bf16[512,384]{1,0:T(8,128)(2,1)S(1)} collective-permute-done((bf16[512,384]{1,0:T(8,128)(2,1)S(1)}, bf16[512,384]{1,0:T(8,128)(2,1)S(1)}, u32[]{:S(2)}, u32[]{:S(2)}) %collective-permute-start.4) | collective-permute-done | bytes 393248 | tf_op jit(solution)/shard_map/ppermute | solution.py:32
  13.3 0.1 broadcast_select_fusion
  13.4 3.1 %collective-permute-start.6 = (bf16[512,384]{1,0:T(8,128)(2,1)S(1)}, bf16[512,384]{1,0:T(8,128)(2,1)S(1)}, u32[]{:S(2)}, u32[]{:S(2)}) collective-permute-start(bf16[512,384]{1,0:T(8,128)(2,1)S(1)} %get-tuple-element.53), channel_id=1, source_target_pairs={{0,2},{1,4},{2,0},{3,6},{4,1},{5,7},{6,3},{7,5},{8,10},{9,12},{10,... | collective-permute-start | bytes 1179656 | tf_op jit(solution)/shard_map/ppermute | solution.py:32
  16.5 1.3 %collective-permute-start.8 = (bf16[512,384]{1,0:T(8,128)(2,1)S(1)}, bf16[512,384]{1,0:T(8,128)(2,1)S(1)}, u32[]{:S(2)}, u32[]{:S(2)}) collective-permute-start(bf16[512,384]{1,0:T(8,128)(2,1)S(1)} %get-tuple-element.54), channel_id=1, source_target_pairs={{1,2},{3,0},{4,7},{6,5},{9,10},{11,8},{12,15},{14,13},{17,18},{19,... | collective-permute-start | bytes 1179656 | tf_op jit(solution)/shard_map/ppermute | solution.py:32
  17.8 0.0 collective-permute-done.1.refs_2_
  17.9 1.2 %collective-permute-start.2 = (bf16[256,384]{1,0:T(8,128)(2,1)S(1)}, bf16[256,384]{1,0:T(8,128)(2,1)S(1)}, u32[]{:S(2)}, u32[]{:S(2)}) collective-permute-start(bf16[256,384]{1,0:T(8,128)(2,1)S(1)} %slice.44), channel_id=1, source_target_pairs={{0,1},{1,0},{2,3},{3,2},{4,5},{5,4},{6,7},{7,6},{8,9},{9,8},{10,11... | collective-permute-start | bytes 589832 | tf_op jit(solution)/shard_map/ppermute | solution.py:32
  19.0 0.0 collective-permute-done.refs_1_
  19.1 2.9 %collective-permute-start.3 = (bf16[256,384]{1,0:T(8,128)(2,1)S(1)}, bf16[256,384]{1,0:T(8,128)(2,1)S(1)}, u32[]{:S(2)}, u32[]{:S(2)}) collective-permute-start(bf16[256,384]{1,0:T(8,128)(2,1)S(1)} %slice.45), channel_id=1, source_target_pairs={{0,3},{1,2},{2,1},{3,0},{4,7},{5,6},{6,5},{7,4},{8,11},{9,10},{10,... | collective-permute-start | bytes 589832 | tf_op jit(solution)/shard_map/ppermute | solution.py:32
  21.9 0.0 copy-start.1
  21.9 3.4 %copy-done.1 = bf16[1,2048,2048]{2,1,0:T(8,128)(2,1)S(1)} copy-done((bf16[1,2048,2048]{2,1,0:T(8,128)(2,1)S(1)}, bf16[1,2048,2048]{2,1,0:T(8,128)(2,1)}, u32[]{:S(2)}) %copy-start.1) | copy-done | bytes 8388632
  25.3 1.3 %pack.1.refs_13_ = bf16[64,128,128]{2,1,0:T(8,128)(2,1)S(1)} custom-call(s32[32]{0:T(128)S(1)} %plan.1.idx, bf16[2048,2048]{1,0:T(8,128)(2,1)S(1)} %bitcast.9), custom_call_target="tpu_custom_call" | custom-call | bytes 4194304 | tf_op jit(solution)/shard_map/pack/pallas_call | solution.py:114
  26.6 1.3 %collective-permute-start.5 = (bf16[512,384]{1,0:T(8,128)(2,1)S(1)}, bf16[512,384]{1,0:T(8,128)(2,1)S(1)}, u32[]{:S(2)}, u32[]{:S(2)}) collective-permute-start(bf16[512,384]{1,0:T(8,128)(2,1)S(1)} %get-tuple-element.30.refs_5_), channel_id=1, source_target_pairs={{0,4},{2,6},{5,1},{7,3},{8,12},{10,14},{13,9},{15,11},{16,20},{18,... | collective-permute-start | bytes 1179656 | tf_op jit(solution)/shard_map/ppermute | solution.py:32
  27.9 1.8 %collective-permute-done.2.refs_3_ = bf16[256,384]{1,0:T(8,128)(2,1)S(1)} collective-permute-done((bf16[256,384]{1,0:T(8,128)(2,1)S(1)}, bf16[256,384]{1,0:T(8,128)(2,1)S(1)}, u32[]{:S(2)}, u32[]{:S(2)}) %collective-permute-start.2) | collective-permute-done | bytes 196640 | tf_op jit(solution)/shard_map/ppermute | solution.py:32
  29.8 3.1 %collective-permute-done.3.refs_4_ = bf16[256,384]{1,0:T(8,128)(2,1)S(1)} collective-permute-done((bf16[256,384]{1,0:T(8,128)(2,1)S(1)}, bf16[256,384]{1,0:T(8,128)(2,1)S(1)}, u32[]{:S(2)}, u32[]{:S(2)}) %collective-permute-start.3) | collective-permute-done | bytes 196640 | tf_op jit(solution)/shard_map/ppermute | solution.py:32
  32.9 0.0 collective-permute-done.6.refs_8_.refs_9_
  32.9 0.0 collective-permute-start.7
  32.9 0.0 collective-permute-done.8.refs_11_
  32.9 2.4 %collective-permute-start.9 = (bf16[512,384]{1,0:T(8,128)(2,1)S(1)}, bf16[512,384]{1,0:T(8,128)(2,1)S(1)}, u32[]{:S(2)}, u32[]{:S(2)}) collective-permute-start(bf16[512,384]{1,0:T(8,128)(2,1)S(1)} %collective-permute-done.8.refs_11_), channel_id=1, source_target_pairs={{0,4},{2,6},{5,1},{7,3},{8,12},{10,14},{13,9},{15,11},{16,20},{18,... | collective-permute-start | bytes 1179656 | tf_op jit(solution)/shard_map/ppermute | solution.py:32
  35.3 0.0 collective-permute-done.5.refs_6_
  35.4 0.0 collective-permute-done.7.refs_7_.refs_10_
  35.4 1.3 %collective-permute-done.9.refs_12_ = bf16[512,384]{1,0:T(8,128)(2,1)S(1)} collective-permute-done((bf16[512,384]{1,0:T(8,128)(2,1)S(1)}, bf16[512,384]{1,0:T(8,128)(2,1)S(1)}, u32[]{:S(2)}, u32[]{:S(2)}) %collective-permute-start.9) | collective-permute-done | bytes 393248 | tf_op jit(solution)/shard_map/ppermute | solution.py:32
  36.7 1.3 %picked.3 = bf16[2048,128]{1,0:T(8,128)(2,1)S(1)} custom-call(s32[32]{0:T(128)S(1)} %plan.1.idx, bf16[512,384]{1,0:T(8,128)(2,1)S(1)} %convolution_convert_fusion.refs_0_, bf16[512,384]{1,0:T(8,128)(2,1)S(1)} %collective-permute-done.refs_1_, bf16[512,384]{1,0:T(8,128)(2,1)S(1)} %collective-permute-done.1.refs_2_, ...), custom_call_target="tpu_custom_call" | custom-call | flops 805306368 | bytes 8388608 | tf_op jit(solution)/shard_map/picked/pallas_call | solution.py:155
  38.0 2.4 %collective-permute-start.10 = (bf16[2048,128]{1,0:T(8,128)(2,1)S(1)}, bf16[2048,128]{1,0:T(8,128)(2,1)S(1)}, u32[]{:S(2)}, u32[]{:S(2)}) collective-permute-start(bf16[2048,128]{1,0:T(8,128)(2,1)S(1)} %picked.3), channel_id=1, source_target_pairs={{16,0},{17,1},{18,2},{19,3},{20,4},{21,5},{22,6},{23,7},{24,8},{25... | collective-permute-start | bytes 1572872 | tf_op jit(solution)/shard_map/ppermute | solution.py:32
  40.4 1.3 %picked.4 = (bf16[512,128]{1,0:T(8,128)(2,1)S(1)}, bf16[512,128]{1,0:T(8,128)(2,1)S(1)}, bf16[512,128]{1,0:T(8,128)(2,1)S(1)}, bf16[512,128]{1,0:T(8,128)(2,1)S(1)}) custom-call(s32[32]{0:T(128)S(1)} %plan.1.idx, bf16[512,384]{1,0:T(8,128)(2,1)S(1)} %convolution_convert_fusion.refs_0_, bf16[512,384]{1,0:T(8,128)(2,1)S(1)} %collective-permute-done.refs_1_, ...), custom_call_target="tpu_custom_call" | custom-call | flops 805306368 | bytes 8388608 | tf_op jit(solution)/shard_map/picked/pallas_call | solution.py:155
  41.7 0.1 collective-permute-start.15
  41.8 1.9 %collective-permute-start.16 = (bf16[512,128]{1,0:T(8,128)(2,1)S(1)}, bf16[512,128]{1,0:T(8,128)(2,1)S(1)}, u32[]{:S(2)}, u32[]{:S(2)}) collective-permute-start(bf16[512,128]{1,0:T(8,128)(2,1)S(1)} %get-tuple-element.45), channel_id=1, source_target_pairs={{0,2},{1,3},{2,0},{3,1},{4,6},{5,7},{6,4},{7,5},{8,10},{9,11},{10,... | collective-permute-start | bytes 393224 | tf_op jit(solution)/shard_map/ppermute | solution.py:32
  43.7 2.8 %collective-permute-start.17 = (bf16[512,128]{1,0:T(8,128)(2,1)S(1)}, bf16[512,128]{1,0:T(8,128)(2,1)S(1)}, u32[]{:S(2)}, u32[]{:S(2)}) collective-permute-start(bf16[512,128]{1,0:T(8,128)(2,1)S(1)} %get-tuple-element.46), channel_id=1, source_target_pairs={{0,3},{1,2},{2,1},{3,0},{4,7},{5,6},{6,5},{7,4},{8,11},{9,10},{10,... | collective-permute-start | bytes 393224 | tf_op jit(solution)/shard_map/ppermute | solution.py:32
  46.5 1.6 %picked.5 = (bf16[2048,128]{1,0:T(8,128)(2,1)S(1)}, bf16[2048,128]{1,0:T(8,128)(2,1)S(1)}) custom-call(s32[32]{0:T(128)S(1)} %plan.1.idx, bf16[512,384]{1,0:T(8,128)(2,1)S(1)} %convolution_convert_fusion.refs_0_, bf16[512,384]{1,0:T(8,128)(2,1)S(1)} %collective-permute-done.refs_1_, bf16[512,384]{1,0:T(8,128)(2,1)S(1)} %collective-permute-done.1.refs_2_, ...), custom_call_target="tpu_custom_call" | custom-call | flops 805306368 | bytes 8388608 | tf_op jit(solution)/shard_map/picked/pallas_call | solution.py:155
  48.1 3.1 %collective-permute-start.19 = (bf16[2048,128]{1,0:T(8,128)(2,1)S(1)}, bf16[2048,128]{1,0:T(8,128)(2,1)S(1)}, u32[]{:S(2)}, u32[]{:S(2)}) collective-permute-start(bf16[2048,128]{1,0:T(8,128)(2,1)S(1)} %get-tuple-element.48), channel_id=1, source_target_pairs={{16,4},{17,5},{18,6},{19,7},{20,0},{21,1},{22,2},{23,3},{24,12},{2... | collective-permute-start | bytes 1572872 | tf_op jit(solution)/shard_map/ppermute | solution.py:32
  51.2 0.0 collective-permute-done.15
  51.2 4.8 %collective-permute-start.11 = (bf16[2048,128]{1,0:T(8,128)(2,1)S(1)}, bf16[2048,128]{1,0:T(8,128)(2,1)S(1)}, u32[]{:S(2)}, u32[]{:S(2)}) collective-permute-start(bf16[2048,128]{1,0:T(8,128)(2,1)S(1)} %get-tuple-element.39), channel_id=1, source_target_pairs={{16,8},{17,9},{18,10},{19,11},{20,12},{21,13},{22,14},{23,15},{24,... | collective-permute-start | bytes 1572872 | tf_op jit(solution)/shard_map/ppermute | solution.py:32
  56.0 0.0 collective-permute-done.16
  56.0 0.0 collective-permute-done.17
  56.1 2.6 %collective-permute-start.18 = (bf16[2048,128]{1,0:T(8,128)(2,1)S(1)}, bf16[2048,128]{1,0:T(8,128)(2,1)S(1)}, u32[]{:S(2)}, u32[]{:S(2)}) collective-permute-start(bf16[2048,128]{1,0:T(8,128)(2,1)S(1)} %pad_maximum_fusion), channel_id=1, source_target_pairs={{16,12},{17,13},{18,14},{19,15},{20,8},{21,9},{22,10},{23,11},{24,... | collective-permute-start | bytes 1572872 | tf_op jit(solution)/shard_map/ppermute | solution.py:32
  58.6 0.0 collective-permute-done.10.refs_2_
  58.7 10.4 %update.1 = (bf16[2048,2048]{1,0:T(8,128)(2,1)}, f32[2048,128]{1,0:T(8,128)S(1)}, f32[2048,128]{1,0:T(8,128)S(1)}, f32[2048,128]{1,0:T(8,128)S(1)}, f32[2048,128]{1,0:T(8,128)S(1)}) custom-call(s32[32]{0:T(128)S(1)} %plan.1.idx, bf16[2048,2048]{1,0:T(8,128)(2,1)} %bitcast.8, bf16[512,384]{1,0:T(8,128)(2,1)S(1)} %convolution_convert_fusion.refs_0_, ...), custom_call_target="tpu_custom_call" | custom-call | flops 3221225472 | bytes 25165824 | tf_op jit(solution)/shard_map/update/pallas_call | solution.py:205
  69.1 0.0 collective-permute-done.19.refs_6_
  69.2 1.7 %collective-permute-start.22 = (bf16[1024,128]{1,0:T(8,128)(2,1)S(1)}, bf16[1024,128]{1,0:T(8,128)(2,1)S(1)}, u32[]{:S(2)}, u32[]{:S(2)}) collective-permute-start(bf16[1024,128]{1,0:T(8,128)(2,1)S(1)} %pad_maximum_fusion.3), channel_id=1, source_target_pairs={{0,3},{1,2},{2,1},{3,0},{4,7},{5,6},{6,5},{7,4},{8,11},{9,10},{10,... | collective-permute-start | bytes 786440 | tf_op jit(solution)/shard_map/ppermute | solution.py:32
  71.0 0.1 collective-permute-start.21
  71.1 2.4 %collective-permute-start.20 = (bf16[1024,128]{1,0:T(8,128)(2,1)S(1)}, bf16[1024,128]{1,0:T(8,128)(2,1)S(1)}, u32[]{:S(2)}, u32[]{:S(2)}) collective-permute-start(bf16[1024,128]{1,0:T(8,128)(2,1)S(1)} %get-tuple-element.49), channel_id=1, source_target_pairs={{0,1},{1,0},{2,3},{3,2},{4,5},{5,4},{6,7},{7,6},{8,9},{9,8},{10,11... | collective-permute-start | bytes 786440 | tf_op jit(solution)/shard_map/ppermute | solution.py:32
  73.5 4.7 %collective-permute-done.11.refs_2_ = bf16[2048,128]{1,0:T(8,128)(2,1)S(1)} collective-permute-done((bf16[2048,128]{1,0:T(8,128)(2,1)S(1)}, bf16[2048,128]{1,0:T(8,128)(2,1)S(1)}, u32[]{:S(2)}, u32[]{:S(2)}) %collective-permute-start.11) | collective-permute-done | bytes 524320 | tf_op jit(solution)/shard_map/ppermute | solution.py:32
  78.2 0.1 collective-permute-start.14
  78.3 6.9 %collective-permute-done.22.refs_5_.refs_9_ = bf16[1024,128]{1,0:T(8,128)(2,1)S(1)} collective-permute-done((bf16[1024,128]{1,0:T(8,128)(2,1)S(1)}, bf16[1024,128]{1,0:T(8,128)(2,1)S(1)}, u32[]{:S(2)}, u32[]{:S(2)}) %collective-permute-start.22) | collective-permute-done | bytes 262176 | tf_op jit(solution)/shard_map/ppermute | solution.py:32
  85.2 0.0 collective-permute-start.13
  85.2 0.0 collective-permute-done.21.refs_4_.refs_8_
  85.2 2.5 %collective-permute-start.12 = (bf16[512,128]{1,0:T(8,128)(2,1)S(1)}, bf16[512,128]{1,0:T(8,128)(2,1)S(1)}, u32[]{:S(2)}, u32[]{:S(2)}) collective-permute-start(bf16[512,128]{1,0:T(8,128)(2,1)S(1)} %get-tuple-element.41), channel_id=1, source_target_pairs={{0,1},{1,0},{2,3},{3,2},{4,5},{5,4},{6,7},{7,6},{8,9},{9,8},{10,11... | collective-permute-start | bytes 393224 | tf_op jit(solution)/shard_map/ppermute | solution.py:32
  87.7 0.0 collective-permute-done.20.refs_3_.refs_7_
  87.7 1.5 %place.2.refs_7_ = bf16[2048,2048]{1,0:T(8,128)(2,1)} custom-call(s32[32]{0:T(128)S(1)} %plan.1.idx, f32[2048,128]{1,0:T(8,128)S(1)} %get-tuple-element.40.refs_0_, f32[2048,128]{1,0:T(8,128)S(1)} %get-tuple-element.47.refs_1_, bf16[2048,128]{1,0:T(8,128)(2,1)S(1)} %collective-permute-done.10.refs_2_, ...), custom_call_target="tpu_custom_call", output_to_operand_aliasing={{}: (11, {})} | custom-call | flops 262144 | bytes 4194304 | tf_op jit(solution)/shard_map/place/pallas_call | solution.py:253
  89.2 0.0 collective-permute-done.18.refs_6_
  89.2 0.0 collective-permute-done.14.refs_5_
  89.2 3.2 %collective-permute-done.13.refs_4_ = bf16[512,128]{1,0:T(8,128)(2,1)S(1)} collective-permute-done((bf16[512,128]{1,0:T(8,128)(2,1)S(1)}, bf16[512,128]{1,0:T(8,128)(2,1)S(1)}, u32[]{:S(2)}, u32[]{:S(2)}) %collective-permute-start.13) | collective-permute-done | bytes 131104 | tf_op jit(solution)/shard_map/ppermute | solution.py:32
  92.4 1.7 %collective-permute-done.12.refs_3_ = bf16[512,128]{1,0:T(8,128)(2,1)S(1)} collective-permute-done((bf16[512,128]{1,0:T(8,128)(2,1)S(1)}, bf16[512,128]{1,0:T(8,128)(2,1)S(1)}, u32[]{:S(2)}, u32[]{:S(2)}) %collective-permute-start.12) | collective-permute-done | bytes 131104 | tf_op jit(solution)/shard_map/ppermute | solution.py:32
  94.2 1.5 %place.3 = bf16[2048,2048]{1,0:T(8,128)(2,1)} custom-call(s32[32]{0:T(128)S(1)} %plan.1.idx, f32[2048,128]{1,0:T(8,128)S(1)} %get-tuple-element.34.refs_0_, f32[2048,128]{1,0:T(8,128)S(1)} %get-tuple-element.35.refs_1_, bf16[2048,128]{1,0:T(8,128)(2,1)S(1)} %collective-permute-done.11.refs_2_, ...), custom_call_target="tpu_custom_call", output_to_operand_aliasing={{}: (8, {})} | custom-call | flops 262144 | bytes 4194304 | tf_op jit(solution)/shard_map/place/pallas_call | solution.py:253
  (8 shorter events, 0.2 us)
Async XLA Ops:
  0.0 1.0 %copy-start = (bf16[1,512,384]{2,1,0:T(8,128)(2,1)S(1)}, bf16[1,512,384]{2,1,0:T(8,128)(2,1)}, u32[]{:S(2)}) copy-start(bf16[1,512,384]{2,1,0:T(8,128)(2,1)} %param.6) | copy-start | bytes 1179652
  2.4 10.9 %collective-permute-start.4 = (bf16[512,384]{1,0:T(8,128)(2,1)S(1)}, bf16[512,384]{1,0:T(8,128)(2,1)S(1)}, u32[]{:S(2)}, u32[]{:S(2)}) collective-permute-start(bf16[512,384]{1,0:T(8,128)(2,1)S(1)} %convolution_convert_fusion.refs_0_), channel_id=1, source_target_pairs={{0,8},{1,9},{2,10},{3,11},{4,12},{5,13},{6,14},{7,15},{8,0},{9,1},... | collective-permute-start | bytes 1179656 | tf_op jit(solution)/shard_map/ppermute | solution.py:32
  4.1 13.7 %collective-permute-start.1 = (bf16[512,384]{1,0:T(8,128)(2,1)S(1)}, bf16[512,384]{1,0:T(8,128)(2,1)S(1)}, u32[]{:S(2)}, u32[]{:S(2)}) collective-permute-start(bf16[512,384]{1,0:T(8,128)(2,1)S(1)} %convolution_convert_fusion.refs_0_), channel_id=1, source_target_pairs={{0,3},{1,2},{2,1},{3,0},{4,7},{5,6},{6,5},{7,4},{8,11},{9,10},{10,... | collective-permute-start | bytes 1179656 | tf_op jit(solution)/shard_map/ppermute | solution.py:32
  6.8 12.2 %collective-permute-start = (bf16[512,384]{1,0:T(8,128)(2,1)S(1)}, bf16[512,384]{1,0:T(8,128)(2,1)S(1)}, u32[]{:S(2)}, u32[]{:S(2)}) collective-permute-start(bf16[512,384]{1,0:T(8,128)(2,1)S(1)} %convolution_convert_fusion.refs_0_), channel_id=1, source_target_pairs={{0,1},{1,0},{2,3},{3,2},{4,5},{5,4},{6,7},{7,6},{8,9},{9,8},{10,11... | collective-permute-start | bytes 1179656 | tf_op jit(solution)/shard_map/ppermute | solution.py:32
  7.1 0.7 copy-start.2
  7.7 0.7 copy-start.3
  13.4 19.5 %collective-permute-start.6 = (bf16[512,384]{1,0:T(8,128)(2,1)S(1)}, bf16[512,384]{1,0:T(8,128)(2,1)S(1)}, u32[]{:S(2)}, u32[]{:S(2)}) collective-permute-start(bf16[512,384]{1,0:T(8,128)(2,1)S(1)} %get-tuple-element.53), channel_id=1, source_target_pairs={{0,2},{1,4},{2,0},{3,6},{4,1},{5,7},{6,3},{7,5},{8,10},{9,12},{10,... | collective-permute-start | bytes 1179656 | tf_op jit(solution)/shard_map/ppermute | solution.py:32
  16.5 16.4 %collective-permute-start.8 = (bf16[512,384]{1,0:T(8,128)(2,1)S(1)}, bf16[512,384]{1,0:T(8,128)(2,1)S(1)}, u32[]{:S(2)}, u32[]{:S(2)}) collective-permute-start(bf16[512,384]{1,0:T(8,128)(2,1)S(1)} %get-tuple-element.54), channel_id=1, source_target_pairs={{1,2},{3,0},{4,7},{6,5},{9,10},{11,8},{12,15},{14,13},{17,18},{19,... | collective-permute-start | bytes 1179656 | tf_op jit(solution)/shard_map/ppermute | solution.py:32
  17.9 11.9 %collective-permute-start.2 = (bf16[256,384]{1,0:T(8,128)(2,1)S(1)}, bf16[256,384]{1,0:T(8,128)(2,1)S(1)}, u32[]{:S(2)}, u32[]{:S(2)}) collective-permute-start(bf16[256,384]{1,0:T(8,128)(2,1)S(1)} %slice.44), channel_id=1, source_target_pairs={{0,1},{1,0},{2,3},{3,2},{4,5},{5,4},{6,7},{7,6},{8,9},{9,8},{10,11... | collective-permute-start | bytes 589832 | tf_op jit(solution)/shard_map/ppermute | solution.py:32
  19.1 13.8 %collective-permute-start.3 = (bf16[256,384]{1,0:T(8,128)(2,1)S(1)}, bf16[256,384]{1,0:T(8,128)(2,1)S(1)}, u32[]{:S(2)}, u32[]{:S(2)}) collective-permute-start(bf16[256,384]{1,0:T(8,128)(2,1)S(1)} %slice.45), channel_id=1, source_target_pairs={{0,3},{1,2},{2,1},{3,0},{4,7},{5,6},{6,5},{7,4},{8,11},{9,10},{10,... | collective-permute-start | bytes 589832 | tf_op jit(solution)/shard_map/ppermute | solution.py:32
  21.9 3.4 %copy-start.1 = (bf16[1,2048,2048]{2,1,0:T(8,128)(2,1)S(1)}, bf16[1,2048,2048]{2,1,0:T(8,128)(2,1)}, u32[]{:S(2)}) copy-start(bf16[1,2048,2048]{2,1,0:T(8,128)(2,1)} %param.5) | copy-start | bytes 25165828
  26.6 8.7 %collective-permute-start.5 = (bf16[512,384]{1,0:T(8,128)(2,1)S(1)}, bf16[512,384]{1,0:T(8,128)(2,1)S(1)}, u32[]{:S(2)}, u32[]{:S(2)}) collective-permute-start(bf16[512,384]{1,0:T(8,128)(2,1)S(1)} %get-tuple-element.30.refs_5_), channel_id=1, source_target_pairs={{0,4},{2,6},{5,1},{7,3},{8,12},{10,14},{13,9},{15,11},{16,20},{18,... | collective-permute-start | bytes 1179656 | tf_op jit(solution)/shard_map/ppermute | solution.py:32
  32.9 2.5 %collective-permute-start.7 = (bf16[512,384]{1,0:T(8,128)(2,1)S(1)}, bf16[512,384]{1,0:T(8,128)(2,1)S(1)}, u32[]{:S(2)}, u32[]{:S(2)}) collective-permute-start(bf16[512,384]{1,0:T(8,128)(2,1)S(1)} %collective-permute-done.6.refs_8_.refs_9_), channel_id=1, source_target_pairs={{0,4},{1,5},{2,6},{3,7},{4,0},{5,1},{6,2},{7,3},{8,12},{9,13},{10,... | collective-permute-start | bytes 1179656 | tf_op jit(solution)/shard_map/ppermute | solution.py:32
  32.9 3.7 %collective-permute-start.9 = (bf16[512,384]{1,0:T(8,128)(2,1)S(1)}, bf16[512,384]{1,0:T(8,128)(2,1)S(1)}, u32[]{:S(2)}, u32[]{:S(2)}) collective-permute-start(bf16[512,384]{1,0:T(8,128)(2,1)S(1)} %collective-permute-done.8.refs_11_), channel_id=1, source_target_pairs={{0,4},{2,6},{5,1},{7,3},{8,12},{10,14},{13,9},{15,11},{16,20},{18,... | collective-permute-start | bytes 1179656 | tf_op jit(solution)/shard_map/ppermute | solution.py:32
  38.0 20.7 %collective-permute-start.10 = (bf16[2048,128]{1,0:T(8,128)(2,1)S(1)}, bf16[2048,128]{1,0:T(8,128)(2,1)S(1)}, u32[]{:S(2)}, u32[]{:S(2)}) collective-permute-start(bf16[2048,128]{1,0:T(8,128)(2,1)S(1)} %picked.3), channel_id=1, source_target_pairs={{16,0},{17,1},{18,2},{19,3},{20,4},{21,5},{22,6},{23,7},{24,8},{25... | collective-permute-start | bytes 1572872 | tf_op jit(solution)/shard_map/ppermute | solution.py:32
  41.7 9.5 %collective-permute-start.15 = (bf16[512,128]{1,0:T(8,128)(2,1)S(1)}, bf16[512,128]{1,0:T(8,128)(2,1)S(1)}, u32[]{:S(2)}, u32[]{:S(2)}) collective-permute-start(bf16[512,128]{1,0:T(8,128)(2,1)S(1)} %get-tuple-element.44), channel_id=1, source_target_pairs={{0,1},{1,0},{2,3},{3,2},{4,5},{5,4},{6,7},{7,6},{8,9},{9,8},{10,11... | collective-permute-start | bytes 393224 | tf_op jit(solution)/shard_map/ppermute | solution.py:32
  41.8 14.2 %collective-permute-start.16 = (bf16[512,128]{1,0:T(8,128)(2,1)S(1)}, bf16[512,128]{1,0:T(8,128)(2,1)S(1)}, u32[]{:S(2)}, u32[]{:S(2)}) collective-permute-start(bf16[512,128]{1,0:T(8,128)(2,1)S(1)} %get-tuple-element.45), channel_id=1, source_target_pairs={{0,2},{1,3},{2,0},{3,1},{4,6},{5,7},{6,4},{7,5},{8,10},{9,11},{10,... | collective-permute-start | bytes 393224 | tf_op jit(solution)/shard_map/ppermute | solution.py:32
  43.7 12.3 %collective-permute-start.17 = (bf16[512,128]{1,0:T(8,128)(2,1)S(1)}, bf16[512,128]{1,0:T(8,128)(2,1)S(1)}, u32[]{:S(2)}, u32[]{:S(2)}) collective-permute-start(bf16[512,128]{1,0:T(8,128)(2,1)S(1)} %get-tuple-element.46), channel_id=1, source_target_pairs={{0,3},{1,2},{2,1},{3,0},{4,7},{5,6},{6,5},{7,4},{8,11},{9,10},{10,... | collective-permute-start | bytes 393224 | tf_op jit(solution)/shard_map/ppermute | solution.py:32
  48.1 21.0 %collective-permute-start.19 = (bf16[2048,128]{1,0:T(8,128)(2,1)S(1)}, bf16[2048,128]{1,0:T(8,128)(2,1)S(1)}, u32[]{:S(2)}, u32[]{:S(2)}) collective-permute-start(bf16[2048,128]{1,0:T(8,128)(2,1)S(1)} %get-tuple-element.48), channel_id=1, source_target_pairs={{16,4},{17,5},{18,6},{19,7},{20,0},{21,1},{22,2},{23,3},{24,12},{2... | collective-permute-start | bytes 1572872 | tf_op jit(solution)/shard_map/ppermute | solution.py:32
  51.2 26.9 %collective-permute-start.11 = (bf16[2048,128]{1,0:T(8,128)(2,1)S(1)}, bf16[2048,128]{1,0:T(8,128)(2,1)S(1)}, u32[]{:S(2)}, u32[]{:S(2)}) collective-permute-start(bf16[2048,128]{1,0:T(8,128)(2,1)S(1)} %get-tuple-element.39), channel_id=1, source_target_pairs={{16,8},{17,9},{18,10},{19,11},{20,12},{21,13},{22,14},{23,15},{24,... | collective-permute-start | bytes 1572872 | tf_op jit(solution)/shard_map/ppermute | solution.py:32
  56.1 33.1 %collective-permute-start.18 = (bf16[2048,128]{1,0:T(8,128)(2,1)S(1)}, bf16[2048,128]{1,0:T(8,128)(2,1)S(1)}, u32[]{:S(2)}, u32[]{:S(2)}) collective-permute-start(bf16[2048,128]{1,0:T(8,128)(2,1)S(1)} %pad_maximum_fusion), channel_id=1, source_target_pairs={{16,12},{17,13},{18,14},{19,15},{20,8},{21,9},{22,10},{23,11},{24,... | collective-permute-start | bytes 1572872 | tf_op jit(solution)/shard_map/ppermute | solution.py:32
  69.2 16.0 %collective-permute-start.22 = (bf16[1024,128]{1,0:T(8,128)(2,1)S(1)}, bf16[1024,128]{1,0:T(8,128)(2,1)S(1)}, u32[]{:S(2)}, u32[]{:S(2)}) collective-permute-start(bf16[1024,128]{1,0:T(8,128)(2,1)S(1)} %pad_maximum_fusion.3), channel_id=1, source_target_pairs={{0,3},{1,2},{2,1},{3,0},{4,7},{5,6},{6,5},{7,4},{8,11},{9,10},{10,... | collective-permute-start | bytes 786440 | tf_op jit(solution)/shard_map/ppermute | solution.py:32
  71.0 14.3 %collective-permute-start.21 = (bf16[1024,128]{1,0:T(8,128)(2,1)S(1)}, bf16[1024,128]{1,0:T(8,128)(2,1)S(1)}, u32[]{:S(2)}, u32[]{:S(2)}) collective-permute-start(bf16[1024,128]{1,0:T(8,128)(2,1)S(1)} %get-tuple-element.50), channel_id=1, source_target_pairs={{0,2},{1,3},{2,0},{3,1},{4,6},{5,7},{6,4},{7,5},{8,10},{9,11},{10,... | collective-permute-start | bytes 786440 | tf_op jit(solution)/shard_map/ppermute | solution.py:32
  71.1 16.7 %collective-permute-start.20 = (bf16[1024,128]{1,0:T(8,128)(2,1)S(1)}, bf16[1024,128]{1,0:T(8,128)(2,1)S(1)}, u32[]{:S(2)}, u32[]{:S(2)}) collective-permute-start(bf16[1024,128]{1,0:T(8,128)(2,1)S(1)} %get-tuple-element.49), channel_id=1, source_target_pairs={{0,1},{1,0},{2,3},{3,2},{4,5},{5,4},{6,7},{7,6},{8,9},{9,8},{10,11... | collective-permute-start | bytes 786440 | tf_op jit(solution)/shard_map/ppermute | solution.py:32
  78.2 11.0 %collective-permute-start.14 = (bf16[512,128]{1,0:T(8,128)(2,1)S(1)}, bf16[512,128]{1,0:T(8,128)(2,1)S(1)}, u32[]{:S(2)}, u32[]{:S(2)}) collective-permute-start(bf16[512,128]{1,0:T(8,128)(2,1)S(1)} %get-tuple-element.43), channel_id=1, source_target_pairs={{0,3},{1,2},{2,1},{3,0},{4,7},{5,6},{6,5},{7,4},{8,11},{9,10},{10,... | collective-permute-start | bytes 393224 | tf_op jit(solution)/shard_map/ppermute | solution.py:32
  85.2 7.2 %collective-permute-start.13 = (bf16[512,128]{1,0:T(8,128)(2,1)S(1)}, bf16[512,128]{1,0:T(8,128)(2,1)S(1)}, u32[]{:S(2)}, u32[]{:S(2)}) collective-permute-start(bf16[512,128]{1,0:T(8,128)(2,1)S(1)} %get-tuple-element.42), channel_id=1, source_target_pairs={{0,2},{1,3},{2,0},{3,1},{4,6},{5,7},{6,4},{7,5},{8,10},{9,11},{10,... | collective-permute-start | bytes 393224 | tf_op jit(solution)/shard_map/ppermute | solution.py:32
  85.2 8.9 %collective-permute-start.12 = (bf16[512,128]{1,0:T(8,128)(2,1)S(1)}, bf16[512,128]{1,0:T(8,128)(2,1)S(1)}, u32[]{:S(2)}, u32[]{:S(2)}) collective-permute-start(bf16[512,128]{1,0:T(8,128)(2,1)S(1)} %get-tuple-element.41), channel_id=1, source_target_pairs={{0,1},{1,0},{2,3},{3,2},{4,5},{5,4},{6,7},{7,6},{8,9},{9,8},{10,11... | collective-permute-start | bytes 393224 | tf_op jit(solution)/shard_map/ppermute | solution.py:32
